TPU v7x, 128 devices: a whole 4x4x4 slice. The times are simulated.
128 devices in a mesh: row: 16 (over y, z_lo, core), col: 8 (over z_hi, x).
Axes of the slice: x: 4, y: 4, z: 4 (z_hi: 2, z_lo: 2; z = z_hi * 2 + z_lo), core: 2. Of those that a mesh axis runs over, the one named last changes fastest.
Arguments:
- images: bfloat16 [24576, 768], P(('row', 'col')), may hold values from -2 to 2
- texts: bfloat16 [24576, 768], P(('col', 'row')), may hold values from -3.5 to 3.5
- pair_index: int32 [24576], P(('row', 'col')), may hold values from 0 to 24575, as said below
- log_scale: float32 [1], replicated, may hold values from 3.87 to 4.16
- bias: float32 [1], replicated, may hold values from -12 to -10
Outputs:
- loss: float32 [1], replicated
- grad_images: float32 [24576, 768], P(('row', 'col'))
- grad_texts: float32 [24576, 768], P(('col', 'row'))
Inputs may be any that keep to these rules, and one draw needn't show every extreme that they name: `pair_index`: every text row is paired with exactly one image row.
All inputs are finite; a program needn't handle non-finite values.
Results may differ from a plain program's by a relative error of at most 0.0051.
Values may be sent and summed in bfloat16 or wider, within the bound.
No kernel may reach another device: no remote copies, remote signals or barrier semaphores. Data moves between devices by JAX's collectives and lax.ppermute only.
A program may use at most 128 MiB of HBM per device.

v0:
```python
import math

import jax
import jax.numpy as jnp
from jax import lax
from jax.sharding import PartitionSpec as P

EPS = 1e-06


def normalize(values):
    wide = values.astype(jnp.float32)
    inverse = lax.rsqrt(jnp.sum(wide * wide, axis=-1, keepdims=True) + EPS)
    return (wide * inverse, inverse)


def unproject(grad_unit, unit, inverse):
    along = jnp.sum(grad_unit * unit, axis=-1, keepdims=True)
    return (grad_unit - unit * along) * inverse


def tile_weight(x_block, pair_block, y_part, columns, scale, shift):
    score = lax.dot_general(
        x_block, y_part, (((1,), (1,)), ((), ())), preferred_element_type=jnp.float32
    )
    logit = scale * score + shift
    sign = jnp.where(pair_block[:, None] == columns[None, :], 1.0, -1.0).astype(jnp.float32)
    loss_part = -jnp.sum(jax.nn.log_sigmoid(sign * logit))
    weight = (-scale * sign * jax.nn.sigmoid(-sign * logit)).astype(jnp.bfloat16)
    return (loss_part, weight)


def local(images, texts, pair_index, log_scale, bias):
    x_unit, inv_x = normalize(images)
    y_unit, inv_y = normalize(texts)
    x_low = lax.all_gather(x_unit.astype(jnp.bfloat16), "col", axis=0, tiled=True)
    pair_rows = lax.all_gather(pair_index, "col", axis=0, tiled=True)
    y_low = lax.all_gather(y_unit.astype(jnp.bfloat16), "row", axis=0, tiled=True)
    scale = jnp.exp(log_scale[0])
    shift = bias[0]
    img_rows = x_low.shape[0]
    txt_rows = y_low.shape[0]
    width = x_low.shape[1]
    pair_count = images.shape[0] * lax.axis_size("row") * lax.axis_size("col")
    col_base = lax.axis_index("col") * txt_rows
    columns = col_base + jnp.arange(txt_rows, dtype=jnp.int32)
    block = math.gcd(img_rows, 512)
    block_total = img_rows // block
    x_blocks = x_low.reshape(block_total, block, width)
    pair_blocks = pair_rows.reshape(block_total, block)

    def full_step(carry, item):
        grad_y, total = carry
        x_block, pair_block = item
        loss_part, weight = tile_weight(x_block, pair_block, y_low, columns, scale, shift)
        grad_x = jnp.dot(weight, y_low, preferred_element_type=jnp.float32)
        grad_y = grad_y + lax.dot_general(
            weight, x_block, (((0,), (0,)), ((), ())), preferred_element_type=jnp.float32
        )
        return ((grad_y, total + loss_part), grad_x)

    start = (jnp.zeros((txt_rows, width), jnp.float32), jnp.zeros((), jnp.float32))
    (gy_part, total), gx_blocks = lax.scan(full_step, start, (x_blocks, pair_blocks))
    gx_unit = lax.psum_scatter(
        gx_blocks.reshape(img_rows, width), "col", scatter_dimension=0, tiled=True
    )
    gy_unit = lax.psum_scatter(gy_part, "row", scatter_dimension=0, tiled=True)
    loss_sum = lax.psum(total, ("row", "col"))
    loss = (loss_sum / pair_count).reshape(1)
    return (loss, unproject(gx_unit, x_unit, inv_x), unproject(gy_unit, y_unit, inv_y))


def solution(mesh):
    return jax.shard_map(
        local,
        mesh=mesh,
        in_specs=(P(("row", "col"), None), P(("col", "row"), None), P(("row", "col")), P(), P()),
        out_specs=(P(), P(("row", "col"), None), P(("col", "row"), None)),
        check_vma=False,
    )
```

profile of v0, /device:TPU:0, one launch (start us, length us, event | category | flops | bytes accessed | tf_op | source)
XLA Modules:
  0.0 423.5 jit_solution(14553768033205507548)
XLA Ops:
  7.2 0.0 all-gather.3.cloned.1.call-start
  7.2 1.1 fusion.29
  8.3 0.0 copy-start.4
  8.3 0.6 copy-done.4
  8.9 1.8 fusion.25
  10.7 0.0 all-gather.3.cloned.1.call-update
  10.7 0.0 all-gather.5.cloned.1.call-start
  10.8 1.1 fusion.33
  11.9 0.0 copy-start.6
  11.9 0.6 copy-done.6
  12.5 1.8 fusion.22
  14.2 0.0 all-gather.5.cloned.1.call-update
  14.3 0.0 reduce-scatter.3.cloned.1.call-start
  15.0 1.3 dynamic-slice
  17.0 0.9 dynamic-update-slice
  17.9 14.7 %all-reduce = s32[1536]{0:T(1024)S(1)} all-reduce(s32[1536]{0:T(1024)S(1)} %dynamic-update-slice), channel_id=1, replica_groups=mesh['row'=16,'col'=8] {'col'}, use_global_device_ids=true, to_apply=%add | all-reduce | flops 1536 | bytes 12288
  32.6 37.7 %all-gather.3.cloned.1.call-done = bf16[1536,768]{1,0:T(8,128)(2,1)} async-done(((bf16[192,768]{1,0:T(8,128)(2,1)}), bf16[1536,768]{1,0:T(8,128)(2,1)}) %all-gather.3.cloned.1.call-update) | async-done | bytes 2359312 | tf_op jit(solution)/shard_map/all_gather | solution.py:36
  70.3 39.4 %all-gather.5.cloned.1.call-done = bf16[3072,768]{1,0:T(8,128)(2,1)} async-done(((bf16[192,768]{1,0:T(8,128)(2,1)}), bf16[3072,768]{1,0:T(8,128)(2,1)}) %all-gather.5.cloned.1.call-update) | async-done | bytes 4718608 | tf_op jit(solution)/shard_map/all_gather | solution.py:38
  109.7 108.0 %while.16 = (s32[]{:T(128)}, f32[3072,768]{1,0:T(8,128)}, f32[]{:T(128)}, f32[3,512,768]{2,1,0:T(8,128)}, f32[]{:T(128)}, /*index=5*/s32[3,512]{1,0:T(4,128)S(1)...) while((s32[]{:T(128)}, f32[3072,768]{1,0:T(8,128)}, ...), condition=%wide.region_4.5_spmd.clone, body=%wide.region_2.4_spmd.clone.sunk | while | flops 7310674944 | bytes 151058704 | solution.py:63
  109.7 12.8 %fusion.47 = (f32[]{:T(128)}, f32[512,3072]{1,0:T(8,128)}) fusion(f32[]{:T(128)} %get-tuple-element.274, f32[]{:T(128)} %get-tuple-element.271, s32[3072]{0:T(1024)S(1)} %iota_add_fusion.2, s32[512]{0:T(512)S(1)} %bitcast.31, bf16[3072,768]{1,0:T(8,128)(2,1)} %get-tuple-element.273, bf16[3,512,768]{2,1,0:T(8,128)(2,1)} %get-tuple-element.272, ...), kind=kOutput, calls=%fused_computation.14.clone.1 | convolution fusion | flops 2436366336 | bytes 11811848 | tf_op jit(solution)/shard_map/while/body/eval_jaxpr/dot_general | solution.py:23
  123.1 0.0 copy-start
  123.1 0.0 copy-start.8
  123.1 10.8 %bitcast_dynamic-update-slice_fusion.2 = f32[3,512,768]{2,1,0:T(8,128)} fusion(f32[3,512,768]{2,1,0:T(8,128)} %get-tuple-element.255, s32[]{:T(128)S(6)} %copy.14, bf16[3072,768]{1,0:T(8,128)(2,1)} %get-tuple-element.273, f32[512,3072]{1,0:T(8,128)} %get-tuple-element.237, f32[]{:T(128)} %get-tuple-element.274, f32[]{:T(128)} %get-tuple-element.271, ...), kind=kOutput, calls=%fused_computation.16.clone.1 | convolution fusion | flops 2434793472 | bytes 12598788 | tf_op jit(solution)/shard_map/while/body/eval_jaxpr/dot_general | solution.py:56
  133.9 0.0 copy-done
  134.0 0.0 copy-done.8
  134.0 8.0 %select_add_fusion.2 = f32[3072,768]{1,0:T(8,128)S(1)} fusion(f32[3072,768]{1,0:T(8,128)S(1)} %copy-done, pred[]{:T(512)S(6)} %compare.3, bf16[3,512,768]{2,1,0:T(8,128)(2,1)} %get-tuple-element.272, s32[]{:T(128)S(6)} %copy.14, f32[512,3072]{1,0:T(8,128)S(1)} %copy-done.8, f32[]{:T(128)} %get-tuple-element.274, f32[]{:T(128)} %get-tuple-element.271, ...), kind=kOutput, calls=%fused_computation.5.clone.1 | convolution fusion | flops 2439512064 | bytes 25968132 | tf_op jit(solution)/shard_map/while/body/eval_jaxpr/dot_general | solution.py:57
  142.0 0.0 copy-start.1
  142.0 3.6 copy-done.1
  145.6 12.8 %fusion.47 = (f32[]{:T(128)}, f32[512,3072]{1,0:T(8,128)}) fusion(f32[]{:T(128)} %get-tuple-element.274, f32[]{:T(128)} %get-tuple-element.271, s32[3072]{0:T(1024)S(1)} %iota_add_fusion.2, s32[512]{0:T(512)S(1)} %bitcast.31, bf16[3072,768]{1,0:T(8,128)(2,1)} %get-tuple-element.273, bf16[3,512,768]{2,1,0:T(8,128)(2,1)} %get-tuple-element.272, ...), kind=kOutput, calls=%fused_computation.14.clone.1 | convolution fusion | flops 2436366336 | bytes 11811848 | tf_op jit(solution)/shard_map/while/body/eval_jaxpr/dot_general | solution.py:23
  159.1 0.0 copy-start
  159.1 0.0 copy-start.8
  159.1 10.9 %bitcast_dynamic-update-slice_fusion.2 = f32[3,512,768]{2,1,0:T(8,128)} fusion(f32[3,512,768]{2,1,0:T(8,128)} %get-tuple-element.255, s32[]{:T(128)S(6)} %copy.14, bf16[3072,768]{1,0:T(8,128)(2,1)} %get-tuple-element.273, f32[512,3072]{1,0:T(8,128)} %get-tuple-element.237, f32[]{:T(128)} %get-tuple-element.274, f32[]{:T(128)} %get-tuple-element.271, ...), kind=kOutput, calls=%fused_computation.16.clone.1 | convolution fusion | flops 2434793472 | bytes 12598788 | tf_op jit(solution)/shard_map/while/body/eval_jaxpr/dot_general | solution.py:56
  170.0 0.0 copy-done
  170.0 0.0 copy-done.8
  170.0 8.0 %select_add_fusion.2 = f32[3072,768]{1,0:T(8,128)S(1)} fusion(f32[3072,768]{1,0:T(8,128)S(1)} %copy-done, pred[]{:T(512)S(6)} %compare.3, bf16[3,512,768]{2,1,0:T(8,128)(2,1)} %get-tuple-element.272, s32[]{:T(128)S(6)} %copy.14, f32[512,3072]{1,0:T(8,128)S(1)} %copy-done.8, f32[]{:T(128)} %get-tuple-element.274, f32[]{:T(128)} %get-tuple-element.271, ...), kind=kOutput, calls=%fused_computation.5.clone.1 | convolution fusion | flops 2439512064 | bytes 25968132 | tf_op jit(solution)/shard_map/while/body/eval_jaxpr/dot_general | solution.py:57
  178.0 0.0 copy-start.1
  178.0 3.6 copy-done.1
  181.7 12.8 %fusion.47 = (f32[]{:T(128)}, f32[512,3072]{1,0:T(8,128)}) fusion(f32[]{:T(128)} %get-tuple-element.274, f32[]{:T(128)} %get-tuple-element.271, s32[3072]{0:T(1024)S(1)} %iota_add_fusion.2, s32[512]{0:T(512)S(1)} %bitcast.31, bf16[3072,768]{1,0:T(8,128)(2,1)} %get-tuple-element.273, bf16[3,512,768]{2,1,0:T(8,128)(2,1)} %get-tuple-element.272, ...), kind=kOutput, calls=%fused_computation.14.clone.1 | convolution fusion | flops 2436366336 | bytes 11811848 | tf_op jit(solution)/shard_map/while/body/eval_jaxpr/dot_general | solution.py:23
  195.1 0.0 copy-start
  195.1 0.0 copy-start.8
  195.1 10.8 %bitcast_dynamic-update-slice_fusion.2 = f32[3,512,768]{2,1,0:T(8,128)} fusion(f32[3,512,768]{2,1,0:T(8,128)} %get-tuple-element.255, s32[]{:T(128)S(6)} %copy.14, bf16[3072,768]{1,0:T(8,128)(2,1)} %get-tuple-element.273, f32[512,3072]{1,0:T(8,128)} %get-tuple-element.237, f32[]{:T(128)} %get-tuple-element.274, f32[]{:T(128)} %get-tuple-element.271, ...), kind=kOutput, calls=%fused_computation.16.clone.1 | convolution fusion | flops 2434793472 | bytes 12598788 | tf_op jit(solution)/shard_map/while/body/eval_jaxpr/dot_general | solution.py:56
  205.9 0.0 copy-done
  205.9 0.0 copy-done.8
  205.9 8.0 %select_add_fusion.2 = f32[3072,768]{1,0:T(8,128)S(1)} fusion(f32[3072,768]{1,0:T(8,128)S(1)} %copy-done, pred[]{:T(512)S(6)} %compare.3, bf16[3,512,768]{2,1,0:T(8,128)(2,1)} %get-tuple-element.272, s32[]{:T(128)S(6)} %copy.14, f32[512,3072]{1,0:T(8,128)S(1)} %copy-done.8, f32[]{:T(128)} %get-tuple-element.274, f32[]{:T(128)} %get-tuple-element.271, ...), kind=kOutput, calls=%fused_computation.5.clone.1 | convolution fusion | flops 2439512064 | bytes 25968132 | tf_op jit(solution)/shard_map/while/body/eval_jaxpr/dot_general | solution.py:57
  214.0 0.0 copy-start.1
  214.0 3.6 copy-done.1
  217.6 0.0 copy-start.2
  217.6 0.0 copy-start.5
  217.6 0.0 reduce-scatter.3.cloned.1.call-update
  217.6 0.0 copy-start.3
  217.7 0.0 copy-start.7
  217.7 0.0 reduce-scatter.5.cloned.1.call-start
  217.7 0.5 reduce-scatter.5.cloned.1.call-update
  218.2 72.7 %psum.7 = f32[]{:T(128)} all-reduce(f32[]{:T(128)} %get-tuple-element.102), channel_id=1, replica_groups=mesh['row'=16,'col'=8] {'row','col'}, use_global_device_ids=true, to_apply=%region_5.6 | all-reduce | flops 1 | bytes 8 | tf_op jit(solution)/shard_map/psum | solution.py:68
  291.6 15.4 %reduce-scatter.3.cloned.1.call-done = f32[192,768]{1,0:T(8,128)} async-done(((f32[1536,768]{1,0:T(8,128)}), f32[192,768]{1,0:T(8,128)}) %reduce-scatter.3.cloned.1.call-update) | async-done | bytes 589840 | tf_op jit(solution)/shard_map/reduce_scatter | solution.py:64
  307.0 0.0 copy-done.2
  307.0 0.0 copy-done.5
  307.0 1.3 fusion.26
  308.3 2.1 fusion.28
  310.4 102.1 %reduce-scatter.5.cloned.1.call-done = f32[192,768]{1,0:T(8,128)} async-done(((f32[3072,768]{1,0:T(8,128)}), f32[192,768]{1,0:T(8,128)}) %reduce-scatter.5.cloned.1.call-update) | async-done | bytes 589840 | tf_op jit(solution)/shard_map/reduce_scatter | solution.py:67
  412.4 0.0 copy-done.3
  412.4 0.0 copy-done.7
  412.4 1.3 fusion.30
  413.7 2.1 fusion.32
  (12 shorter events, 0.1 us)
Async XLA Ops:
  7.2 63.1 %all-gather.3.cloned.1.call-start = ((), (), s32[]{:S(2)}) async-start(), calls=%async_computation.2 | async-start | bytes 2654208 | tf_op jit(solution)/shard_map/all_gather | solution.py:36
  8.3 0.6 copy-start.4
  10.7 98.9 %all-gather.5.cloned.1.call-start = ((), (), s32[]{:S(2)}) async-start(), calls=%async_computation.3 | async-start | bytes 5013504 | tf_op jit(solution)/shard_map/all_gather | solution.py:38
  11.9 0.6 copy-start.6
  14.3 292.7 %reduce-scatter.3.cloned.1.call-start = ((), (), s32[]{:S(2)}) async-start(), calls=%async_computation.4 | async-start | bytes 5308416 | tf_op jit(solution)/shard_map/reduce_scatter | solution.py:64
  123.1 10.9 %copy-start = (f32[3072,768]{1,0:T(8,128)S(1)}, f32[3072,768]{1,0:T(8,128)}, u32[]{:S(2)}) copy-start(f32[3072,768]{1,0:T(8,128)} %get-tuple-element.253) | copy-start | bytes 28311556 | tf_op jit(solution)/shard_map/while
  123.1 10.9 %copy-start.8 = (f32[512,3072]{1,0:T(8,128)S(1)}, f32[512,3072]{1,0:T(8,128)}, u32[]{:S(2)}) copy-start(f32[512,3072]{1,0:T(8,128)} %get-tuple-element.237) | copy-start | bytes 18874372 | tf_op jit(solution)/shard_map/while
  142.0 3.6 copy-start.1
  159.1 10.9 %copy-start = (f32[3072,768]{1,0:T(8,128)S(1)}, f32[3072,768]{1,0:T(8,128)}, u32[]{:S(2)}) copy-start(f32[3072,768]{1,0:T(8,128)} %get-tuple-element.253) | copy-start | bytes 28311556 | tf_op jit(solution)/shard_map/while
  159.1 10.9 %copy-start.8 = (f32[512,3072]{1,0:T(8,128)S(1)}, f32[512,3072]{1,0:T(8,128)}, u32[]{:S(2)}) copy-start(f32[512,3072]{1,0:T(8,128)} %get-tuple-element.237) | copy-start | bytes 18874372 | tf_op jit(solution)/shard_map/while
  178.0 3.6 copy-start.1
  195.1 10.8 %copy-start = (f32[3072,768]{1,0:T(8,128)S(1)}, f32[3072,768]{1,0:T(8,128)}, u32[]{:S(2)}) copy-start(f32[3072,768]{1,0:T(8,128)} %get-tuple-element.253) | copy-start | bytes 28311556 | tf_op jit(solution)/shard_map/while
  195.1 10.8 %copy-start.8 = (f32[512,3072]{1,0:T(8,128)S(1)}, f32[512,3072]{1,0:T(8,128)}, u32[]{:S(2)}) copy-start(f32[512,3072]{1,0:T(8,128)} %get-tuple-element.237) | copy-start | bytes 18874372 | tf_op jit(solution)/shard_map/while
  214.0 3.6 copy-start.1
  217.6 89.4 %copy-start.2 = (bf16[192,768]{1,0:T(8,128)(2,1)S(1)}, bf16[192,768]{1,0:T(8,128)(2,1)}, u32[]{:S(2)}) copy-start(bf16[192,768]{1,0:T(8,128)(2,1)} %param.7) | copy-start | bytes 884740
  217.6 89.4 %copy-start.5 = (f32[192]{0:T(256)S(1)}, f32[192]{0:T(256)}, u32[]{:S(2)}) copy-start(f32[192]{0:T(256)} %copy-done.4) | copy-start | bytes 2308
  217.6 194.8 %copy-start.3 = (bf16[192,768]{1,0:T(8,128)(2,1)S(1)}, bf16[192,768]{1,0:T(8,128)(2,1)}, u32[]{:S(2)}) copy-start(bf16[192,768]{1,0:T(8,128)(2,1)} %param.8) | copy-start | bytes 884740
  217.7 194.8 %copy-start.7 = (f32[192]{0:T(256)S(1)}, f32[192]{0:T(256)}, u32[]{:S(2)}) copy-start(f32[192]{0:T(256)} %copy-done.6) | copy-start | bytes 2308
  217.7 194.8 %reduce-scatter.5.cloned.1.call-start = ((), (), s32[]{:S(2)}) async-start(), calls=%async_computation.5 | async-start | bytes 10027008 | tf_op jit(solution)/shard_map/reduce_scatter | solution.py:67
Sparse Core Ops, SparseCore 0:
  10.9 59.3 all-gather.2
  72.6 37.0 all-gather.4
  217.8 89.1 reduce-scatter.2
  309.4 103.0 reduce-scatter.4
where the time goes:
time: 428 us; the launch traced here: 423 us
  waiting for transfers between devices  195 us (46%)
  matrix products  95 us (22%)
  blocking collectives  87.4 us (20%)
  between operations  17 us (4%)
  local copies, waits for them, and re-layouts  14.2 us (3%)
  other arithmetic  12.6 us (3%)
    reduce_scatter x1, waiting for transfers between devices, local(): gy_unit = lax.psum_scatter(gy_part, 'row', scatter_dimension=0, tiled=True)  102 us
    psum x1, blocking collectives, local(): loss_sum = lax.psum(total, ('row', 'col'))  72.7 us
    all_gather x1, waiting for transfers between devices, local(): lax.all_gather(y_unit.astype(jnp.bfloat16), 'row', axis=0, tiled=True)  39.4 us
    dot_general x3, matrix products, tile_weight(): lax.dot_general(x_block, y_part, (((1,), (1,)), ((), ())), preferred_elem...  38.3 us
    all_gather x1, waiting for transfers between devices, local(): lax.all_gather(x_unit.astype(jnp.bfloat16), 'col', axis=0, tiled=True)  37.7 us
    dot_general x3, matrix products, full_step(): grad_x = jnp.dot(weight, y_low, preferred_element_type=jnp.float32)  32.5 us
    dot_general x3, matrix products, full_step(): lax.dot_general(weight, x_block, (((0,), (0,)), ((), ())), preferred_elem...  24.1 us
    reduce_scatter x1, waiting for transfers between devices, local(): lax.psum_scatter(gx_blocks.reshape(img_rows, width), 'col', scatter_dimen...  15.4 us
  transfers between devices with their start and end apart: 4, of which 4 were waited for; matrix products, arithmetic and copies ran while one was open for 2% of the time, Pallas kernels for 0%

commit v1 on v0

v1 whole, which is shorter than its diff:
```python
import functools

import jax
import jax.numpy as jnp
from jax import lax
from jax.experimental import pallas as pl
from jax.experimental.pallas import tpu as pltpu
from jax.sharding import PartitionSpec as P

EPS = 1e-06
LOG2E = 1.4426950408889634
N_ROW = 16
N_COL = 8
R = 192
D = 768
RX = R + 16
NX = R * N_COL
NY = R * N_ROW
BM = 512
NT = (((1,), (1,)), ((), ()))
TN = (((0,), (0,)), ((), ()))
VMEM = pl.BlockSpec(memory_space=pltpu.VMEM)
SMEM = pl.BlockSpec(memory_space=pltpu.SMEM)


def row_pairs(dy, dz, dc):
    out = []
    for r in range(N_ROW):
        y, z, c = r // 4, (r // 2) % 2, r % 2
        out.append((r, (((y + dy) % 4) * 2 + (z ^ dz)) * 2 + (c ^ dc)))
    return out


def col_pairs(dx, dz):
    return [(c, ((c // 4) ^ dz) * 4 + (c % 4 + dx) % 4) for c in range(N_COL)]


def send_row(value, dy=0, dz=0, dc=0):
    return lax.ppermute(value, "row", row_pairs(dy, dz, dc))


def send_col(value, dx=0, dz=0):
    return lax.ppermute(value, "col", col_pairs(dx, dz))


def normalize(ref):
    wide = ref[...].astype(jnp.float32)
    inverse = lax.rsqrt(jnp.sum(wide * wide, axis=-1, keepdims=True) + EPS)
    return wide * inverse, inverse


def prep_kernel(images_ref, texts_ref, pair_ref, x_ref, y_ref):
    x_ref[:R, :] = normalize(images_ref)[0].astype(jnp.bfloat16)
    y_ref[...] = normalize(texts_ref)[0].astype(jnp.bfloat16)
    x_ref[R:, :] = jnp.broadcast_to(pair_ref[...], (16, D)).astype(jnp.bfloat16)


def score_kernel(*refs):
    sc_ref, at_ref = refs[:2]
    xs = refs[2 : 2 + N_COL]
    ys = refs[2 + N_COL : 2 + N_COL + N_ROW]
    gx_out, gy_own, gy_sib, loss_ref, x_all, y_all, place, gx_acc, loss_acc = refs[2 + N_COL + N_ROW :]
    col, row_y, row_z, row_c = at_ref[0], at_ref[1], at_ref[2], at_ref[3]
    slope, shift, scale = sc_ref[0], sc_ref[1], sc_ref[2]
    for k, ref in enumerate(xs):
        x_all[k * R : (k + 1) * R, :] = ref[:R, :]
        tail = ref[R : R + 16, :].astype(jnp.float32).astype(jnp.int32)[:1, :]
        shard, offset = tail[:, :R], tail[:, 256 : 256 + R]
        rel = (
            ((shard & 1) ^ row_c) * 8
            + (((shard >> 2) - row_y) & 3) * 2
            + (((shard >> 1) & 1) ^ row_z)
        )
        place[:, k * R : (k + 1) * R] = jnp.where((shard >> 4) == col, rel * R + offset, -1)
    for k, ref in enumerate(ys):
        y_all[k * R : (k + 1) * R, :] = ref[...]
    gx_acc[...] = jnp.zeros_like(gx_acc)
    loss_acc[...] = jnp.zeros_like(loss_acc)
    x = x_all[...]

    def tile(base):
        y = y_all[pl.ds(base, BM), :]
        score = lax.dot_general(y, x, NT, preferred_element_type=jnp.float32)
        rows = base + lax.broadcasted_iota(jnp.int32, (BM, NX), 0)
        paired = place[...] == rows
        z = score * slope + shift
        z = jnp.where(paired, -z, z)
        t = jnp.exp2(z)
        total = 1.0 + t
        weight = (jnp.where(paired, -scale, scale) * (t / total)).astype(jnp.bfloat16)
        small = t * (1.0 - t * (0.5 - t * (1.0 / 3.0)))
        loss = jnp.where(t < 2.0**-6, small, jnp.log(total))
        loss_acc[...] += jnp.sum(loss.reshape(BM // 8, 8, NX), axis=0)
        gx_acc[...] += lax.dot_general(weight, y, TN, preferred_element_type=jnp.float32)
        return jnp.dot(weight, x, preferred_element_type=jnp.float32)

    half = NY // 2 // BM

    def sib_step(i, carry):
        base = pl.multiple_of(i * BM, BM)
        gy_sib[pl.ds(base, BM), :] = tile(base + NY // 2).astype(jnp.bfloat16)
        return carry

    def own_step(i, carry):
        base = pl.multiple_of(i * BM, BM)
        gy_own[pl.ds(base, BM), :] = tile(base)
        return carry

    lax.fori_loop(0, half, sib_step, 0)
    lax.fori_loop(0, half, own_step, 0)
    gx_out[...] = gx_acc[...].astype(jnp.bfloat16)
    loss_ref[...] = jnp.broadcast_to(jnp.sum(loss_acc[...]), (8, 128))


def final_kernel(values_ref, own_ref, *refs):
    out_ref = refs[-1]
    unit, inverse = normalize(values_ref)
    grad = own_ref[...].astype(jnp.float32)
    for ref in refs[:-1]:
        grad = grad + ref[...].astype(jnp.float32)
    along = jnp.sum(grad * unit, axis=-1, keepdims=True)
    out_ref[...] = (grad - unit * along) * inverse


def finish(values, own, *parts):
    return pl.pallas_call(
        final_kernel,
        in_specs=[VMEM] * (2 + len(parts)),
        out_specs=VMEM,
        out_shape=jax.ShapeDtypeStruct((R, D), jnp.float32),
        name="unproject",
    )(values, own, *parts)


def f32(value):
    return value.astype(jnp.float32)


def local(images, texts, pair_index, log_scale, bias):
    row, col = lax.axis_index("row"), lax.axis_index("col")
    shard = pair_index // R
    codes = jnp.zeros((1, D), jnp.float32)
    codes = codes.at[0, :R].set(shard.astype(jnp.float32)).at[0, 256 : 256 + R].set((pair_index - shard * R).astype(jnp.float32))
    x_low, y_low = pl.pallas_call(
        prep_kernel,
        in_specs=[VMEM] * 3,
        out_specs=[VMEM] * 2,
        out_shape=[jax.ShapeDtypeStruct((RX, D), jnp.bfloat16), jax.ShapeDtypeStruct((R, D), jnp.bfloat16)],
        name="prep",
    )(images, texts, codes)

    x_z = send_col(x_low, dz=1)
    y_z = send_row(y_low, dz=1)
    xs = [x_low, x_z] + [send_col(v, dx=d) for d in (1, 3, 2) for v in (x_low, x_z)]
    ys = [y_low, y_z] + [send_row(v, dy=d) for d in (1, 3, 2) for v in (y_low, y_z)]
    xs = [xs[i] for i in (0, 1, 4, 5, 6, 7, 2, 3)]
    ys = [ys[i] for i in (0, 1, 4, 5, 6, 7, 2, 3)]
    ys = ys + [send_row(v, dc=1) for v in ys]

    scale = jnp.exp(log_scale[0])
    scalars = jnp.stack([scale * LOG2E, bias[0] * LOG2E, scale])
    at = jnp.stack([col, row // 4, (row // 2) % 2, row % 2]).astype(jnp.int32)
    gx, gy_own, gy_sib, loss = pl.pallas_call(
        score_kernel,
        in_specs=[SMEM] * 2 + [VMEM] * (N_COL + N_ROW),
        out_specs=[VMEM] * 4,
        out_shape=[
            jax.ShapeDtypeStruct((NX, D), jnp.bfloat16),
            jax.ShapeDtypeStruct((NY // 2, D), jnp.float32),
            jax.ShapeDtypeStruct((NY // 2, D), jnp.bfloat16),
            jax.ShapeDtypeStruct((8, 128), jnp.float32),
        ],
        scratch_shapes=[
            pltpu.VMEM((NX, D), jnp.bfloat16),
            pltpu.VMEM((NY, D), jnp.bfloat16),
            pltpu.VMEM((1, NX), jnp.int32),
            pltpu.VMEM((NX, D), jnp.float32),
            pltpu.VMEM((8, NX), jnp.float32),
        ],
        compiler_params=pltpu.CompilerParams(vmem_limit_bytes=60 << 20),
        cost_estimate=pl.CostEstimate(flops=6 * NX * NY * D, bytes_accessed=20 << 20, transcendentals=0),
        name="score",
    )(scalars, at, *xs, *ys)

    gy_core = send_row(gy_sib, dc=1)
    gx = [gx[k * R : (k + 1) * R] for k in range(N_COL)]
    gx_far = [send_col(gx[2 * d + 1], dx=d) for d in (1, 2, 3)]
    gx_near = [send_col(gx[2 * d], dx=d) for d in (1, 2, 3)]
    gx_z = sum((f32(v) for v in gx_far), f32(gx[1])).astype(jnp.bfloat16)
    gx_z = send_col(gx_z, dz=1)

    gy = [gy_own[k * R : (k + 1) * R] + f32(gy_core[k * R : (k + 1) * R]) for k in range(N_ROW // 2)]
    low = [v.astype(jnp.bfloat16) for v in gy]
    gy_far = [send_row(low[2 * d + 1], dy=d) for d in (1, 2, 3)]
    gy_near = [send_row(low[2 * d], dy=d) for d in (1, 2, 3)]
    gy_z = sum((f32(v) for v in gy_far), gy[1]).astype(jnp.bfloat16)
    gy_z = send_row(gy_z, dz=1)

    loss = loss + send_row(loss, dc=1)
    loss = loss + send_row(loss, dz=1)
    loss = loss + send_row(loss, dy=1) + send_row(loss, dy=2) + send_row(loss, dy=3)
    loss = loss + send_col(loss, dz=1)
    loss = loss + send_col(loss, dx=1) + send_col(loss, dx=2) + send_col(loss, dx=3)
    loss = loss[0, :1] / (R * N_ROW * N_COL)

    grad_x = finish(images, gx[0], *gx_near, gx_z)
    grad_y = finish(texts, gy[0], *gy_near, gy_z)
    return loss, grad_x, grad_y


def solution(mesh):
    return jax.shard_map(
        local,
        mesh=mesh,
        in_specs=(P(("row", "col"), None), P(("col", "row"), None), P(("row", "col")), P(), P()),
        out_specs=(P(), P(("row", "col"), None), P(("col", "row"), None)),
        check_vma=False,
    )
```

time: 428 us -> 176 us (0.41)
  waiting for transfers between devices: 195 us -> 44 us
  matrix products: 95 us -> 0 us
  blocking collectives: 87.4 us -> 0 us
  starting transfers between devices: 0.16 us -> 63.8 us
  Pallas kernels: 0 us -> 46.5 us
  between operations: 17 us -> 4.12 us
  local copies, waits for them, and re-layouts: 14.2 us -> 6.88 us
    reduce_scatter x2 -> x0, waiting for transfers between devices: 117 us -> none  [the longest x1 102 us: local(): gy_unit = lax.psum_scatter(gy_part, 'row', scatter_dimension=0, tiled=True)]
    dot_general x9 -> x0, matrix products: 95 us -> none  [the longest x3 38.3 us: tile_weight(): lax.dot_general(x_block, y_part, (((1,), (1,)), ((), ())), preferred_elem...]
    all_gather x2 -> x0, waiting for transfers between devices: 77.1 us -> none  [the longest x1 39.4 us: local(): lax.all_gather(y_unit.astype(jnp.bfloat16), 'row', axis=0, tiled=True)]
    psum x1 -> x0, blocking collectives: 72.7 us -> none  [local(): loss_sum = lax.psum(total, ('row', 'col'))]
    ppermute x0 -> x46, starting transfers between devices: none -> 63.8 us  [the longest x28 31.9 us: send_row(): return lax.ppermute(value, 'row', row_pairs(dy, dz, dc))]
    pallas_call x0 -> x4, Pallas kernels: none -> 46.5 us  [the longest x1 39.2 us: local(): pl.pallas_call(score_kernel, in_specs=[SMEM] * 2 + [VMEM] * (N_COL + N_RO...]
    ppermute x0 -> x46, waiting for transfers between devices: none -> 44 us  [the longest x28 22.3 us: send_row(): return lax.ppermute(value, 'row', row_pairs(dy, dz, dc))]
    unnamed x1 -> x0, blocking collectives: 14.7 us -> none
  transfers between devices with their start and end apart: 4 -> 46, of which waited for: 4 -> 14; matrix products, arithmetic and copies ran while one was open for 2% -> 5% of each run, Pallas kernels for 0% -> 1%
where the time goes in v1:
time: 176 us
  starting transfers between devices  63.8 us (36%)
  Pallas kernels  46.5 us (26%)
  waiting for transfers between devices  44 us (25%)
  other arithmetic  10.1 us (6%)
  local copies, waits for them, and re-layouts  6.88 us (4%)
  between operations  4.12 us (2%)
    pallas_call x1, Pallas kernels, local(): pl.pallas_call(score_kernel, in_specs=[SMEM] * 2 + [VMEM] * (N_COL + N_RO...  39.2 us
    ppermute x28, starting transfers between devices, send_row(): return lax.ppermute(value, 'row', row_pairs(dy, dz, dc))  31.9 us
    ppermute x18, starting transfers between devices, send_col(): return lax.ppermute(value, 'col', col_pairs(dx, dz))  31.9 us
    ppermute x28, waiting for transfers between devices, send_row(): return lax.ppermute(value, 'row', row_pairs(dy, dz, dc))  22.3 us
    ppermute x18, waiting for transfers between devices, send_col(): return lax.ppermute(value, 'col', col_pairs(dx, dz))  21.7 us
    pallas_call x2, Pallas kernels, finish(): pl.pallas_call(final_kernel, in_specs=[VMEM] * (2 + len(parts)), out_spec...  5.25 us
  transfers between devices with their start and end apart: 46, of which 14 were waited for; matrix products, arithmetic and copies ran while one was open for 5% of the time, Pallas kernels for 1%

profile of v1, /device:TPU:0, one launch (start us, length us, event | category | flops | bytes accessed | tf_op | source)
XLA Modules:
  0.0 175.5 jit_solution(1365292764004078891)
XLA Ops:
  0.6 0.6 compare_reduce_fusion
  1.3 0.6 and_reduce_fusion
  1.9 0.6 slice.111
  2.5 0.7 subtract_convert_fusion
  3.2 0.7 convert_select_fusion
  3.9 1.4 broadcast_select_fusion
  5.2 0.8 scatter.9.pair_ref
  6.1 0.6 copy-done.9
  6.6 2.0 %prep.1 = (bf16[208,768]{1,0:T(8,128)(2,1)}, bf16[192,768]{1,0:T(8,128)(2,1)}) custom-call(bf16[192,768]{1,0:T(8,128)(2,1)} %values_ref.2, bf16[192,768]{1,0:T(8,128)(2,1)} %values_ref.3, f32[1,768]{1,0:T(1,128)} %copy-done.9), custom_call_target="tpu_custom_call" | custom-call | tf_op jit(solution)/shard_map/prep/pallas_call | solution.py:144
  8.7 1.7 collective-permute-start.12
  10.3 2.9 %collective-permute-start.10 = (bf16[192,768]{1,0:T(8,128)(2,1)}, bf16[192,768]{1,0:T(8,128)(2,1)S(1)}, u32[]{:S(2)}, u32[]{:S(2)}) collective-permute-start(bf16[192,768]{1,0:T(8,128)(2,1)} %get-tuple-element.34.refs_10_), channel_id=1, source_target_pairs={{0,64},{8,72},{16,80},{24,88},{32,96},{40,104},{48,112},{56,120},{... | collective-permute-start | bytes 884744 | tf_op jit(solution)/shard_map/ppermute | solution.py:39
  13.2 1.3 collective-permute-start.8
  14.6 1.5 collective-permute-start.5
  16.1 2.7 %collective-permute-start.3 = (bf16[208,768]{1,0:T(8,128)(2,1)}, bf16[208,768]{1,0:T(8,128)(2,1)S(1)}, u32[]{:S(2)}, u32[]{:S(2)}) collective-permute-start(bf16[208,768]{1,0:T(8,128)(2,1)} %get-tuple-element.33.refs_2_), channel_id=1, source_target_pairs={{0,2},{1,3},{2,0},{3,1},{4,6},{5,7},{6,4},{7,5},{8,10},{9,11},{10,... | collective-permute-start | bytes 958472 | tf_op jit(solution)/shard_map/ppermute | solution.py:43
  18.8 0.8 collective-permute-done.12.refs_16_
  19.7 1.9 %collective-permute-start.7 = (bf16[192,768]{1,0:T(8,128)(2,1)}, bf16[192,768]{1,0:T(8,128)(2,1)S(1)}, u32[]{:S(2)}, u32[]{:S(2)}) collective-permute-start(bf16[192,768]{1,0:T(8,128)(2,1)} %get-tuple-element.34.refs_10_), channel_id=1, source_target_pairs={{0,16},{8,24},{16,0},{24,8},{32,48},{40,56},{48,32},{56,40},{64,80... | collective-permute-start | bytes 884744 | tf_op jit(solution)/shard_map/ppermute | solution.py:39
  21.6 5.6 %collective-permute-done.10.refs_14_ = bf16[192,768]{1,0:T(8,128)(2,1)S(1)} collective-permute-done((bf16[192,768]{1,0:T(8,128)(2,1)}, bf16[192,768]{1,0:T(8,128)(2,1)S(1)}, u32[]{:S(2)}, u32[]{:S(2)}) %collective-permute-start.10) | collective-permute-done | bytes 294944 | tf_op jit(solution)/shard_map/ppermute | solution.py:39
  27.2 2.8 %collective-permute-start.1 = (bf16[208,768]{1,0:T(8,128)(2,1)}, bf16[208,768]{1,0:T(8,128)(2,1)S(1)}, u32[]{:S(2)}, u32[]{:S(2)}) collective-permute-start(bf16[208,768]{1,0:T(8,128)(2,1)} %get-tuple-element.33.refs_2_), channel_id=1, source_target_pairs={{0,3},{1,0},{2,1},{3,2},{4,7},{5,4},{6,5},{7,6},{8,11},{9,8},{10,9... | collective-permute-start | bytes 958472 | tf_op jit(solution)/shard_map/ppermute | solution.py:43
  29.9 3.9 %collective-permute-start = (bf16[208,768]{1,0:T(8,128)(2,1)}, bf16[208,768]{1,0:T(8,128)(2,1)S(1)}, u32[]{:S(2)}, u32[]{:S(2)}) collective-permute-start(bf16[208,768]{1,0:T(8,128)(2,1)} %get-tuple-element.33.refs_2_), channel_id=1, source_target_pairs={{0,4},{1,5},{2,6},{3,7},{4,0},{5,1},{6,2},{7,3},{8,12},{9,13},{10,... | collective-permute-start | bytes 958472 | tf_op jit(solution)/shard_map/ppermute | solution.py:43
  33.8 0.5 collective-permute-start.18
  34.4 2.5 %collective-permute-done.1.refs_4_ = bf16[208,768]{1,0:T(8,128)(2,1)S(1)} collective-permute-done((bf16[208,768]{1,0:T(8,128)(2,1)}, bf16[208,768]{1,0:T(8,128)(2,1)S(1)}, u32[]{:S(2)}, u32[]{:S(2)}) %collective-permute-start.1) | collective-permute-done | bytes 319520 | tf_op jit(solution)/shard_map/ppermute | solution.py:43
  36.9 4.3 %collective-permute-done.refs_3_ = bf16[208,768]{1,0:T(8,128)(2,1)S(1)} collective-permute-done((bf16[208,768]{1,0:T(8,128)(2,1)}, bf16[208,768]{1,0:T(8,128)(2,1)S(1)}, u32[]{:S(2)}, u32[]{:S(2)}) %collective-permute-start) | collective-permute-done | bytes 319520 | tf_op jit(solution)/shard_map/ppermute | solution.py:43
  41.3 4.4 %collective-permute-start.11 = (bf16[192,768]{1,0:T(8,128)(2,1)S(1)}, bf16[192,768]{1,0:T(8,128)(2,1)}, u32[]{:S(2)}, u32[]{:S(2)}) collective-permute-start(bf16[192,768]{1,0:T(8,128)(2,1)S(1)} %collective-permute-done.7.refs_11_), channel_id=1, source_target_pairs={{0,64},{8,72},{16,80},{24,88},{32,96},{40,104},{48,112},{56,120},{... | collective-permute-start | bytes 884744 | tf_op jit(solution)/shard_map/ppermute | solution.py:39
  45.7 2.6 %collective-permute-start.9 = (bf16[192,768]{1,0:T(8,128)(2,1)S(1)}, bf16[192,768]{1,0:T(8,128)(2,1)}, u32[]{:S(2)}, u32[]{:S(2)}) collective-permute-start(bf16[192,768]{1,0:T(8,128)(2,1)S(1)} %collective-permute-done.7.refs_11_), channel_id=1, source_target_pairs={{0,96},{8,104},{16,112},{24,120},{32,0},{40,8},{48,16},{56,24},{64... | collective-permute-start | bytes 884744 | tf_op jit(solution)/shard_map/ppermute | solution.py:39
  48.2 2.8 %collective-permute-start.4 = (bf16[208,768]{1,0:T(8,128)(2,1)S(1)}, bf16[208,768]{1,0:T(8,128)(2,1)S(1)}, u32[]{:S(2)}, u32[]{:S(2)}) collective-permute-start(bf16[208,768]{1,0:T(8,128)(2,1)S(1)} %collective-permute-done.refs_3_), channel_id=1, source_target_pairs={{0,2},{1,3},{2,0},{3,1},{4,6},{5,7},{6,4},{7,5},{8,10},{9,11},{10,... | collective-permute-start | bytes 958472 | tf_op jit(solution)/shard_map/ppermute | solution.py:43
  51.1 5.5 %collective-permute-done.13.refs_17_ = bf16[192,768]{1,0:T(8,128)(2,1)} collective-permute-done((bf16[192,768]{1,0:T(8,128)(2,1)S(1)}, bf16[192,768]{1,0:T(8,128)(2,1)}, u32[]{:S(2)}, u32[]{:S(2)}) %collective-permute-start.13) | collective-permute-done | bytes 294944 | tf_op jit(solution)/shard_map/ppermute | solution.py:39
  56.6 0.7 collective-permute-done.9.refs_13_
  59.4 0.6 pad_maximum_fusion.refs_0_
  60.0 0.7 pad_add_fusion.refs_1_
  60.7 3.0 %collective-permute-done.2.refs_5_ = bf16[208,768]{1,0:T(8,128)(2,1)S(1)} collective-permute-done((bf16[208,768]{1,0:T(8,128)(2,1)S(1)}, bf16[208,768]{1,0:T(8,128)(2,1)S(1)}, u32[]{:S(2)}, u32[]{:S(2)}) %collective-permute-start.2) | collective-permute-done | bytes 319520 | tf_op jit(solution)/shard_map/ppermute | solution.py:43
  63.8 0.6 copy-done.16
  64.4 39.2 %score.1 = (bf16[1536,768]{1,0:T(8,128)(2,1)}, f32[1536,768]{1,0:T(8,128)}, bf16[1536,768]{1,0:T(8,128)(2,1)}, f32[8,128]{1,0:T(8,128)}) custom-call(f32[3]{0:T(128)} %pad_maximum_fusion.refs_0_, s32[4]{0:T(128)} %pad_add_fusion.refs_1_, bf16[208,768]{1,0:T(8,128)(2,1)} %get-tuple-element.33.refs_2_, bf16[208,768]{1,0:T(8,128)(2,1)} %copy-done.13, ...), custom_call_target="tpu_custom_call" | custom-call | flops 21743271936 | bytes 20971520 | tf_op jit(solution)/shard_map/score/pallas_call | solution.py:163
  103.7 0.5 collective-permute-start.22
  104.2 4.2 %collective-permute-done.22 = f32[8,128]{1,0:T(8,128)S(1)} collective-permute-done((f32[8,128]{1,0:T(8,128)}, f32[8,128]{1,0:T(8,128)S(1)}, u32[]{:S(2)}, u32[]{:S(2)}) %collective-permute-start.22) | collective-permute-done | bytes 4128 | tf_op jit(solution)/shard_map/ppermute | solution.py:39
  108.5 0.7 add.87
  109.1 0.8 collective-permute-start.23
  110.0 2.8 %collective-permute-done.23 = f32[8,128]{1,0:T(8,128)S(1)} collective-permute-done((f32[8,128]{1,0:T(8,128)S(1)}, f32[8,128]{1,0:T(8,128)S(1)}, u32[]{:S(2)}, u32[]{:S(2)}) %collective-permute-start.23) | collective-permute-done | bytes 4128 | tf_op jit(solution)/shard_map/ppermute | solution.py:39
  112.8 1.5 collective-permute-start.25
  114.2 1.4 collective-permute-start.24
  115.6 2.3 %fusion = (bf16[192,768]{1,0:T(8,128)(2,1)S(1)}, bf16[192,768]{1,0:T(8,128)(2,1)S(1)}, bf16[192,768]{1,0:T(8,128)(2,1)S(1)}, bf16[192,768]{1,0:T(8,128)(2,1)S(1)...) fusion(bf16[1536,768]{1,0:T(8,128)(2,1)} %get-tuple-element.36), kind=kLoop, calls=%fused_computation.21 | loop fusion | bytes 4128768 | tf_op jit(solution)/shard_map/slice | solution.py:186
  118.3 3.0 %collective-permute-start.36 = (bf16[192,768]{1,0:T(8,128)(2,1)S(1)}, bf16[192,768]{1,0:T(8,128)(2,1)S(1)}, u32[]{:S(2)}, u32[]{:S(2)}) collective-permute-start(bf16[192,768]{1,0:T(8,128)(2,1)S(1)} %get-tuple-element.50), channel_id=1, source_target_pairs={{0,3},{1,0},{2,1},{3,2},{4,7},{5,4},{6,5},{7,6},{8,11},{9,8},{10,9... | collective-permute-start | bytes 884744 | tf_op jit(solution)/shard_map/ppermute | solution.py:43
  121.2 1.1 collective-permute-start.35
  122.3 2.4 %collective-permute-start.27 = (f32[8,128]{1,0:T(8,128)S(1)}, f32[8,128]{1,0:T(8,128)S(1)}, u32[]{:S(2)}, u32[]{:S(2)}) collective-permute-start(f32[8,128]{1,0:T(8,128)S(1)} %add_add_fusion.1), channel_id=1, source_target_pairs={{0,4},{1,5},{2,6},{3,7},{4,0},{5,1},{6,2},{7,3},{8,12},{9,13},{10,... | collective-permute-start | bytes 12296 | tf_op jit(solution)/shard_map/ppermute | solution.py:43
  124.7 1.8 %add_convert_fusion.3 = (bf16[192,768]{1,0:T(8,128)(2,1)S(1)}, bf16[192,768]{1,0:T(8,128)(2,1)S(1)}, bf16[192,768]{1,0:T(8,128)(2,1)S(1)}) fusion(f32[1536,768]{1,0:T(8,128)} %get-tuple-element.37, bf16[1536,768]{1,0:T(8,128)(2,1)S(1)} %collective-permute-done.38), kind=kLoop, calls=%fused_computation.3 | loop fusion | flops 1327104 | bytes 3538944 | tf_op jit(solution)/shard_map/convert_element_type | solution.py:193
  126.5 1.8 %collective-permute-start.42 = (bf16[192,768]{1,0:T(8,128)(2,1)S(1)}, bf16[192,768]{1,0:T(8,128)(2,1)S(1)}, u32[]{:S(2)}, u32[]{:S(2)}) collective-permute-start(bf16[192,768]{1,0:T(8,128)(2,1)S(1)} %get-tuple-element.46), channel_id=1, source_target_pairs={{0,32},{8,40},{16,48},{24,56},{32,64},{40,72},{48,80},{56,88},{64,... | collective-permute-start | bytes 884744 | tf_op jit(solution)/shard_map/ppermute | solution.py:39
  128.3 1.5 collective-permute-start.44
  129.8 2.9 %collective-permute-start.43 = (bf16[192,768]{1,0:T(8,128)(2,1)S(1)}, bf16[192,768]{1,0:T(8,128)(2,1)S(1)}, u32[]{:S(2)}, u32[]{:S(2)}) collective-permute-start(bf16[192,768]{1,0:T(8,128)(2,1)S(1)} %get-tuple-element.48), channel_id=1, source_target_pairs={{0,64},{8,72},{16,80},{24,88},{32,96},{40,104},{48,112},{56,120},{... | collective-permute-start | bytes 884744 | tf_op jit(solution)/shard_map/ppermute | solution.py:39
  133.1 3.7 %collective-permute-start.33 = (bf16[192,768]{1,0:T(8,128)(2,1)S(1)}, bf16[192,768]{1,0:T(8,128)(2,1)S(1)}, u32[]{:S(2)}, u32[]{:S(2)}) collective-permute-start(bf16[192,768]{1,0:T(8,128)(2,1)S(1)} %get-tuple-element.52), channel_id=1, source_target_pairs={{0,3},{1,0},{2,1},{3,2},{4,7},{5,4},{6,5},{7,6},{8,11},{9,8},{10,9... | collective-permute-start | bytes 884744 | tf_op jit(solution)/shard_map/ppermute | solution.py:43
  136.8 1.1 add_convert_fusion.7
  137.9 6.3 %collective-permute-done.30 = f32[8,128]{1,0:T(8,128)S(1)} collective-permute-done((f32[8,128]{1,0:T(8,128)S(1)}, f32[8,128]{1,0:T(8,128)S(1)}, u32[]{:S(2)}, u32[]{:S(2)}) %collective-permute-start.30) | collective-permute-done | bytes 4128 | tf_op jit(solution)/shard_map/ppermute | solution.py:43
  144.3 4.5 %collective-permute-start.31 = (bf16[192,768]{1,0:T(8,128)(2,1)S(1)}, bf16[192,768]{1,0:T(8,128)(2,1)S(1)}, u32[]{:S(2)}, u32[]{:S(2)}) collective-permute-start(bf16[192,768]{1,0:T(8,128)(2,1)S(1)} %get-tuple-element.54), channel_id=1, source_target_pairs={{0,1},{1,2},{2,3},{3,0},{4,5},{5,6},{6,7},{7,4},{8,9},{9,10},{10,1... | collective-permute-start | bytes 884744 | tf_op jit(solution)/shard_map/ppermute | solution.py:43
  148.8 0.6 collective-permute-start.29
  149.5 1.3 add_convert_fusion
  150.7 5.0 %collective-permute-done.29 = f32[8,128]{1,0:T(8,128)S(1)} collective-permute-done((f32[8,128]{1,0:T(8,128)S(1)}, f32[8,128]{1,0:T(8,128)S(1)}, u32[]{:S(2)}, u32[]{:S(2)}) %collective-permute-start.29) | collective-permute-done | bytes 4128 | tf_op jit(solution)/shard_map/ppermute | solution.py:43
  155.8 2.5 %collective-permute-start.37 = (bf16[192,768]{1,0:T(8,128)(2,1)S(1)}, bf16[192,768]{1,0:T(8,128)(2,1)S(1)}, u32[]{:S(2)}, u32[]{:S(2)}) collective-permute-start(bf16[192,768]{1,0:T(8,128)(2,1)S(1)} %add_convert_fusion.7), channel_id=1, source_target_pairs={{0,4},{1,5},{2,6},{3,7},{4,0},{5,1},{6,2},{7,3},{8,12},{9,13},{10,... | collective-permute-start | bytes 884744 | tf_op jit(solution)/shard_map/ppermute | solution.py:43
  158.3 1.2 collective-permute-start.45
  159.6 3.3 %collective-permute-start.40 = (bf16[192,768]{1,0:T(8,128)(2,1)S(1)}, bf16[192,768]{1,0:T(8,128)(2,1)S(1)}, u32[]{:S(2)}, u32[]{:S(2)}) collective-permute-start(bf16[192,768]{1,0:T(8,128)(2,1)S(1)} %get-tuple-element.43), channel_id=1, source_target_pairs={{0,64},{8,72},{16,80},{24,88},{32,96},{40,104},{48,112},{56,120},{... | collective-permute-start | bytes 884744 | tf_op jit(solution)/shard_map/ppermute | solution.py:39
  162.8 1.1 collective-permute-start.39
  163.9 0.5 slice.112
  165.1 0.7 copy-done.4
  165.8 2.6 %unproject.2 = f32[192,768]{1,0:T(8,128)} custom-call(bf16[192,768]{1,0:T(8,128)(2,1)} %values_ref.2, bf16[192,768]{1,0:T(8,128)(2,1)} %get-tuple-element.55.own_ref, bf16[192,768]{1,0:T(8,128)(2,1)} %copy-done.3, bf16[192,768]{1,0:T(8,128)(2,1)} %copy-done.2, bf16[192,768]{1,0:T(8,128)(2,1)} %copy-done.1, bf16[192,768]{1,0:T(8,128)(2,1)} %copy-done.4), custom_call_target="tpu_custom_call" | custom-call | tf_op jit(solution)/shard_map/unproject/pallas_call | solution.py:126
  168.4 2.6 %collective-permute-done.39.refs_0_ = bf16[192,768]{1,0:T(8,128)(2,1)S(1)} collective-permute-done((bf16[192,768]{1,0:T(8,128)(2,1)S(1)}, bf16[192,768]{1,0:T(8,128)(2,1)S(1)}, u32[]{:S(2)}, u32[]{:S(2)}) %collective-permute-start.39) | collective-permute-done | bytes 294944 | tf_op jit(solution)/shard_map/ppermute | solution.py:39
  171.0 0.7 copy-done.8
  171.7 2.7 %unproject.3 = f32[192,768]{1,0:T(8,128)} custom-call(bf16[192,768]{1,0:T(8,128)(2,1)} %values_ref.3, f32[192,768]{1,0:T(8,128)} %get-tuple-element.45.own_ref, bf16[192,768]{1,0:T(8,128)(2,1)} %copy-done.8, bf16[192,768]{1,0:T(8,128)(2,1)} %copy-done.7, bf16[192,768]{1,0:T(8,128)(2,1)} %copy-done.6, bf16[192,768]{1,0:T(8,128)(2,1)} %copy-done.5), custom_call_target="tpu_custom_call" | custom-call | tf_op jit(solution)/shard_map/unproject/pallas_call | solution.py:126
  (103 shorter events, 1.9 us)
Async XLA Ops:
  8.7 7.4 %collective-permute-start.14 = (bf16[192,768]{1,0:T(8,128)(2,1)}, bf16[192,768]{1,0:T(8,128)(2,1)S(1)}, u32[]{:S(2)}, u32[]{:S(2)}) collective-permute-start(bf16[192,768]{1,0:T(8,128)(2,1)} %get-tuple-element.34.refs_10_), channel_id=1, source_target_pairs={{0,8},{8,0},{16,24},{24,16},{32,40},{40,32},{48,56},{56,48},{64,72... | collective-permute-start | bytes 884744 | tf_op jit(solution)/shard_map/ppermute | solution.py:39
  8.7 11.0 %collective-permute-start.12 = (bf16[192,768]{1,0:T(8,128)(2,1)}, bf16[192,768]{1,0:T(8,128)(2,1)S(1)}, u32[]{:S(2)}, u32[]{:S(2)}) collective-permute-start(bf16[192,768]{1,0:T(8,128)(2,1)} %get-tuple-element.34.refs_10_), channel_id=1, source_target_pairs={{0,32},{8,40},{16,48},{24,56},{32,64},{40,72},{48,80},{56,88},{64,... | collective-permute-start | bytes 884744 | tf_op jit(solution)/shard_map/ppermute | solution.py:39
  10.3 16.8 %collective-permute-start.10 = (bf16[192,768]{1,0:T(8,128)(2,1)}, bf16[192,768]{1,0:T(8,128)(2,1)S(1)}, u32[]{:S(2)}, u32[]{:S(2)}) collective-permute-start(bf16[192,768]{1,0:T(8,128)(2,1)} %get-tuple-element.34.refs_10_), channel_id=1, source_target_pairs={{0,64},{8,72},{16,80},{24,88},{32,96},{40,104},{48,112},{56,120},{... | collective-permute-start | bytes 884744 | tf_op jit(solution)/shard_map/ppermute | solution.py:39
  13.2 16.7 %collective-permute-start.8 = (bf16[192,768]{1,0:T(8,128)(2,1)}, bf16[192,768]{1,0:T(8,128)(2,1)S(1)}, u32[]{:S(2)}, u32[]{:S(2)}) collective-permute-start(bf16[192,768]{1,0:T(8,128)(2,1)} %get-tuple-element.34.refs_10_), channel_id=1, source_target_pairs={{0,96},{8,104},{16,112},{24,120},{32,0},{40,8},{48,16},{56,24},{64... | collective-permute-start | bytes 884744 | tf_op jit(solution)/shard_map/ppermute | solution.py:39
  14.6 19.2 %collective-permute-start.5 = (bf16[208,768]{1,0:T(8,128)(2,1)}, bf16[208,768]{1,0:T(8,128)(2,1)S(1)}, u32[]{:S(2)}, u32[]{:S(2)}) collective-permute-start(bf16[208,768]{1,0:T(8,128)(2,1)} %get-tuple-element.33.refs_2_), channel_id=1, source_target_pairs={{0,1},{1,2},{2,3},{3,0},{4,5},{5,6},{6,7},{7,4},{8,9},{9,10},{10,1... | collective-permute-start | bytes 958472 | tf_op jit(solution)/shard_map/ppermute | solution.py:43
  16.1 47.6 %copy-start.17 = (bf16[192,768]{1,0:T(8,128)(2,1)}, bf16[192,768]{1,0:T(8,128)(2,1)S(1)}, u32[]{:S(2)}) copy-start(bf16[192,768]{1,0:T(8,128)(2,1)S(1)} %collective-permute-done.14.refs_18_) | copy-start | bytes 884740
  16.1 18.2 %collective-permute-start.3 = (bf16[208,768]{1,0:T(8,128)(2,1)}, bf16[208,768]{1,0:T(8,128)(2,1)S(1)}, u32[]{:S(2)}, u32[]{:S(2)}) collective-permute-start(bf16[208,768]{1,0:T(8,128)(2,1)} %get-tuple-element.33.refs_2_), channel_id=1, source_target_pairs={{0,2},{1,3},{2,0},{3,1},{4,6},{5,7},{6,4},{7,5},{8,10},{9,11},{10,... | collective-permute-start | bytes 958472 | tf_op jit(solution)/shard_map/ppermute | solution.py:43
  19.7 44.0 %copy-start.18 = (bf16[192,768]{1,0:T(8,128)(2,1)}, bf16[192,768]{1,0:T(8,128)(2,1)S(1)}, u32[]{:S(2)}) copy-start(bf16[192,768]{1,0:T(8,128)(2,1)S(1)} %collective-permute-done.12.refs_16_) | copy-start | bytes 884740
  19.7 14.1 %collective-permute-start.7 = (bf16[192,768]{1,0:T(8,128)(2,1)}, bf16[192,768]{1,0:T(8,128)(2,1)S(1)}, u32[]{:S(2)}, u32[]{:S(2)}) collective-permute-start(bf16[192,768]{1,0:T(8,128)(2,1)} %get-tuple-element.34.refs_10_), channel_id=1, source_target_pairs={{0,16},{8,24},{16,0},{24,8},{32,48},{40,56},{48,32},{56,40},{64,80... | collective-permute-start | bytes 884744 | tf_op jit(solution)/shard_map/ppermute | solution.py:39
  27.2 36.6 %copy-start.19 = (bf16[192,768]{1,0:T(8,128)(2,1)}, bf16[192,768]{1,0:T(8,128)(2,1)S(1)}, u32[]{:S(2)}) copy-start(bf16[192,768]{1,0:T(8,128)(2,1)S(1)} %collective-permute-done.10.refs_14_) | copy-start | bytes 884740
  27.2 9.8 %collective-permute-start.1 = (bf16[208,768]{1,0:T(8,128)(2,1)}, bf16[208,768]{1,0:T(8,128)(2,1)S(1)}, u32[]{:S(2)}, u32[]{:S(2)}) collective-permute-start(bf16[208,768]{1,0:T(8,128)(2,1)} %get-tuple-element.33.refs_2_), channel_id=1, source_target_pairs={{0,3},{1,0},{2,1},{3,2},{4,7},{5,4},{6,5},{7,6},{8,11},{9,8},{10,9... | collective-permute-start | bytes 958472 | tf_op jit(solution)/shard_map/ppermute | solution.py:43
  29.9 33.8 %copy-start.20 = (bf16[192,768]{1,0:T(8,128)(2,1)}, bf16[192,768]{1,0:T(8,128)(2,1)S(1)}, u32[]{:S(2)}) copy-start(bf16[192,768]{1,0:T(8,128)(2,1)S(1)} %collective-permute-done.8.refs_12_) | copy-start | bytes 884740
  29.9 11.3 %collective-permute-start = (bf16[208,768]{1,0:T(8,128)(2,1)}, bf16[208,768]{1,0:T(8,128)(2,1)S(1)}, u32[]{:S(2)}, u32[]{:S(2)}) collective-permute-start(bf16[208,768]{1,0:T(8,128)(2,1)} %get-tuple-element.33.refs_2_), channel_id=1, source_target_pairs={{0,4},{1,5},{2,6},{3,7},{4,0},{5,1},{6,2},{7,3},{8,12},{9,13},{10,... | collective-permute-start | bytes 958472 | tf_op jit(solution)/shard_map/ppermute | solution.py:43
  33.8 23.8 %copy-start.21 = (bf16[192,768]{1,0:T(8,128)(2,1)}, bf16[192,768]{1,0:T(8,128)(2,1)S(1)}, u32[]{:S(2)}) copy-start(bf16[192,768]{1,0:T(8,128)(2,1)S(1)} %collective-permute-done.7.refs_11_) | copy-start | bytes 884740
  33.8 7.4 %collective-permute-start.20 = (bf16[192,768]{1,0:T(8,128)(2,1)S(1)}, bf16[192,768]{1,0:T(8,128)(2,1)}, u32[]{:S(2)}, u32[]{:S(2)}) collective-permute-start(bf16[192,768]{1,0:T(8,128)(2,1)S(1)} %collective-permute-done.12.refs_16_), channel_id=1, source_target_pairs={{0,8},{8,0},{16,24},{24,16},{32,40},{40,32},{48,56},{56,48},{64,72... | collective-permute-start | bytes 884744 | tf_op jit(solution)/shard_map/ppermute | solution.py:39
  33.8 29.9 %copy-start.10 = (bf16[208,768]{1,0:T(8,128)(2,1)}, bf16[208,768]{1,0:T(8,128)(2,1)S(1)}, u32[]{:S(2)}) copy-start(bf16[208,768]{1,0:T(8,128)(2,1)S(1)} %collective-permute-done.5.refs_8_) | copy-start | bytes 958468
  33.8 7.4 %collective-permute-start.18 = (bf16[192,768]{1,0:T(8,128)(2,1)S(1)}, bf16[192,768]{1,0:T(8,128)(2,1)S(1)}, u32[]{:S(2)}, u32[]{:S(2)}) collective-permute-start(bf16[192,768]{1,0:T(8,128)(2,1)S(1)} %collective-permute-done.10.refs_14_), channel_id=1, source_target_pairs={{0,8},{8,0},{16,24},{24,16},{32,40},{40,32},{48,56},{56,48},{64,72... | collective-permute-start | bytes 884744 | tf_op jit(solution)/shard_map/ppermute | solution.py:39
  34.3 29.4 %copy-start.11 = (bf16[208,768]{1,0:T(8,128)(2,1)}, bf16[208,768]{1,0:T(8,128)(2,1)S(1)}, u32[]{:S(2)}) copy-start(bf16[208,768]{1,0:T(8,128)(2,1)S(1)} %collective-permute-done.3.refs_6_) | copy-start | bytes 958468
  34.3 11.3 %collective-permute-start.16 = (bf16[192,768]{1,0:T(8,128)(2,1)S(1)}, bf16[192,768]{1,0:T(8,128)(2,1)S(1)}, u32[]{:S(2)}, u32[]{:S(2)}) collective-permute-start(bf16[192,768]{1,0:T(8,128)(2,1)S(1)} %collective-permute-done.8.refs_12_), channel_id=1, source_target_pairs={{0,8},{8,0},{16,24},{24,16},{32,40},{40,32},{48,56},{56,48},{64,72... | collective-permute-start | bytes 884744 | tf_op jit(solution)/shard_map/ppermute | solution.py:39
  36.9 26.8 %copy-start.12 = (bf16[208,768]{1,0:T(8,128)(2,1)}, bf16[208,768]{1,0:T(8,128)(2,1)S(1)}, u32[]{:S(2)}) copy-start(bf16[208,768]{1,0:T(8,128)(2,1)S(1)} %collective-permute-done.1.refs_4_) | copy-start | bytes 958468
  36.9 11.3 %collective-permute-start.15 = (bf16[192,768]{1,0:T(8,128)(2,1)S(1)}, bf16[192,768]{1,0:T(8,128)(2,1)S(1)}, u32[]{:S(2)}, u32[]{:S(2)}) collective-permute-start(bf16[192,768]{1,0:T(8,128)(2,1)S(1)} %collective-permute-done.7.refs_11_), channel_id=1, source_target_pairs={{0,8},{8,0},{16,24},{24,16},{32,40},{40,32},{48,56},{56,48},{64,72... | collective-permute-start | bytes 884744 | tf_op jit(solution)/shard_map/ppermute | solution.py:39
  41.2 22.6 %copy-start.13 = (bf16[208,768]{1,0:T(8,128)(2,1)}, bf16[208,768]{1,0:T(8,128)(2,1)S(1)}, u32[]{:S(2)}) copy-start(bf16[208,768]{1,0:T(8,128)(2,1)S(1)} %collective-permute-done.refs_3_) | copy-start | bytes 958468
  41.2 15.4 %collective-permute-start.13 = (bf16[192,768]{1,0:T(8,128)(2,1)S(1)}, bf16[192,768]{1,0:T(8,128)(2,1)}, u32[]{:S(2)}, u32[]{:S(2)}) collective-permute-start(bf16[192,768]{1,0:T(8,128)(2,1)S(1)} %collective-permute-done.7.refs_11_), channel_id=1, source_target_pairs={{0,32},{8,40},{16,48},{24,56},{32,64},{40,72},{48,80},{56,88},{64,... | collective-permute-start | bytes 884744 | tf_op jit(solution)/shard_map/ppermute | solution.py:39
  41.2 16.4 %collective-permute-start.6 = (bf16[208,768]{1,0:T(8,128)(2,1)S(1)}, bf16[208,768]{1,0:T(8,128)(2,1)S(1)}, u32[]{:S(2)}, u32[]{:S(2)}) collective-permute-start(bf16[208,768]{1,0:T(8,128)(2,1)S(1)} %collective-permute-done.refs_3_), channel_id=1, source_target_pairs={{0,1},{1,2},{2,3},{3,0},{4,5},{5,6},{6,7},{7,4},{8,9},{9,10},{10,1... | collective-permute-start | bytes 958472 | tf_op jit(solution)/shard_map/ppermute | solution.py:43
  41.3 6.9 %copy-start.22 = (bf16[192,768]{1,0:T(8,128)(2,1)}, bf16[192,768]{1,0:T(8,128)(2,1)S(1)}, u32[]{:S(2)}) copy-start(bf16[192,768]{1,0:T(8,128)(2,1)S(1)} %collective-permute-done.18.refs_22_) | copy-start | bytes 884740
  41.3 15.3 %collective-permute-start.11 = (bf16[192,768]{1,0:T(8,128)(2,1)S(1)}, bf16[192,768]{1,0:T(8,128)(2,1)}, u32[]{:S(2)}, u32[]{:S(2)}) collective-permute-start(bf16[192,768]{1,0:T(8,128)(2,1)S(1)} %collective-permute-done.7.refs_11_), channel_id=1, source_target_pairs={{0,64},{8,72},{16,80},{24,88},{32,96},{40,104},{48,112},{56,120},{... | collective-permute-start | bytes 884744 | tf_op jit(solution)/shard_map/ppermute | solution.py:39
  45.7 11.6 %collective-permute-start.9 = (bf16[192,768]{1,0:T(8,128)(2,1)S(1)}, bf16[192,768]{1,0:T(8,128)(2,1)}, u32[]{:S(2)}, u32[]{:S(2)}) collective-permute-start(bf16[192,768]{1,0:T(8,128)(2,1)S(1)} %collective-permute-done.7.refs_11_), channel_id=1, source_target_pairs={{0,96},{8,104},{16,112},{24,120},{32,0},{40,8},{48,16},{56,24},{64... | collective-permute-start | bytes 884744 | tf_op jit(solution)/shard_map/ppermute | solution.py:39
  48.2 9.8 %copy-start.24 = (bf16[192,768]{1,0:T(8,128)(2,1)}, bf16[192,768]{1,0:T(8,128)(2,1)S(1)}, u32[]{:S(2)}) copy-start(bf16[192,768]{1,0:T(8,128)(2,1)S(1)} %collective-permute-done.15.refs_19_) | copy-start | bytes 884740
  48.2 12.4 %collective-permute-start.4 = (bf16[208,768]{1,0:T(8,128)(2,1)S(1)}, bf16[208,768]{1,0:T(8,128)(2,1)S(1)}, u32[]{:S(2)}, u32[]{:S(2)}) collective-permute-start(bf16[208,768]{1,0:T(8,128)(2,1)S(1)} %collective-permute-done.refs_3_), channel_id=1, source_target_pairs={{0,2},{1,3},{2,0},{3,1},{4,6},{5,7},{6,4},{7,5},{8,10},{9,11},{10,... | collective-permute-start | bytes 958472 | tf_op jit(solution)/shard_map/ppermute | solution.py:43
  56.6 7.1 %collective-permute-start.2 = (bf16[208,768]{1,0:T(8,128)(2,1)S(1)}, bf16[208,768]{1,0:T(8,128)(2,1)S(1)}, u32[]{:S(2)}, u32[]{:S(2)}) collective-permute-start(bf16[208,768]{1,0:T(8,128)(2,1)S(1)} %collective-permute-done.refs_3_), channel_id=1, source_target_pairs={{0,3},{1,0},{2,1},{3,2},{4,7},{5,4},{6,5},{7,6},{8,11},{9,8},{10,9... | collective-permute-start | bytes 958472 | tf_op jit(solution)/shard_map/ppermute | solution.py:43
  56.6 7.1 %collective-permute-start.21 = (bf16[192,768]{1,0:T(8,128)(2,1)}, bf16[192,768]{1,0:T(8,128)(2,1)}, u32[]{:S(2)}, u32[]{:S(2)}) collective-permute-start(bf16[192,768]{1,0:T(8,128)(2,1)} %collective-permute-done.13.refs_17_), channel_id=1, source_target_pairs={{0,8},{8,0},{16,24},{24,16},{32,40},{40,32},{48,56},{56,48},{64,72... | collective-permute-start | bytes 884744 | tf_op jit(solution)/shard_map/ppermute | solution.py:39
  57.3 6.4 %collective-permute-start.19 = (bf16[192,768]{1,0:T(8,128)(2,1)}, bf16[192,768]{1,0:T(8,128)(2,1)}, u32[]{:S(2)}, u32[]{:S(2)}) collective-permute-start(bf16[192,768]{1,0:T(8,128)(2,1)} %collective-permute-done.11.refs_15_), channel_id=1, source_target_pairs={{0,8},{8,0},{16,24},{24,16},{32,40},{40,32},{48,56},{56,48},{64,72... | collective-permute-start | bytes 884744 | tf_op jit(solution)/shard_map/ppermute | solution.py:39
  57.6 6.2 %copy-start.14 = (bf16[208,768]{1,0:T(8,128)(2,1)}, bf16[208,768]{1,0:T(8,128)(2,1)S(1)}, u32[]{:S(2)}) copy-start(bf16[208,768]{1,0:T(8,128)(2,1)S(1)} %collective-permute-done.6.refs_9_) | copy-start | bytes 958468
  57.6 6.1 %collective-permute-start.17 = (bf16[192,768]{1,0:T(8,128)(2,1)}, bf16[192,768]{1,0:T(8,128)(2,1)}, u32[]{:S(2)}, u32[]{:S(2)}) collective-permute-start(bf16[192,768]{1,0:T(8,128)(2,1)} %collective-permute-done.9.refs_13_), channel_id=1, source_target_pairs={{0,8},{8,0},{16,24},{24,16},{32,40},{40,32},{48,56},{56,48},{64,72... | collective-permute-start | bytes 884744 | tf_op jit(solution)/shard_map/ppermute | solution.py:39
  60.7 3.1 %copy-start.15 = (bf16[208,768]{1,0:T(8,128)(2,1)}, bf16[208,768]{1,0:T(8,128)(2,1)S(1)}, u32[]{:S(2)}) copy-start(bf16[208,768]{1,0:T(8,128)(2,1)S(1)} %collective-permute-done.4.refs_7_) | copy-start | bytes 958468
  103.6 21.1 %collective-permute-start.38 = (bf16[1536,768]{1,0:T(8,128)(2,1)}, bf16[1536,768]{1,0:T(8,128)(2,1)S(1)}, u32[]{:S(2)}, u32[]{:S(2)}) collective-permute-start(bf16[1536,768]{1,0:T(8,128)(2,1)} %get-tuple-element.38), channel_id=1, source_target_pairs={{0,8},{8,0},{16,24},{24,16},{32,40},{40,32},{48,56},{56,48},{64,72... | collective-permute-start | bytes 7077896 | tf_op jit(solution)/shard_map/ppermute | solution.py:39
  103.7 4.7 %collective-permute-start.22 = (f32[8,128]{1,0:T(8,128)}, f32[8,128]{1,0:T(8,128)S(1)}, u32[]{:S(2)}, u32[]{:S(2)}) collective-permute-start(f32[8,128]{1,0:T(8,128)} %get-tuple-element.35), channel_id=1, source_target_pairs={{0,8},{8,0},{16,24},{24,16},{32,40},{40,32},{48,56},{56,48},{64,72... | collective-permute-start | bytes 12296 | tf_op jit(solution)/shard_map/ppermute | solution.py:39
  109.1 3.6 %collective-permute-start.23 = (f32[8,128]{1,0:T(8,128)S(1)}, f32[8,128]{1,0:T(8,128)S(1)}, u32[]{:S(2)}, u32[]{:S(2)}) collective-permute-start(f32[8,128]{1,0:T(8,128)S(1)} %add.87), channel_id=1, source_target_pairs={{0,16},{8,24},{16,0},{24,8},{32,48},{40,56},{48,32},{56,40},{64,80... | collective-permute-start | bytes 12296 | tf_op jit(solution)/shard_map/ppermute | solution.py:39
  112.7 5.5 %collective-permute-start.26 = (f32[8,128]{1,0:T(8,128)S(1)}, f32[8,128]{1,0:T(8,128)S(1)}, u32[]{:S(2)}, u32[]{:S(2)}) collective-permute-start(f32[8,128]{1,0:T(8,128)S(1)} %add.88), channel_id=1, source_target_pairs={{0,96},{8,104},{16,112},{24,120},{32,0},{40,8},{48,16},{56,24},{64... | collective-permute-start | bytes 12296 | tf_op jit(solution)/shard_map/ppermute | solution.py:39
  112.8 8.5 %collective-permute-start.25 = (f32[8,128]{1,0:T(8,128)S(1)}, f32[8,128]{1,0:T(8,128)S(1)}, u32[]{:S(2)}, u32[]{:S(2)}) collective-permute-start(f32[8,128]{1,0:T(8,128)S(1)} %add.88), channel_id=1, source_target_pairs={{0,64},{8,72},{16,80},{24,88},{32,96},{40,104},{48,112},{56,120},{... | collective-permute-start | bytes 12296 | tf_op jit(solution)/shard_map/ppermute | solution.py:39
  114.2 8.1 %collective-permute-start.24 = (f32[8,128]{1,0:T(8,128)S(1)}, f32[8,128]{1,0:T(8,128)S(1)}, u32[]{:S(2)}, u32[]{:S(2)}) collective-permute-start(f32[8,128]{1,0:T(8,128)S(1)} %add.88), channel_id=1, source_target_pairs={{0,32},{8,40},{16,48},{24,56},{32,64},{40,72},{48,80},{56,88},{64,... | collective-permute-start | bytes 12296 | tf_op jit(solution)/shard_map/ppermute | solution.py:39
  118.0 11.9 %collective-permute-start.34 = (bf16[192,768]{1,0:T(8,128)(2,1)S(1)}, bf16[192,768]{1,0:T(8,128)(2,1)S(1)}, u32[]{:S(2)}, u32[]{:S(2)}) collective-permute-start(bf16[192,768]{1,0:T(8,128)(2,1)S(1)} %get-tuple-element.49), channel_id=1, source_target_pairs={{0,1},{1,2},{2,3},{3,0},{4,5},{5,6},{6,7},{7,4},{8,9},{9,10},{10,1... | collective-permute-start | bytes 884744 | tf_op jit(solution)/shard_map/ppermute | solution.py:43
  118.3 14.8 %collective-permute-start.36 = (bf16[192,768]{1,0:T(8,128)(2,1)S(1)}, bf16[192,768]{1,0:T(8,128)(2,1)S(1)}, u32[]{:S(2)}, u32[]{:S(2)}) collective-permute-start(bf16[192,768]{1,0:T(8,128)(2,1)S(1)} %get-tuple-element.50), channel_id=1, source_target_pairs={{0,3},{1,0},{2,1},{3,2},{4,7},{5,4},{6,5},{7,6},{8,11},{9,8},{10,9... | collective-permute-start | bytes 884744 | tf_op jit(solution)/shard_map/ppermute | solution.py:43
  121.2 15.6 %collective-permute-start.35 = (bf16[192,768]{1,0:T(8,128)(2,1)S(1)}, bf16[192,768]{1,0:T(8,128)(2,1)S(1)}, u32[]{:S(2)}, u32[]{:S(2)}) collective-permute-start(bf16[192,768]{1,0:T(8,128)(2,1)S(1)} %get-tuple-element.51), channel_id=1, source_target_pairs={{0,2},{1,3},{2,0},{3,1},{4,6},{5,7},{6,4},{7,5},{8,10},{9,11},{10,... | collective-permute-start | bytes 884744 | tf_op jit(solution)/shard_map/ppermute | solution.py:43
  122.3 6.0 %collective-permute-start.27 = (f32[8,128]{1,0:T(8,128)S(1)}, f32[8,128]{1,0:T(8,128)S(1)}, u32[]{:S(2)}, u32[]{:S(2)}) collective-permute-start(f32[8,128]{1,0:T(8,128)S(1)} %add_add_fusion.1), channel_id=1, source_target_pairs={{0,4},{1,5},{2,6},{3,7},{4,0},{5,1},{6,2},{7,3},{8,12},{9,13},{10,... | collective-permute-start | bytes 12296 | tf_op jit(solution)/shard_map/ppermute | solution.py:43
  124.7 24.7 %copy-start = (f32[1536,768]{1,0:T(8,128)S(1)}, f32[1536,768]{1,0:T(8,128)}, u32[]{:S(2)}) copy-start(f32[1536,768]{1,0:T(8,128)} %get-tuple-element.37) | copy-start | bytes 14155780
  126.5 17.7 %collective-permute-start.42 = (bf16[192,768]{1,0:T(8,128)(2,1)S(1)}, bf16[192,768]{1,0:T(8,128)(2,1)S(1)}, u32[]{:S(2)}, u32[]{:S(2)}) collective-permute-start(bf16[192,768]{1,0:T(8,128)(2,1)S(1)} %get-tuple-element.46), channel_id=1, source_target_pairs={{0,32},{8,40},{16,48},{24,56},{32,64},{40,72},{48,80},{56,88},{64,... | collective-permute-start | bytes 884744 | tf_op jit(solution)/shard_map/ppermute | solution.py:39
  128.3 20.5 %collective-permute-start.44 = (bf16[192,768]{1,0:T(8,128)(2,1)S(1)}, bf16[192,768]{1,0:T(8,128)(2,1)S(1)}, u32[]{:S(2)}, u32[]{:S(2)}) collective-permute-start(bf16[192,768]{1,0:T(8,128)(2,1)S(1)} %get-tuple-element.47), channel_id=1, source_target_pairs={{0,96},{8,104},{16,112},{24,120},{32,0},{40,8},{48,16},{56,24},{64... | collective-permute-start | bytes 884744 | tf_op jit(solution)/shard_map/ppermute | solution.py:39
  129.8 19.6 %collective-permute-start.43 = (bf16[192,768]{1,0:T(8,128)(2,1)S(1)}, bf16[192,768]{1,0:T(8,128)(2,1)S(1)}, u32[]{:S(2)}, u32[]{:S(2)}) collective-permute-start(bf16[192,768]{1,0:T(8,128)(2,1)S(1)} %get-tuple-element.48), channel_id=1, source_target_pairs={{0,64},{8,72},{16,80},{24,88},{32,96},{40,104},{48,112},{56,120},{... | collective-permute-start | bytes 884744 | tf_op jit(solution)/shard_map/ppermute | solution.py:39
  133.1 26.4 %collective-permute-start.33 = (bf16[192,768]{1,0:T(8,128)(2,1)S(1)}, bf16[192,768]{1,0:T(8,128)(2,1)S(1)}, u32[]{:S(2)}, u32[]{:S(2)}) collective-permute-start(bf16[192,768]{1,0:T(8,128)(2,1)S(1)} %get-tuple-element.52), channel_id=1, source_target_pairs={{0,3},{1,0},{2,1},{3,2},{4,7},{5,4},{6,5},{7,6},{8,11},{9,8},{10,9... | collective-permute-start | bytes 884744 | tf_op jit(solution)/shard_map/ppermute | solution.py:43
  136.8 7.5 %collective-permute-start.30 = (f32[8,128]{1,0:T(8,128)S(1)}, f32[8,128]{1,0:T(8,128)S(1)}, u32[]{:S(2)}, u32[]{:S(2)}) collective-permute-start(f32[8,128]{1,0:T(8,128)S(1)} %add.92), channel_id=1, source_target_pairs={{0,3},{1,0},{2,1},{3,2},{4,7},{5,4},{6,5},{7,6},{8,11},{9,8},{10,9... | collective-permute-start | bytes 12296 | tf_op jit(solution)/shard_map/ppermute | solution.py:43
  144.3 15.3 %collective-permute-start.32 = (bf16[192,768]{1,0:T(8,128)(2,1)S(1)}, bf16[192,768]{1,0:T(8,128)(2,1)S(1)}, u32[]{:S(2)}, u32[]{:S(2)}) collective-permute-start(bf16[192,768]{1,0:T(8,128)(2,1)S(1)} %get-tuple-element.53), channel_id=1, source_target_pairs={{0,2},{1,3},{2,0},{3,1},{4,6},{5,7},{6,4},{7,5},{8,10},{9,11},{10,... | collective-permute-start | bytes 884744 | tf_op jit(solution)/shard_map/ppermute | solution.py:43
  144.3 18.5 %collective-permute-start.31 = (bf16[192,768]{1,0:T(8,128)(2,1)S(1)}, bf16[192,768]{1,0:T(8,128)(2,1)S(1)}, u32[]{:S(2)}, u32[]{:S(2)}) collective-permute-start(bf16[192,768]{1,0:T(8,128)(2,1)S(1)} %get-tuple-element.54), channel_id=1, source_target_pairs={{0,1},{1,2},{2,3},{3,0},{4,5},{5,6},{6,7},{7,4},{8,9},{9,10},{10,1... | collective-permute-start | bytes 884744 | tf_op jit(solution)/shard_map/ppermute | solution.py:43
  148.8 6.9 %collective-permute-start.29 = (f32[8,128]{1,0:T(8,128)S(1)}, f32[8,128]{1,0:T(8,128)S(1)}, u32[]{:S(2)}, u32[]{:S(2)}) collective-permute-start(f32[8,128]{1,0:T(8,128)S(1)} %add.92), channel_id=1, source_target_pairs={{0,2},{1,3},{2,0},{3,1},{4,6},{5,7},{6,4},{7,5},{8,10},{9,11},{10,... | collective-permute-start | bytes 12296 | tf_op jit(solution)/shard_map/ppermute | solution.py:43
  149.4 8.9 %collective-permute-start.28 = (f32[8,128]{1,0:T(8,128)S(1)}, f32[8,128]{1,0:T(8,128)S(1)}, u32[]{:S(2)}, u32[]{:S(2)}) collective-permute-start(f32[8,128]{1,0:T(8,128)S(1)} %add.92), channel_id=1, source_target_pairs={{0,1},{1,2},{2,3},{3,0},{4,5},{5,6},{6,7},{7,4},{8,9},{9,10},{10,1... | collective-permute-start | bytes 12296 | tf_op jit(solution)/shard_map/ppermute | solution.py:43
  155.8 9.3 %collective-permute-start.37 = (bf16[192,768]{1,0:T(8,128)(2,1)S(1)}, bf16[192,768]{1,0:T(8,128)(2,1)S(1)}, u32[]{:S(2)}, u32[]{:S(2)}) collective-permute-start(bf16[192,768]{1,0:T(8,128)(2,1)S(1)} %add_convert_fusion.7), channel_id=1, source_target_pairs={{0,4},{1,5},{2,6},{3,7},{4,0},{5,1},{6,2},{7,3},{8,12},{9,13},{10,... | collective-permute-start | bytes 884744 | tf_op jit(solution)/shard_map/ppermute | solution.py:43
  158.3 10.1 %collective-permute-start.45 = (bf16[192,768]{1,0:T(8,128)(2,1)S(1)}, bf16[192,768]{1,0:T(8,128)(2,1)S(1)}, u32[]{:S(2)}, u32[]{:S(2)}) collective-permute-start(bf16[192,768]{1,0:T(8,128)(2,1)S(1)} %get-tuple-element.41), channel_id=1, source_target_pairs={{0,16},{8,24},{16,0},{24,8},{32,48},{40,56},{48,32},{56,40},{64,80... | collective-permute-start | bytes 884744 | tf_op jit(solution)/shard_map/ppermute | solution.py:39
  159.5 5.6 %copy-start.1 = (bf16[192,768]{1,0:T(8,128)(2,1)}, bf16[192,768]{1,0:T(8,128)(2,1)S(1)}, u32[]{:S(2)}) copy-start(bf16[192,768]{1,0:T(8,128)(2,1)S(1)} %collective-permute-done.33.refs_2_) | copy-start | bytes 884740
  159.5 8.9 %collective-permute-start.41 = (bf16[192,768]{1,0:T(8,128)(2,1)S(1)}, bf16[192,768]{1,0:T(8,128)(2,1)S(1)}, u32[]{:S(2)}, u32[]{:S(2)}) collective-permute-start(bf16[192,768]{1,0:T(8,128)(2,1)S(1)} %get-tuple-element.42), channel_id=1, source_target_pairs={{0,96},{8,104},{16,112},{24,120},{32,0},{40,8},{48,16},{56,24},{64... | collective-permute-start | bytes 884744 | tf_op jit(solution)/shard_map/ppermute | solution.py:39
  159.5 5.6 %copy-start.2 = (bf16[192,768]{1,0:T(8,128)(2,1)}, bf16[192,768]{1,0:T(8,128)(2,1)S(1)}, u32[]{:S(2)}) copy-start(bf16[192,768]{1,0:T(8,128)(2,1)S(1)} %collective-permute-done.32.refs_1_) | copy-start | bytes 884740
  159.6 8.9 %collective-permute-start.40 = (bf16[192,768]{1,0:T(8,128)(2,1)S(1)}, bf16[192,768]{1,0:T(8,128)(2,1)S(1)}, u32[]{:S(2)}, u32[]{:S(2)}) collective-permute-start(bf16[192,768]{1,0:T(8,128)(2,1)S(1)} %get-tuple-element.43), channel_id=1, source_target_pairs={{0,64},{8,72},{16,80},{24,88},{32,96},{40,104},{48,112},{56,120},{... | collective-permute-start | bytes 884744 | tf_op jit(solution)/shard_map/ppermute | solution.py:39
  162.8 8.2 %collective-permute-start.39 = (bf16[192,768]{1,0:T(8,128)(2,1)S(1)}, bf16[192,768]{1,0:T(8,128)(2,1)S(1)}, u32[]{:S(2)}, u32[]{:S(2)}) collective-permute-start(bf16[192,768]{1,0:T(8,128)(2,1)S(1)} %get-tuple-element.44), channel_id=1, source_target_pairs={{0,32},{8,40},{16,48},{24,56},{32,64},{40,72},{48,80},{56,88},{64,... | collective-permute-start | bytes 884744 | tf_op jit(solution)/shard_map/ppermute | solution.py:39
  168.4 2.6 %copy-start.5 = (bf16[192,768]{1,0:T(8,128)(2,1)}, bf16[192,768]{1,0:T(8,128)(2,1)S(1)}, u32[]{:S(2)}) copy-start(bf16[192,768]{1,0:T(8,128)(2,1)S(1)} %collective-permute-done.45.refs_3_) | copy-start | bytes 884740
  168.4 2.6 %copy-start.6 = (bf16[192,768]{1,0:T(8,128)(2,1)}, bf16[192,768]{1,0:T(8,128)(2,1)S(1)}, u32[]{:S(2)}) copy-start(bf16[192,768]{1,0:T(8,128)(2,1)S(1)} %collective-permute-done.41.refs_2_) | copy-start | bytes 884740
  (7 other events, 10.2 us)

commit v2 on v0

v2 whole, which is shorter than its diff:
```python
import functools

import jax
import jax.numpy as jnp
from jax import lax
from jax.experimental import pallas as pl
from jax.experimental.pallas import tpu as pltpu
from jax.sharding import PartitionSpec as P

EPS = 1e-06
LOG2E = 1.4426950408889634
N_ROW = 16
N_COL = 8
R = 192
D = 768
RX = R + 16
NX = R * 8
NY = R * 8
BM = 768
NT = (((1,), (1,)), ((), ()))
TN = (((0,), (0,)), ((), ()))
VMEM = pl.BlockSpec(memory_space=pltpu.VMEM)
SMEM = pl.BlockSpec(memory_space=pltpu.SMEM)


def send(value, move):
    pairs = []
    for r in range(N_ROW):
        for c in range(N_COL):
            y, zl, k, zh, x = move(r // 4, (r // 2) % 2, r % 2, c // 4, c % 4)
            pairs.append((r * N_COL + c, (((y % 4) * 2 + zl % 2) * 2 + k % 2) * N_COL + (zh % 2) * 4 + x % 4))
    return lax.ppermute(value, ("row", "col"), pairs)


def send_x(value, d):
    return send(value, lambda y, zl, k, zh, x: (y, zl, k, zh, x + d))


def send_y(value, d):
    return send(value, lambda y, zl, k, zh, x: (y + d, zl, k, zh, x))


def send_core(value):
    return send(value, lambda y, zl, k, zh, x: (y, zl, 1 - k, zh, x))


def swap_image_z(value):
    return send(value, lambda y, zl, k, zh, x: (y, 1 - zl, k, zh, x))


def swap_text_z(value):
    return send(value, lambda y, zl, k, zh, x: (y, 1 - zl, k, 1 - zh, x))


def normalize(ref):
    wide = ref[...].astype(jnp.float32)
    inverse = lax.rsqrt(jnp.sum(wide * wide, axis=-1, keepdims=True) + EPS)
    return wide * inverse, inverse


def call(kernel, outs, *args, name, scalars=0, aliases=None, scratch=(), flops=0, vmem=4):
    return pl.pallas_call(
        kernel,
        in_specs=[SMEM] * scalars + [VMEM] * (len(args) - scalars),
        out_specs=[VMEM] * len(outs),
        out_shape=[jax.ShapeDtypeStruct(shape, dtype) for shape, dtype in outs],
        input_output_aliases=aliases or {},
        scratch_shapes=scratch,
        compiler_params=pltpu.CompilerParams(vmem_limit_bytes=vmem << 20),
        cost_estimate=pl.CostEstimate(flops=flops, bytes_accessed=4 << 20, transcendentals=0),
        name=name,
    )(*args)


def prep_kernel(images_ref, texts_ref, pair_ref, x_ref, y_ref):
    x_ref[:R, :] = normalize(images_ref)[0].astype(jnp.bfloat16)
    y_ref[...] = normalize(texts_ref)[0].astype(jnp.bfloat16)
    pair = pair_ref[...]
    shard = ((pair.astype(jnp.float32) + 0.5) * (1.0 / R)).astype(jnp.int32)
    x_ref[R:, :] = jnp.zeros((16, D), jnp.bfloat16)
    x_ref[R:, :R] = jnp.broadcast_to(shard.astype(jnp.float32), (16, R)).astype(jnp.bfloat16)
    x_ref[R:, 256 : 256 + R] = jnp.broadcast_to((pair - shard * R).astype(jnp.float32), (16, R)).astype(jnp.bfloat16)


def join_kernel(a_ref, b_ref, out_ref):
    rows = a_ref.shape[0]
    out_ref[:rows, :] = a_ref[...]
    out_ref[rows:, :] = b_ref[...]


def join(a, b):
    return call(join_kernel, [((2 * a.shape[0], D), jnp.bfloat16)], a, b, name="join")[0]


def pack_kernel(at_ref, *refs):
    xs, ys = refs[:5], refs[5:10]
    x_all, place, y_all = refs[10:]
    my_y, my_zl, my_k, my_zh, my_x = [at_ref[i] for i in range(5)]
    slot = 0
    for ref in xs:
        for i in range(ref.shape[0] // RX):
            here = slice(slot * R, slot * R + R)
            x_all[here, :] = ref[i * RX : i * RX + R, :]
            codes = ref[i * RX + R : i * RX + RX, :].astype(jnp.float32).astype(jnp.int32)[:1, :]
            shard, offset = codes[:, :R], codes[:, 256 : 256 + R]
            dz = (shard >> 6) ^ my_zh
            dy = (((shard >> 2) & 3) - my_y) & 3
            dk = (shard & 1) ^ my_k
            mine = (((shard >> 4) & 3) == my_x) & (dz == (((shard >> 1) & 1) ^ my_zl))
            step = jnp.where(dy == 2, 6, jnp.where(dy == 3, 4, dy * 2))
            place[:, here] = jnp.where(mine, (dk * 8 + step + dz) * R + offset, -1)
            slot += 1
    slot = 0
    for ref in ys:
        y_all[slot * R : slot * R + ref.shape[0], :] = ref[...]
        slot += ref.shape[0] // R


def score_kernel(first, sc_ref, x_all, y_all, place, loss_in, gy_out, weights, loss_ref, loss_acc):
    slope, shift, scale = sc_ref[0], sc_ref[1], sc_ref[2]
    loss_acc[...] = jnp.zeros_like(loss_acc)

    def step(i, carry):
        base = pl.multiple_of(i * BM, BM)
        here = pl.ds(base, BM)
        x = x_all[...]
        score = lax.dot_general(y_all[here, :], x, NT, preferred_element_type=jnp.float32)
        rows = first + base + lax.broadcasted_iota(jnp.int32, (BM, NX), 0)
        paired = place[...] == rows
        z = score * slope + shift
        z = jnp.where(paired, -z, z)
        t = jnp.exp2(z)
        total = 1.0 + t
        weight = (jnp.where(paired, -scale, scale) * (t / total)).astype(jnp.bfloat16)
        small = t * (1.0 - t * (0.5 - t * (1.0 / 3.0)))
        loss = jnp.where(t < 2.0**-6, small, jnp.log(total))
        loss_acc[...] += jnp.sum(loss.reshape(BM // 8, 8, NX), axis=0)
        weights[here, :] = weight
        gy_out[here, :] = jnp.dot(weight, x, preferred_element_type=jnp.float32).astype(gy_out.dtype)
        return carry

    lax.fori_loop(0, NY // BM, step, 0)
    loss = loss_in[...] + jnp.sum(loss_acc[...])
    loss_ref[...] = loss
    if gy_out.shape[0] > NY:
        gy_out[NY:, :] = jnp.zeros((16, D), gy_out.dtype)
        for i in range(3):
            part = loss.astype(jnp.bfloat16)
            gy_out[NY:, i * 128 : i * 128 + 128] = jnp.concatenate([part, part], axis=0)
            loss = loss - part.astype(jnp.float32)


def image_kernel(slots, w_own, w_sib, y_own, y_sib, *outs):
    outs = list(outs)
    for slot in slots:
        here = slice(slot * R, slot * R + 2 * R)
        grad = lax.dot_general(w_own[:, here], y_own[...], TN, preferred_element_type=jnp.float32)
        grad += lax.dot_general(w_sib[:, here], y_sib[...], TN, preferred_element_type=jnp.float32)
        at = 0
        while at < 2 * R:
            ref = outs.pop(0)
            ref[...] = grad[at : at + ref.shape[0], :].astype(ref.dtype)
            at += ref.shape[0]


def add_kernel(direct, sibling, loss, own, zed, plus, minus, two, two_z, loss_out):
    slot = 0
    for ref in (own, zed, plus, minus, two, two_z):
        here = slice(slot, slot + ref.shape[0])
        ref[...] = (direct[here, :] + sibling[here, :].astype(jnp.float32)).astype(ref.dtype)
        slot += ref.shape[0]
    total = loss[...]
    for i in range(3):
        total = total + sibling[NY : NY + 8, i * 128 : i * 128 + 128].astype(jnp.float32)
    loss_out[...] = total


F32, BF16 = jnp.float32, jnp.bfloat16
LOSS = ((8, 128), F32)
NEAR = [((R, D), F32), ((R, D), F32), ((2 * R, D), F32), ((2 * R, D), F32)]
AWAY = [((R, D), BF16), ((R, D), BF16)]


def turn_kernel(plus, minus, two, two_z, plus_out, minus_out):
    plus_out[:R, :] = (plus[:R, :] + two[...].astype(F32)).astype(BF16)
    plus_out[R:, :] = plus[R:, :].astype(BF16)
    minus_out[:R, :] = minus[:R, :].astype(BF16)
    minus_out[R:, :] = (minus[R:, :] + two_z[...].astype(F32)).astype(BF16)


def turn_loss_kernel(plus, minus, two, two_z, loss, plus_out, minus_out, loss_out):
    turn_kernel(plus, minus, two, two_z, plus_out, minus_out)
    loss_out[...] = loss[...]


def far_kernel(own, plus, minus, out):
    out[...] = (own[...] + plus[R:, :].astype(F32) + minus[R:, :].astype(F32)).astype(BF16)


def far_loss_kernel(own, plus, minus, loss, step, out, loss_out):
    far_kernel(own, plus, minus, out)
    loss_out[...] = loss[...] + step[...]


def final_kernel(values_ref, own_ref, plus, minus, zed, out_ref):
    unit, inverse = normalize(values_ref)
    grad = own_ref[...] + plus[:R, :].astype(F32) + minus[:R, :].astype(F32) + zed[...].astype(F32)
    along = jnp.sum(grad * unit, axis=-1, keepdims=True)
    out_ref[...] = (grad - unit * along) * inverse


def final_loss_kernel(values_ref, own_ref, plus, minus, zed, loss, step, out_ref, loss_out):
    final_kernel(values_ref, own_ref, plus, minus, zed, out_ref)
    loss_out[...] = (loss[...] + step[...]) * (1.0 / (R * N_ROW * N_COL))


def gather(own, swap, shift):
    zed = swap(own)
    two = shift(own, 2)
    both = join(own, zed)
    return [both, shift(both, -1), shift(both, 1), two, shift(zed, 2)]


def turn(near, away, shift, *loss):
    two, two_z = shift(away[0], 1), shift(away[1], -1)
    outs = [((2 * R, D), BF16)] * 2
    if loss:
        return call(turn_loss_kernel, outs + [LOSS], near[2], near[3], two, two_z, *loss, name="turn", vmem=8)
    return call(turn_kernel, outs, near[2], near[3], two, two_z, name="turn", vmem=8)


def far(near, plus, minus, swap, *loss):
    out = ((R, D), BF16)
    if loss:
        value, total = call(far_loss_kernel, [out, LOSS], near[1], plus, minus, *loss, name="far")
        return swap(value), total
    return swap(call(far_kernel, [out], near[1], plus, minus, name="far")[0])


def local(images, texts, pair_index, log_scale, bias):
    row, col = lax.axis_index("row"), lax.axis_index("col")
    x_low, y_low = call(
        prep_kernel,
        [((RX, D), jnp.bfloat16), ((R, D), jnp.bfloat16)],
        images, texts, pair_index.reshape(1, R),
        name="prep",
    )
    xs = gather(x_low, swap_image_z, send_x)
    ys = gather(y_low, swap_text_z, send_y)

    scale = jnp.exp(log_scale[0])
    scalars = jnp.stack([scale * LOG2E, bias[0] * LOG2E, scale])
    at = jnp.stack([row // 4, (row // 2) % 2, row % 2, col // 4, col % 4]).astype(jnp.int32)
    x_all, place, y_own = call(
        pack_kernel,
        [((NX, D), jnp.bfloat16), ((1, NX), jnp.int32), ((NY, D), jnp.bfloat16)],
        at, *xs, *ys,
        name="pack", scalars=1, vmem=12,
    )
    y_sib = send_core(y_own)
    flops = 4 * NX * NY * D

    def score(first, y_all, loss, out, name):
        return call(
            functools.partial(score_kernel, first),
            [out, ((NY, NX), BF16), LOSS],
            scalars, x_all, y_all, place, loss,
            name=name, scalars=1, flops=flops, vmem=30,
            scratch=[pltpu.VMEM((8, NX), F32)],
        )

    gy_own, w_own, loss = score(0, y_own, jnp.zeros((8, 128), F32), ((NY, D), F32), "score_own")
    gy_sib, w_sib, loss = score(NY, y_sib, loss, ((NY + 16, D), BF16), "score_sib")
    gy_core = send_core(gy_sib)
    weights = (w_own, w_sib, y_own, y_sib)
    gx_away = call(functools.partial(image_kernel, (6,)), AWAY, *weights, name="image_away", flops=flops // 8, vmem=16)
    *gy, loss = call(add_kernel, NEAR + AWAY + [LOSS], gy_own, gy_core, loss, name="add", vmem=16)
    gy_near, gy_away = gy[:4], gy[4:]

    gx_near = call(
        functools.partial(image_kernel, (0, 2, 4)), NEAR, *weights, name="image_near", flops=3 * flops // 8, vmem=16
    )
    gx_plus, gx_minus = turn(gx_near, gx_away, send_x)
    gy_plus, gy_minus, loss = turn(gy_near, gy_away, send_y, loss)
    gx_plus, gx_minus = send_x(gx_plus, 1), send_x(gx_minus, -1)
    gy_plus, gy_minus = send_y(gy_plus, 1), send_y(gy_minus, -1)

    loss = loss + swap_image_z(loss)
    loss = loss + swap_text_z(loss)
    step = send(loss, lambda y, zl, k, zh, x: (y, zl, k, zh, x ^ 1))
    gx_far, loss = far(gx_near, gx_plus, gx_minus, swap_image_z, loss, step)
    gy_far = far(gy_near, gy_plus, gy_minus, swap_text_z)
    loss = loss + send(loss, lambda y, zl, k, zh, x: (y, zl, k, zh, x ^ 2))
    loss = loss + send(loss, lambda y, zl, k, zh, x: (y ^ 1, zl, k, zh, x))
    step = send(loss, lambda y, zl, k, zh, x: (y ^ 2, zl, k, zh, x))

    grad = ((R, D), F32)
    grad_x = call(final_kernel, [grad], images, gx_near[0], gx_plus, gx_minus, gx_far, name="unproject")[0]
    grad_y, loss = call(
        final_loss_kernel, [grad, LOSS], texts, gy_near[0], gy_plus, gy_minus, gy_far, loss, step, name="unproject"
    )
    return loss[0, :1], grad_x, grad_y


def solution(mesh):
    return jax.shard_map(
        local,
        mesh=mesh,
        in_specs=(P(("row", "col"), None), P(("col", "row"), None), P(("row", "col")), P(), P()),
        out_specs=(P(), P(("row", "col"), None), P(("col", "row"), None)),
        check_vma=False,
    )
```

time: 428 us -> 123 us (0.29)
  waiting for transfers between devices: 195 us -> 32.3 us
  matrix products: 95 us -> 0 us
  blocking collectives: 87.4 us -> 0 us
  starting transfers between devices: 0.16 us -> 43.9 us
  Pallas kernels: 0 us -> 37.6 us
  between operations: 17 us -> 2.17 us
  other arithmetic: 12.6 us -> 0.09 us
  local copies, waits for them, and re-layouts: 14.2 us -> 6.55 us
    reduce_scatter x2 -> x0, waiting for transfers between devices: 117 us -> none  [the longest x1 102 us: local(): gy_unit = lax.psum_scatter(gy_part, 'row', scatter_dimension=0, tiled=True)]
    dot_general x9 -> x0, matrix products: 95 us -> none  [the longest x3 38.3 us: tile_weight(): lax.dot_general(x_block, y_part, (((1,), (1,)), ((), ())), preferred_elem...]
    all_gather x2 -> x0, waiting for transfers between devices: 77.1 us -> none  [the longest x1 39.4 us: local(): lax.all_gather(y_unit.astype(jnp.bfloat16), 'row', axis=0, tiled=True)]
    psum x1 -> x0, blocking collectives: 72.7 us -> none  [local(): loss_sum = lax.psum(total, ('row', 'col'))]
    ppermute x0 -> x28, starting transfers between devices: none -> 43.9 us  [send(): return lax.ppermute(value, ('row', 'col'), pairs)]
    pallas_call x0 -> x15, Pallas kernels: none -> 37.6 us  [call(): pl.pallas_call(kernel, in_specs=[SMEM] * scalars + [VMEM] * (len(args) -...]
    ppermute x0 -> x28, waiting for transfers between devices: none -> 32.3 us  [send(): return lax.ppermute(value, ('row', 'col'), pairs)]
    unnamed x1 -> x0, blocking collectives: 14.7 us -> none
  transfers between devices with their start and end apart: 4 -> 28, of which waited for: 4 -> 10; matrix products, arithmetic and copies ran while one was open for 2% -> 0% of each run, Pallas kernels for 0% -> 19%
where the time goes in v2:
time: 123 us
  starting transfers between devices  43.9 us (36%)
  Pallas kernels  37.6 us (31%)
  waiting for transfers between devices  32.3 us (26%)
  local copies, waits for them, and re-layouts  6.55 us (5%)
  between operations  2.17 us (2%)
    ppermute x28, starting transfers between devices, send(): return lax.ppermute(value, ('row', 'col'), pairs)  43.9 us
    pallas_call x15, Pallas kernels, call(): pl.pallas_call(kernel, in_specs=[SMEM] * scalars + [VMEM] * (len(args) -...  37.6 us
    ppermute x28, waiting for transfers between devices, send(): return lax.ppermute(value, ('row', 'col'), pairs)  32.3 us
    unnamed x18, local copies, waits for them, and re-layouts  5.95 us
  transfers between devices with their start and end apart: 28, of which 10 were waited for; matrix products, arithmetic and copies ran while one was open for 0% of the time, Pallas kernels for 19%

profile of v2, /device:TPU:0, one launch (start us, length us, event | category | flops | bytes accessed | tf_op | source)
XLA Modules:
  0.0 122.6 jit_solution(7846707632391397654)
XLA Ops:
  0.6 0.0 copy-start
  0.6 1.0 copy-done
  1.6 1.0 copy-done.2
  2.6 0.7 copy-done.8
  3.2 0.2 prep.1
  3.4 2.1 %collective-permute-start = (bf16[208,768]{1,0:T(8,128)(2,1)S(1)}, bf16[208,768]{1,0:T(8,128)(2,1)}, u32[]{:S(2)}, u32[]{:S(2)}) collective-permute-start(bf16[208,768]{1,0:T(8,128)(2,1)S(1)} %get-tuple-element.36.a_ref), channel_id=1, source_target_pairs={{0,16},{1,17},{2,18},{3,19},{4,20},{5,21},{6,22},{7,23},{8,24},{9,... | collective-permute-start | bytes 958472 | tf_op jit(solution)/shard_map/ppermute | solution.py:32
  5.5 2.5 %collective-permute-start.5 = (bf16[192,768]{1,0:T(8,128)(2,1)S(1)}, bf16[192,768]{1,0:T(8,128)(2,1)S(1)}, u32[]{:S(2)}, u32[]{:S(2)}) collective-permute-start(bf16[192,768]{1,0:T(8,128)(2,1)S(1)} %get-tuple-element.37.a_ref), channel_id=1, source_target_pairs={{0,20},{1,21},{2,22},{3,23},{4,16},{5,17},{6,18},{7,19},{8,28},{9,... | collective-permute-start | bytes 884744 | tf_op jit(solution)/shard_map/ppermute | solution.py:32
  8.0 3.0 %collective-permute-start.3 = (bf16[208,768]{1,0:T(8,128)(2,1)S(1)}, bf16[208,768]{1,0:T(8,128)(2,1)S(1)}, u32[]{:S(2)}, u32[]{:S(2)}) collective-permute-start(bf16[208,768]{1,0:T(8,128)(2,1)S(1)} %get-tuple-element.36.a_ref), channel_id=1, source_target_pairs={{0,2},{1,3},{2,0},{3,1},{4,6},{5,7},{6,4},{7,5},{8,10},{9,11},{10,... | collective-permute-start | bytes 958472 | tf_op jit(solution)/shard_map/ppermute | solution.py:32
  11.1 3.2 %collective-permute-start.8 = (bf16[192,768]{1,0:T(8,128)(2,1)S(1)}, bf16[192,768]{1,0:T(8,128)(2,1)S(1)}, u32[]{:S(2)}, u32[]{:S(2)}) collective-permute-start(bf16[192,768]{1,0:T(8,128)(2,1)S(1)} %get-tuple-element.37.a_ref), channel_id=1, source_target_pairs={{0,64},{1,65},{2,66},{3,67},{4,68},{5,69},{6,70},{7,71},{8,72},{9,... | collective-permute-start | bytes 884744 | tf_op jit(solution)/shard_map/ppermute | solution.py:32
  14.3 1.0 join.2.refs_0_
  15.3 0.7 collective-permute-start.2
  15.9 2.6 %collective-permute-start.1 = (bf16[416,768]{1,0:T(8,128)(2,1)S(1)}, bf16[416,768]{1,0:T(8,128)(2,1)S(1)}, u32[]{:S(2)}, u32[]{:S(2)}) collective-permute-start(bf16[416,768]{1,0:T(8,128)(2,1)S(1)} %join.2.refs_0_), channel_id=1, source_target_pairs={{0,3},{1,0},{2,1},{3,2},{4,7},{5,4},{6,5},{7,6},{8,11},{9,8},{10,9... | collective-permute-start | bytes 1916936 | tf_op jit(solution)/shard_map/ppermute | solution.py:32
  18.6 2.1 %collective-permute-start.9 = (bf16[192,768]{1,0:T(8,128)(2,1)S(1)}, bf16[192,768]{1,0:T(8,128)(2,1)S(1)}, u32[]{:S(2)}, u32[]{:S(2)}) collective-permute-start(bf16[192,768]{1,0:T(8,128)(2,1)S(1)} %collective-permute-done.5.b_ref), channel_id=1, source_target_pairs={{0,64},{1,65},{2,66},{3,67},{4,68},{5,69},{6,70},{7,71},{8,72},{9,... | collective-permute-start | bytes 884744 | tf_op jit(solution)/shard_map/ppermute | solution.py:32
  20.7 0.0 copy-start.4
  20.7 0.7 copy-done.4
  21.4 1.5 %collective-permute-start.7 = (bf16[384,768]{1,0:T(8,128)(2,1)S(1)}, bf16[384,768]{1,0:T(8,128)(2,1)S(1)}, u32[]{:S(2)}, u32[]{:S(2)}) collective-permute-start(bf16[384,768]{1,0:T(8,128)(2,1)S(1)} %join.3.refs_5_), channel_id=1, source_target_pairs={{0,32},{1,33},{2,34},{3,35},{4,36},{5,37},{6,38},{7,39},{8,40},{9,... | collective-permute-start | bytes 1769480 | tf_op jit(solution)/shard_map/ppermute | solution.py:32
  23.0 1.7 %collective-permute-start.6 = (bf16[384,768]{1,0:T(8,128)(2,1)S(1)}, bf16[384,768]{1,0:T(8,128)(2,1)}, u32[]{:S(2)}, u32[]{:S(2)}) collective-permute-start(bf16[384,768]{1,0:T(8,128)(2,1)S(1)} %join.3.refs_5_), channel_id=1, source_target_pairs={{0,96},{1,97},{2,98},{3,99},{4,100},{5,101},{6,102},{7,103},{8,104... | collective-permute-start | bytes 1769480 | tf_op jit(solution)/shard_map/ppermute | solution.py:32
  24.7 5.3 %collective-permute-done.9.refs_9_ = bf16[192,768]{1,0:T(8,128)(2,1)S(1)} collective-permute-done((bf16[192,768]{1,0:T(8,128)(2,1)S(1)}, bf16[192,768]{1,0:T(8,128)(2,1)S(1)}, u32[]{:S(2)}, u32[]{:S(2)}) %collective-permute-start.9) | collective-permute-done | bytes 294944 | tf_op jit(solution)/shard_map/ppermute | solution.py:32
  30.0 0.7 copy-done.6
  30.7 0.7 collective-permute-start.4
  31.5 0.1 stack.30.at_ref
  31.5 8.0 %collective-permute-done.4.refs_4_ = bf16[208,768]{1,0:T(8,128)(2,1)} collective-permute-done((bf16[208,768]{1,0:T(8,128)(2,1)}, bf16[208,768]{1,0:T(8,128)(2,1)}, u32[]{:S(2)}, u32[]{:S(2)}) %collective-permute-start.4) | collective-permute-done | bytes 319520 | tf_op jit(solution)/shard_map/ppermute | solution.py:32
  39.5 0.3 collective-permute-done.7.refs_7_
  39.8 0.1 collective-permute-done.6.refs_6_
  39.9 1.0 copy-done.5
  40.9 1.0 copy-done.7
  41.8 1.5 %pack.1 = (bf16[1536,768]{1,0:T(8,128)(2,1)S(1)}, s32[1,1536]{1,0:T(1,128)S(1)}, bf16[1536,768]{1,0:T(8,128)(2,1)S(1)}) custom-call(s32[5]{0:T(128)S(1)} %stack.30.at_ref, bf16[416,768]{1,0:T(8,128)(2,1)S(1)} %join.2.refs_0_, bf16[416,768]{1,0:T(8,128)(2,1)S(1)} %collective-permute-done.1.refs_1_, bf16[416,768]{1,0:T(8,128)(2,1)S(1)} %collective-permute-done.2.refs_2_, ...), custom_call_target="tpu_custom_call" | custom-call | bytes 4194304 | tf_op jit(solution)/shard_map/pack/pallas_call | solution.py:62
  43.3 0.3 collective-permute-start.10
  45.0 0.1 pad_maximum_fusion.sc_ref
  45.0 11.8 %score_own.1 = (f32[1536,768]{1,0:T(8,128)S(1)}, bf16[1536,1536]{1,0:T(8,128)(2,1)S(1)}, f32[8,128]{1,0:T(8,128)S(1)}) custom-call(f32[3]{0:T(128)S(1)} %pad_maximum_fusion.sc_ref, bf16[1536,768]{1,0:T(8,128)(2,1)S(1)} %get-tuple-element.38.x_all, bf16[1536,768]{1,0:T(8,128)(2,1)S(1)} %get-tuple-element.39.y_all.y_own, ...), custom_call_target="tpu_custom_call" | custom-call | flops 7247757312 | bytes 4194304 | tf_op jit(solution)/shard_map/score_own/pallas_call | solution.py:62
  56.8 11.9 %score_sib.1 = (bf16[1552,768]{1,0:T(8,128)(2,1)S(1)}, bf16[1536,1536]{1,0:T(8,128)(2,1)S(1)}, f32[8,128]{1,0:T(8,128)S(1)}) custom-call(f32[3]{0:T(128)S(1)} %pad_maximum_fusion.sc_ref, bf16[1536,768]{1,0:T(8,128)(2,1)S(1)} %get-tuple-element.38.x_all, bf16[1536,768]{1,0:T(8,128)(2,1)S(1)} %collective-permute-done.10.y_all.y_sib, ...), custom_call_target="tpu_custom_call" | custom-call | flops 7247757312 | bytes 4194304 | tf_op jit(solution)/shard_map/score_sib/pallas_call | solution.py:62
  68.7 0.6 collective-permute-start.11
  69.3 2.0 %image_away.1 = (bf16[192,768]{1,0:T(8,128)(2,1)S(1)}, bf16[192,768]{1,0:T(8,128)(2,1)S(1)}) custom-call(bf16[1536,1536]{1,0:T(8,128)(2,1)S(1)} %get-tuple-element.54.w_own, bf16[1536,1536]{1,0:T(8,128)(2,1)S(1)} %get-tuple-element.55.w_sib, bf16[1536,768]{1,0:T(8,128)(2,1)S(1)} %get-tuple-element.39.y_all.y_own, ...), custom_call_target="tpu_custom_call" | custom-call | flops 905969664 | bytes 4194304 | tf_op jit(solution)/shard_map/image_away/pallas_call | solution.py:62
  71.3 0.7 collective-permute-start.17
  72.0 2.6 %collective-permute-start.18 = (bf16[192,768]{1,0:T(8,128)(2,1)S(1)}, bf16[192,768]{1,0:T(8,128)(2,1)S(1)}, u32[]{:S(2)}, u32[]{:S(2)}) collective-permute-start(bf16[192,768]{1,0:T(8,128)(2,1)S(1)} %get-tuple-element.60), channel_id=1, source_target_pairs={{0,3},{1,0},{2,1},{3,2},{4,7},{5,4},{6,5},{7,6},{8,11},{9,8},{10,9... | collective-permute-start | bytes 884744 | tf_op jit(solution)/shard_map/ppermute | solution.py:32
  74.6 0.5 add.33
  75.2 1.4 %collective-permute-start.12 = (bf16[192,768]{1,0:T(8,128)(2,1)S(1)}, bf16[192,768]{1,0:T(8,128)(2,1)S(1)}, u32[]{:S(2)}, u32[]{:S(2)}) collective-permute-start(bf16[192,768]{1,0:T(8,128)(2,1)S(1)} %get-tuple-element.48), channel_id=1, source_target_pairs={{0,32},{1,33},{2,34},{3,35},{4,36},{5,37},{6,38},{7,39},{8,40},{9,... | collective-permute-start | bytes 884744 | tf_op jit(solution)/shard_map/ppermute | solution.py:32
  76.5 1.9 %collective-permute-start.13 = (bf16[192,768]{1,0:T(8,128)(2,1)S(1)}, bf16[192,768]{1,0:T(8,128)(2,1)S(1)}, u32[]{:S(2)}, u32[]{:S(2)}) collective-permute-start(bf16[192,768]{1,0:T(8,128)(2,1)S(1)} %get-tuple-element.49), channel_id=1, source_target_pairs={{0,96},{1,97},{2,98},{3,99},{4,100},{5,101},{6,102},{7,103},{8,104... | collective-permute-start | bytes 884744 | tf_op jit(solution)/shard_map/ppermute | solution.py:32
  78.5 5.8 %image_near.1 = (f32[192,768]{1,0:T(8,128)S(1)}, f32[192,768]{1,0:T(8,128)S(1)}, f32[384,768]{1,0:T(8,128)S(1)}, f32[384,768]{1,0:T(8,128)S(1)}) custom-call(bf16[1536,1536]{1,0:T(8,128)(2,1)S(1)} %get-tuple-element.54.w_own, bf16[1536,1536]{1,0:T(8,128)(2,1)S(1)} %get-tuple-element.55.w_sib, bf16[1536,768]{1,0:T(8,128)(2,1)S(1)} %get-tuple-element.39.y_all.y_own, ...), custom_call_target="tpu_custom_call" | custom-call | flops 2717908992 | bytes 4194304 | tf_op jit(solution)/shard_map/image_near/pallas_call | solution.py:62
  84.2 0.2 turn.3
  84.4 0.1 collective-permute-start.19
  84.5 3.2 %collective-permute-start.20 = (bf16[384,768]{1,0:T(8,128)(2,1)S(1)}, bf16[384,768]{1,0:T(8,128)(2,1)S(1)}, u32[]{:S(2)}, u32[]{:S(2)}) collective-permute-start(bf16[384,768]{1,0:T(8,128)(2,1)S(1)} %get-tuple-element.62), channel_id=1, source_target_pairs={{0,3},{1,0},{2,1},{3,2},{4,7},{5,4},{6,5},{7,6},{8,11},{9,8},{10,9... | collective-permute-start | bytes 1769480 | tf_op jit(solution)/shard_map/ppermute | solution.py:32
  87.8 0.2 turn.2
  87.9 0.0 copy-start.1
  87.9 0.1 collective-permute-start.14
  88.1 3.2 %collective-permute-start.15 = (bf16[384,768]{1,0:T(8,128)(2,1)S(1)}, bf16[384,768]{1,0:T(8,128)(2,1)S(1)}, u32[]{:S(2)}, u32[]{:S(2)}) collective-permute-start(bf16[384,768]{1,0:T(8,128)(2,1)S(1)} %get-tuple-element.52), channel_id=1, source_target_pairs={{0,96},{1,97},{2,98},{3,99},{4,100},{5,101},{6,102},{7,103},{8,104... | collective-permute-start | bytes 1769480 | tf_op jit(solution)/shard_map/ppermute | solution.py:32
  91.2 1.2 %collective-permute-start.21 = (f32[8,128]{1,0:T(8,128)S(1)}, f32[8,128]{1,0:T(8,128)S(1)}, u32[]{:S(2)}, u32[]{:S(2)}) collective-permute-start(f32[8,128]{1,0:T(8,128)S(1)} %get-tuple-element.63), channel_id=1, source_target_pairs={{0,16},{1,17},{2,18},{3,19},{4,20},{5,21},{6,22},{7,23},{8,24},{9,... | collective-permute-start | bytes 12296 | tf_op jit(solution)/shard_map/ppermute | solution.py:32
  92.5 2.4 %collective-permute-done.21 = f32[8,128]{1,0:T(8,128)S(1)} collective-permute-done((f32[8,128]{1,0:T(8,128)S(1)}, f32[8,128]{1,0:T(8,128)S(1)}, u32[]{:S(2)}, u32[]{:S(2)}) %collective-permute-start.21) | collective-permute-done | bytes 4128 | tf_op jit(solution)/shard_map/ppermute | solution.py:32
  94.9 3.4 %collective-permute-start.22 = (f32[8,128]{1,0:T(8,128)S(1)}, f32[8,128]{1,0:T(8,128)S(1)}, u32[]{:S(2)}, u32[]{:S(2)}) collective-permute-start(f32[8,128]{1,0:T(8,128)S(1)} %add.29), channel_id=1, source_target_pairs={{0,20},{1,21},{2,22},{3,23},{4,16},{5,17},{6,18},{7,19},{8,28},{9,... | collective-permute-start | bytes 12296 | tf_op jit(solution)/shard_map/ppermute | solution.py:32
  98.2 1.6 %collective-permute-done.22 = f32[8,128]{1,0:T(8,128)S(1)} collective-permute-done((f32[8,128]{1,0:T(8,128)S(1)}, f32[8,128]{1,0:T(8,128)S(1)}, u32[]{:S(2)}, u32[]{:S(2)}) %collective-permute-start.22) | collective-permute-done | bytes 4128 | tf_op jit(solution)/shard_map/ppermute | solution.py:32
  99.8 0.0 collective-permute-done.19.plus
  99.8 3.6 %collective-permute-done.23.step = f32[8,128]{1,0:T(8,128)S(1)} collective-permute-done((f32[8,128]{1,0:T(8,128)S(1)}, f32[8,128]{1,0:T(8,128)S(1)}, u32[]{:S(2)}, u32[]{:S(2)}) %collective-permute-start.23) | collective-permute-done | bytes 4128 | tf_op jit(solution)/shard_map/ppermute | solution.py:32
  103.4 0.1 far.3
  103.5 0.1 collective-permute-start.27
  103.6 0.0 copy-start.3
  103.7 0.1 far.2
  103.8 3.3 %collective-permute-start.16 = (bf16[192,768]{1,0:T(8,128)(2,1)S(1)}, bf16[192,768]{1,0:T(8,128)(2,1)S(1)}, u32[]{:S(2)}, u32[]{:S(2)}) collective-permute-start(bf16[192,768]{1,0:T(8,128)(2,1)S(1)} %far.2), channel_id=1, source_target_pairs={{0,20},{1,21},{2,22},{3,23},{4,16},{5,17},{6,18},{7,19},{8,28},{9,... | collective-permute-start | bytes 884744 | tf_op jit(solution)/shard_map/ppermute | solution.py:32
  107.1 5.1 %collective-permute-done.24 = f32[8,128]{1,0:T(8,128)S(1)} collective-permute-done((f32[8,128]{1,0:T(8,128)S(1)}, f32[8,128]{1,0:T(8,128)S(1)}, u32[]{:S(2)}, u32[]{:S(2)}) %collective-permute-start.24) | collective-permute-done | bytes 4128 | tf_op jit(solution)/shard_map/ppermute | solution.py:32
  112.2 3.6 %collective-permute-done.25 = f32[8,128]{1,0:T(8,128)S(1)} collective-permute-done((f32[8,128]{1,0:T(8,128)S(1)}, f32[8,128]{1,0:T(8,128)S(1)}, u32[]{:S(2)}, u32[]{:S(2)}) %collective-permute-start.25) | collective-permute-done | bytes 4128 | tf_op jit(solution)/shard_map/ppermute | solution.py:32
  115.8 1.7 %collective-permute-start.26 = (f32[8,128]{1,0:T(8,128)S(1)}, f32[8,128]{1,0:T(8,128)S(1)}, u32[]{:S(2)}, u32[]{:S(2)}) collective-permute-start(f32[8,128]{1,0:T(8,128)S(1)} %add.32.loss), channel_id=1, source_target_pairs={{0,64},{1,65},{2,66},{3,67},{4,68},{5,69},{6,70},{7,71},{8,72},{9,... | collective-permute-start | bytes 12296 | tf_op jit(solution)/shard_map/ppermute | solution.py:32
  117.5 1.2 unproject.3
  118.6 2.3 %collective-permute-done.26.step = f32[8,128]{1,0:T(8,128)S(1)} collective-permute-done((f32[8,128]{1,0:T(8,128)S(1)}, f32[8,128]{1,0:T(8,128)S(1)}, u32[]{:S(2)}, u32[]{:S(2)}) %collective-permute-start.26) | collective-permute-done | bytes 4128 | tf_op jit(solution)/shard_map/ppermute | solution.py:32
  120.9 1.2 unproject.2
  122.1 0.5 slice.3
  (33 shorter events, 0.1 us)
Async XLA Ops:
  0.6 1.0 copy-start
  1.6 1.0 copy-start.2
  2.6 0.7 copy-start.8
  3.4 10.8 %collective-permute-start = (bf16[208,768]{1,0:T(8,128)(2,1)S(1)}, bf16[208,768]{1,0:T(8,128)(2,1)}, u32[]{:S(2)}, u32[]{:S(2)}) collective-permute-start(bf16[208,768]{1,0:T(8,128)(2,1)S(1)} %get-tuple-element.36.a_ref), channel_id=1, source_target_pairs={{0,16},{1,17},{2,18},{3,19},{4,20},{5,21},{6,22},{7,23},{8,24},{9,... | collective-permute-start | bytes 958472 | tf_op jit(solution)/shard_map/ppermute | solution.py:32
  5.5 13.1 %collective-permute-start.5 = (bf16[192,768]{1,0:T(8,128)(2,1)S(1)}, bf16[192,768]{1,0:T(8,128)(2,1)S(1)}, u32[]{:S(2)}, u32[]{:S(2)}) collective-permute-start(bf16[192,768]{1,0:T(8,128)(2,1)S(1)} %get-tuple-element.37.a_ref), channel_id=1, source_target_pairs={{0,20},{1,21},{2,22},{3,23},{4,16},{5,17},{6,18},{7,19},{8,28},{9,... | collective-permute-start | bytes 884744 | tf_op jit(solution)/shard_map/ppermute | solution.py:32
  8.0 14.9 %collective-permute-start.3 = (bf16[208,768]{1,0:T(8,128)(2,1)S(1)}, bf16[208,768]{1,0:T(8,128)(2,1)S(1)}, u32[]{:S(2)}, u32[]{:S(2)}) collective-permute-start(bf16[208,768]{1,0:T(8,128)(2,1)S(1)} %get-tuple-element.36.a_ref), channel_id=1, source_target_pairs={{0,2},{1,3},{2,0},{3,1},{4,6},{5,7},{6,4},{7,5},{8,10},{9,11},{10,... | collective-permute-start | bytes 958472 | tf_op jit(solution)/shard_map/ppermute | solution.py:32
  11.1 9.7 %collective-permute-start.8 = (bf16[192,768]{1,0:T(8,128)(2,1)S(1)}, bf16[192,768]{1,0:T(8,128)(2,1)S(1)}, u32[]{:S(2)}, u32[]{:S(2)}) collective-permute-start(bf16[192,768]{1,0:T(8,128)(2,1)S(1)} %get-tuple-element.37.a_ref), channel_id=1, source_target_pairs={{0,64},{1,65},{2,66},{3,67},{4,68},{5,69},{6,70},{7,71},{8,72},{9,... | collective-permute-start | bytes 884744 | tf_op jit(solution)/shard_map/ppermute | solution.py:32
  15.3 24.6 %collective-permute-start.2 = (bf16[416,768]{1,0:T(8,128)(2,1)S(1)}, bf16[416,768]{1,0:T(8,128)(2,1)S(1)}, u32[]{:S(2)}, u32[]{:S(2)}) collective-permute-start(bf16[416,768]{1,0:T(8,128)(2,1)S(1)} %join.2.refs_0_), channel_id=1, source_target_pairs={{0,1},{1,2},{2,3},{3,0},{4,5},{5,6},{6,7},{7,4},{8,9},{9,10},{10,1... | collective-permute-start | bytes 1916936 | tf_op jit(solution)/shard_map/ppermute | solution.py:32
  15.9 24.0 %collective-permute-start.1 = (bf16[416,768]{1,0:T(8,128)(2,1)S(1)}, bf16[416,768]{1,0:T(8,128)(2,1)S(1)}, u32[]{:S(2)}, u32[]{:S(2)}) collective-permute-start(bf16[416,768]{1,0:T(8,128)(2,1)S(1)} %join.2.refs_0_), channel_id=1, source_target_pairs={{0,3},{1,0},{2,1},{3,2},{4,7},{5,4},{6,5},{7,6},{8,11},{9,8},{10,9... | collective-permute-start | bytes 1916936 | tf_op jit(solution)/shard_map/ppermute | solution.py:32
  18.6 11.4 %collective-permute-start.9 = (bf16[192,768]{1,0:T(8,128)(2,1)S(1)}, bf16[192,768]{1,0:T(8,128)(2,1)S(1)}, u32[]{:S(2)}, u32[]{:S(2)}) collective-permute-start(bf16[192,768]{1,0:T(8,128)(2,1)S(1)} %collective-permute-done.5.b_ref), channel_id=1, source_target_pairs={{0,64},{1,65},{2,66},{3,67},{4,68},{5,69},{6,70},{7,71},{8,72},{9,... | collective-permute-start | bytes 884744 | tf_op jit(solution)/shard_map/ppermute | solution.py:32
  20.7 0.7 copy-start.4
  21.4 18.4 %collective-permute-start.7 = (bf16[384,768]{1,0:T(8,128)(2,1)S(1)}, bf16[384,768]{1,0:T(8,128)(2,1)S(1)}, u32[]{:S(2)}, u32[]{:S(2)}) collective-permute-start(bf16[384,768]{1,0:T(8,128)(2,1)S(1)} %join.3.refs_5_), channel_id=1, source_target_pairs={{0,32},{1,33},{2,34},{3,35},{4,36},{5,37},{6,38},{7,39},{8,40},{9,... | collective-permute-start | bytes 1769480 | tf_op jit(solution)/shard_map/ppermute | solution.py:32
  23.0 16.9 %collective-permute-start.6 = (bf16[384,768]{1,0:T(8,128)(2,1)S(1)}, bf16[384,768]{1,0:T(8,128)(2,1)}, u32[]{:S(2)}, u32[]{:S(2)}) collective-permute-start(bf16[384,768]{1,0:T(8,128)(2,1)S(1)} %join.3.refs_5_), channel_id=1, source_target_pairs={{0,96},{1,97},{2,98},{3,99},{4,100},{5,101},{6,102},{7,103},{8,104... | collective-permute-start | bytes 1769480 | tf_op jit(solution)/shard_map/ppermute | solution.py:32
  30.0 0.7 copy-start.6
  30.7 8.8 %collective-permute-start.4 = (bf16[208,768]{1,0:T(8,128)(2,1)}, bf16[208,768]{1,0:T(8,128)(2,1)}, u32[]{:S(2)}, u32[]{:S(2)}) collective-permute-start(bf16[208,768]{1,0:T(8,128)(2,1)} %collective-permute-done.b_ref), channel_id=1, source_target_pairs={{0,2},{1,3},{2,0},{3,1},{4,6},{5,7},{6,4},{7,5},{8,10},{9,11},{10,... | collective-permute-start | bytes 958472 | tf_op jit(solution)/shard_map/ppermute | solution.py:32
  39.9 1.0 copy-start.5
  40.9 1.0 copy-start.7
  43.3 13.5 %collective-permute-start.10 = (bf16[1536,768]{1,0:T(8,128)(2,1)S(1)}, bf16[1536,768]{1,0:T(8,128)(2,1)S(1)}, u32[]{:S(2)}, u32[]{:S(2)}) collective-permute-start(bf16[1536,768]{1,0:T(8,128)(2,1)S(1)} %get-tuple-element.39.y_all.y_own), channel_id=1, source_target_pairs={{0,8},{1,9},{2,10},{3,11},{4,12},{5,13},{6,14},{7,15},{8,0},{9,1},... | collective-permute-start | bytes 7077896 | tf_op jit(solution)/shard_map/ppermute | solution.py:32
  68.7 5.9 %collective-permute-start.11 = (bf16[1552,768]{1,0:T(8,128)(2,1)S(1)}, bf16[1552,768]{1,0:T(8,128)(2,1)S(1)}, u32[]{:S(2)}, u32[]{:S(2)}) collective-permute-start(bf16[1552,768]{1,0:T(8,128)(2,1)S(1)} %get-tuple-element.43), channel_id=1, source_target_pairs={{0,8},{1,9},{2,10},{3,11},{4,12},{5,13},{6,14},{7,15},{8,0},{9,1},... | collective-permute-start | bytes 7151624 | tf_op jit(solution)/shard_map/ppermute | solution.py:32
  71.3 12.9 %collective-permute-start.17 = (bf16[192,768]{1,0:T(8,128)(2,1)S(1)}, bf16[192,768]{1,0:T(8,128)(2,1)S(1)}, u32[]{:S(2)}, u32[]{:S(2)}) collective-permute-start(bf16[192,768]{1,0:T(8,128)(2,1)S(1)} %get-tuple-element.59), channel_id=1, source_target_pairs={{0,1},{1,2},{2,3},{3,0},{4,5},{5,6},{6,7},{7,4},{8,9},{9,10},{10,1... | collective-permute-start | bytes 884744 | tf_op jit(solution)/shard_map/ppermute | solution.py:32
  72.0 12.2 %collective-permute-start.18 = (bf16[192,768]{1,0:T(8,128)(2,1)S(1)}, bf16[192,768]{1,0:T(8,128)(2,1)S(1)}, u32[]{:S(2)}, u32[]{:S(2)}) collective-permute-start(bf16[192,768]{1,0:T(8,128)(2,1)S(1)} %get-tuple-element.60), channel_id=1, source_target_pairs={{0,3},{1,0},{2,1},{3,2},{4,7},{5,4},{6,5},{7,6},{8,11},{9,8},{10,9... | collective-permute-start | bytes 884744 | tf_op jit(solution)/shard_map/ppermute | solution.py:32
  75.2 12.6 %collective-permute-start.12 = (bf16[192,768]{1,0:T(8,128)(2,1)S(1)}, bf16[192,768]{1,0:T(8,128)(2,1)S(1)}, u32[]{:S(2)}, u32[]{:S(2)}) collective-permute-start(bf16[192,768]{1,0:T(8,128)(2,1)S(1)} %get-tuple-element.48), channel_id=1, source_target_pairs={{0,32},{1,33},{2,34},{3,35},{4,36},{5,37},{6,38},{7,39},{8,40},{9,... | collective-permute-start | bytes 884744 | tf_op jit(solution)/shard_map/ppermute | solution.py:32
  76.5 11.2 %collective-permute-start.13 = (bf16[192,768]{1,0:T(8,128)(2,1)S(1)}, bf16[192,768]{1,0:T(8,128)(2,1)S(1)}, u32[]{:S(2)}, u32[]{:S(2)}) collective-permute-start(bf16[192,768]{1,0:T(8,128)(2,1)S(1)} %get-tuple-element.49), channel_id=1, source_target_pairs={{0,96},{1,97},{2,98},{3,99},{4,100},{5,101},{6,102},{7,103},{8,104... | collective-permute-start | bytes 884744 | tf_op jit(solution)/shard_map/ppermute | solution.py:32
  84.4 15.4 %collective-permute-start.19 = (bf16[384,768]{1,0:T(8,128)(2,1)S(1)}, bf16[384,768]{1,0:T(8,128)(2,1)S(1)}, u32[]{:S(2)}, u32[]{:S(2)}) collective-permute-start(bf16[384,768]{1,0:T(8,128)(2,1)S(1)} %get-tuple-element.61), channel_id=1, source_target_pairs={{0,1},{1,2},{2,3},{3,0},{4,5},{5,6},{6,7},{7,4},{8,9},{9,10},{10,1... | collective-permute-start | bytes 1769480 | tf_op jit(solution)/shard_map/ppermute | solution.py:32
  84.5 15.3 %collective-permute-start.20 = (bf16[384,768]{1,0:T(8,128)(2,1)S(1)}, bf16[384,768]{1,0:T(8,128)(2,1)S(1)}, u32[]{:S(2)}, u32[]{:S(2)}) collective-permute-start(bf16[384,768]{1,0:T(8,128)(2,1)S(1)} %get-tuple-element.62), channel_id=1, source_target_pairs={{0,3},{1,0},{2,1},{3,2},{4,7},{5,4},{6,5},{7,6},{8,11},{9,8},{10,9... | collective-permute-start | bytes 1769480 | tf_op jit(solution)/shard_map/ppermute | solution.py:32
  87.9 29.5 %copy-start.1 = (bf16[192,768]{1,0:T(8,128)(2,1)S(1)}, bf16[192,768]{1,0:T(8,128)(2,1)}, u32[]{:S(2)}) copy-start(bf16[192,768]{1,0:T(8,128)(2,1)} %values_ref.3) | copy-start | bytes 884740
  87.9 15.7 %collective-permute-start.14 = (bf16[384,768]{1,0:T(8,128)(2,1)S(1)}, bf16[384,768]{1,0:T(8,128)(2,1)S(1)}, u32[]{:S(2)}, u32[]{:S(2)}) collective-permute-start(bf16[384,768]{1,0:T(8,128)(2,1)S(1)} %get-tuple-element.51), channel_id=1, source_target_pairs={{0,32},{1,33},{2,34},{3,35},{4,36},{5,37},{6,38},{7,39},{8,40},{9,... | collective-permute-start | bytes 1769480 | tf_op jit(solution)/shard_map/ppermute | solution.py:32
  88.1 15.6 %collective-permute-start.15 = (bf16[384,768]{1,0:T(8,128)(2,1)S(1)}, bf16[384,768]{1,0:T(8,128)(2,1)S(1)}, u32[]{:S(2)}, u32[]{:S(2)}) collective-permute-start(bf16[384,768]{1,0:T(8,128)(2,1)S(1)} %get-tuple-element.52), channel_id=1, source_target_pairs={{0,96},{1,97},{2,98},{3,99},{4,100},{5,101},{6,102},{7,103},{8,104... | collective-permute-start | bytes 1769480 | tf_op jit(solution)/shard_map/ppermute | solution.py:32
  91.2 3.6 %collective-permute-start.21 = (f32[8,128]{1,0:T(8,128)S(1)}, f32[8,128]{1,0:T(8,128)S(1)}, u32[]{:S(2)}, u32[]{:S(2)}) collective-permute-start(f32[8,128]{1,0:T(8,128)S(1)} %get-tuple-element.63), channel_id=1, source_target_pairs={{0,16},{1,17},{2,18},{3,19},{4,20},{5,21},{6,22},{7,23},{8,24},{9,... | collective-permute-start | bytes 12296 | tf_op jit(solution)/shard_map/ppermute | solution.py:32
  94.9 5.0 %collective-permute-start.22 = (f32[8,128]{1,0:T(8,128)S(1)}, f32[8,128]{1,0:T(8,128)S(1)}, u32[]{:S(2)}, u32[]{:S(2)}) collective-permute-start(f32[8,128]{1,0:T(8,128)S(1)} %add.29), channel_id=1, source_target_pairs={{0,20},{1,21},{2,22},{3,23},{4,16},{5,17},{6,18},{7,19},{8,28},{9,... | collective-permute-start | bytes 12296 | tf_op jit(solution)/shard_map/ppermute | solution.py:32
  99.8 3.6 %collective-permute-start.23 = (f32[8,128]{1,0:T(8,128)S(1)}, f32[8,128]{1,0:T(8,128)S(1)}, u32[]{:S(2)}, u32[]{:S(2)}) collective-permute-start(f32[8,128]{1,0:T(8,128)S(1)} %add.30.loss), channel_id=1, source_target_pairs={{0,1},{1,0},{2,3},{3,2},{4,5},{5,4},{6,7},{7,6},{8,9},{9,8},{10,11... | collective-permute-start | bytes 12296 | tf_op jit(solution)/shard_map/ppermute | solution.py:32
  103.5 13.9 %collective-permute-start.27 = (bf16[192,768]{1,0:T(8,128)(2,1)S(1)}, bf16[192,768]{1,0:T(8,128)(2,1)S(1)}, u32[]{:S(2)}, u32[]{:S(2)}) collective-permute-start(bf16[192,768]{1,0:T(8,128)(2,1)S(1)} %get-tuple-element.67), channel_id=1, source_target_pairs={{0,16},{1,17},{2,18},{3,19},{4,20},{5,21},{6,22},{7,23},{8,24},{9,... | collective-permute-start | bytes 884744 | tf_op jit(solution)/shard_map/ppermute | solution.py:32
  103.6 17.3 %copy-start.3 = (bf16[192,768]{1,0:T(8,128)(2,1)S(1)}, bf16[192,768]{1,0:T(8,128)(2,1)}, u32[]{:S(2)}) copy-start(bf16[192,768]{1,0:T(8,128)(2,1)} %values_ref.2) | copy-start | bytes 884740
  103.8 17.2 %collective-permute-start.16 = (bf16[192,768]{1,0:T(8,128)(2,1)S(1)}, bf16[192,768]{1,0:T(8,128)(2,1)S(1)}, u32[]{:S(2)}, u32[]{:S(2)}) collective-permute-start(bf16[192,768]{1,0:T(8,128)(2,1)S(1)} %far.2), channel_id=1, source_target_pairs={{0,20},{1,21},{2,22},{3,23},{4,16},{5,17},{6,18},{7,19},{8,28},{9,... | collective-permute-start | bytes 884744 | tf_op jit(solution)/shard_map/ppermute | solution.py:32
  107.1 5.1 %collective-permute-start.24 = (f32[8,128]{1,0:T(8,128)S(1)}, f32[8,128]{1,0:T(8,128)S(1)}, u32[]{:S(2)}, u32[]{:S(2)}) collective-permute-start(f32[8,128]{1,0:T(8,128)S(1)} %get-tuple-element.64), channel_id=1, source_target_pairs={{0,2},{1,3},{2,0},{3,1},{4,6},{5,7},{6,4},{7,5},{8,10},{9,11},{10,... | collective-permute-start | bytes 12296 | tf_op jit(solution)/shard_map/ppermute | solution.py:32
  112.2 3.6 %collective-permute-start.25 = (f32[8,128]{1,0:T(8,128)S(1)}, f32[8,128]{1,0:T(8,128)S(1)}, u32[]{:S(2)}, u32[]{:S(2)}) collective-permute-start(f32[8,128]{1,0:T(8,128)S(1)} %add.31), channel_id=1, source_target_pairs={{0,32},{1,33},{2,34},{3,35},{4,36},{5,37},{6,38},{7,39},{8,40},{9,... | collective-permute-start | bytes 12296 | tf_op jit(solution)/shard_map/ppermute | solution.py:32
  115.8 5.1 %collective-permute-start.26 = (f32[8,128]{1,0:T(8,128)S(1)}, f32[8,128]{1,0:T(8,128)S(1)}, u32[]{:S(2)}, u32[]{:S(2)}) collective-permute-start(f32[8,128]{1,0:T(8,128)S(1)} %add.32.loss), channel_id=1, source_target_pairs={{0,64},{1,65},{2,66},{3,67},{4,68},{5,69},{6,70},{7,71},{8,72},{9,... | collective-permute-start | bytes 12296 | tf_op jit(solution)/shard_map/ppermute | solution.py:32

commit v3 on v2

v3 whole, which is shorter than its diff:
```python
import functools

import jax
import jax.numpy as jnp
from jax import lax
from jax.experimental import pallas as pl
from jax.experimental.pallas import tpu as pltpu
from jax.sharding import PartitionSpec as P

EPS = 1e-06
LOG2E = 1.4426950408889634
N_ROW = 16
N_COL = 8
R = 192
D = 768
RX = R + 16
NX = R * 8
NY = R * 8
FIRST = 4 * R
NEAR = 6 * R
NT = (((1,), (1,)), ((), ()))
TN = (((0,), (0,)), ((), ()))
F32, BF16 = jnp.float32, jnp.bfloat16
LOSS = ((8, 128), F32)
PARTS = [((R, D), F32), ((R, D), F32), ((2 * R, D), F32), ((2 * R, D), F32)]
AWAY = [((R, D), BF16), ((R, D), BF16)]
VMEM = pl.BlockSpec(memory_space=pltpu.VMEM)
SMEM = pl.BlockSpec(memory_space=pltpu.SMEM)


def send(value, move):
    pairs = []
    for r in range(N_ROW):
        for c in range(N_COL):
            y, zl, k, zh, x = move(r // 4, (r // 2) % 2, r % 2, c // 4, c % 4)
            pairs.append((r * N_COL + c, (((y % 4) * 2 + zl % 2) * 2 + k % 2) * N_COL + (zh % 2) * 4 + x % 4))
    return lax.ppermute(value, ("row", "col"), pairs)


def send_x(value, d):
    return send(value, lambda y, zl, k, zh, x: (y, zl, k, zh, x + d))


def send_y(value, d):
    return send(value, lambda y, zl, k, zh, x: (y + d, zl, k, zh, x))


def send_core(value):
    return send(value, lambda y, zl, k, zh, x: (y, zl, 1 - k, zh, x))


def swap_image_z(value):
    return send(value, lambda y, zl, k, zh, x: (y, 1 - zl, k, zh, x))


def swap_text_z(value):
    return send(value, lambda y, zl, k, zh, x: (y, 1 - zl, k, 1 - zh, x))


def normalize(ref):
    wide = ref[...].astype(jnp.float32)
    inverse = lax.rsqrt(jnp.sum(wide * wide, axis=-1, keepdims=True) + EPS)
    return wide * inverse, inverse


def call(kernel, outs, *args, name, scalars=0, aliases=None, scratch=(), flops=0, vmem=4, after=()):
    count = len(args)

    def body(*refs):
        kernel(*refs[:count], *refs[count + len(after) :])

    return pl.pallas_call(
        body,
        in_specs=[SMEM] * scalars + [VMEM] * (count - scalars + len(after)),
        out_specs=[VMEM] * len(outs),
        out_shape=[jax.ShapeDtypeStruct(shape, dtype) for shape, dtype in outs],
        input_output_aliases=aliases or {},
        scratch_shapes=scratch,
        compiler_params=pltpu.CompilerParams(vmem_limit_bytes=vmem << 20),
        cost_estimate=pl.CostEstimate(flops=flops, bytes_accessed=4 << 20, transcendentals=0),
        name=name,
    )(*args, *after)


def prep_kernel(log_scale_ref, bias_ref, images_hbm, texts_hbm, pair_hbm, x_ref, y_ref, const_ref, images, texts, pairs, sems):
    copies = [
        pltpu.make_async_copy(source, target, sems.at[i])
        for i, (source, target) in enumerate(((images_hbm, images), (texts_hbm, texts), (pair_hbm, pairs)))
    ]
    for copy in copies:
        copy.start()
    scale = jnp.exp(jnp.full((8, 128), log_scale_ref[0], F32))
    const_ref[:8, :] = scale * LOG2E
    const_ref[8:16, :] = jnp.full((8, 128), bias_ref[0] * LOG2E, F32)
    const_ref[16:, :] = scale
    for copy in copies:
        copy.wait()
    x_ref[:R, :] = normalize(images)[0].astype(BF16)
    y_ref[...] = normalize(texts)[0].astype(BF16)
    pair = pairs[...]
    shard = ((pair.astype(F32) + 0.5) * (1.0 / R)).astype(jnp.int32)
    x_ref[R:, :] = jnp.zeros((16, D), BF16)
    x_ref[R:, :R] = jnp.broadcast_to(shard.astype(F32), (16, R)).astype(BF16)
    x_ref[R:, 256 : 256 + R] = jnp.broadcast_to((pair - shard * R).astype(F32), (16, R)).astype(BF16)


def place_codes(codes):
    row, col = lax.axis_index("row"), lax.axis_index("col")
    my_y, my_zl, my_k, my_zh, my_x = row >> 2, (row >> 1) & 1, row & 1, col >> 2, col & 3
    codes = codes.astype(jnp.float32).astype(jnp.int32)[:1, :]
    shard, offset = codes[:, :R], codes[:, 256 : 256 + R]
    dz = (shard >> 6) ^ my_zh
    dy = (((shard >> 2) & 3) - my_y) & 3
    dk = (shard & 1) ^ my_k
    mine = (((shard >> 4) & 3) == my_x) & (dz == (((shard >> 1) & 1) ^ my_zl))
    slot = jnp.where(dy == 2, 6 + dz, jnp.where(dy == 0, dz, 2 * dz + jnp.where(dy == 1, 2, 3)))
    return jnp.where(mine, (dk * 8 + slot) * R + offset, -1)


def near_image_kernel(*refs):
    for i, ref in enumerate(refs[:6]):
        here = slice(i * R, (i + 1) * R)
        refs[6][here, :] = ref[:R, :]
        refs[7][:, here] = place_codes(ref[R:, :])


def text_kernel(first, *refs):
    slot = first
    for ref in refs[:-1]:
        if ref.shape[0] == R:
            refs[-1][slot * R : (slot + 1) * R, :] = ref[...]
            slot += 1


def gate_kernel(value, out):
    out[...] = value[...]


def gate(value, *after):
    return call(gate_kernel, [(value.shape, value.dtype)], value, name="gate", after=after)[0]


def away_image_kernel(x_in, place_in, two, two_z, out, place):
    place[...] = place_in[...]
    for slot, ref in ((6, two), (7, two_z)):
        here = slice(slot * R, (slot + 1) * R)
        out[here, :] = ref[:R, :]
        place[:, here] = place_codes(ref[R:, :])


def weigh(x, y, first, place, sc_ref):
    slope, shift, scale = sc_ref[0:1, 0:1], sc_ref[8:9, 0:1], sc_ref[16:17, 0:1]
    score = lax.dot_general(y, x, NT, preferred_element_type=jnp.float32)
    paired = place == first + lax.broadcasted_iota(jnp.int32, score.shape, 0)
    z = score * slope + shift
    z = jnp.where(paired, -z, z)
    t = jnp.exp2(z)
    total = 1.0 + t
    weight = (jnp.where(paired, -scale, scale) * (t / total)).astype(jnp.bfloat16)
    loss = jnp.where(t < 2.0**-8, t * (LOG2E - t * (0.5 * LOG2E)), jnp.log2(total))
    return weight, jnp.sum(loss.reshape(y.shape[0] // 8, 8, x.shape[0]), axis=0)


def score_first_kernel(consts, x_all, y_all, place, gy_out, weights, loss_ref):
    x = x_all[:NEAR, :]
    weight, loss = weigh(x, y_all[:FIRST, :], 0, place[:, :NEAR], consts)
    weights[:FIRST, :NEAR] = weight
    gy_out[:FIRST, :] = jnp.dot(weight, x, preferred_element_type=F32)
    loss_ref[...] = jnp.zeros((8, 128), F32) + jnp.sum(loss)


def score_second_kernel(consts, x_all, y_all, place, loss_in, gy_in, w_in, gy_out, weights, loss_ref):
    x = x_all[:NEAR, :]
    weight, loss = weigh(x, y_all[FIRST:NEAR, :], FIRST, place[:, :NEAR], consts)
    weights[FIRST:NEAR, :NEAR] = weight
    gy_out[FIRST:NEAR, :] = jnp.dot(weight, x, preferred_element_type=F32)
    loss_ref[...] = loss_in[...] + jnp.sum(loss)


def score_rest_kernel(consts, x_all, y_all, place, loss_in, gy_in, w_in, gy_out, weights, loss_ref):
    x = x_all[NEAR:, :]
    weight, loss = weigh(x, y_all[:NEAR, :], 0, place[:, NEAR:], consts)
    weights[:NEAR, NEAR:] = weight
    gy_out[:NEAR, :] = gy_in[:NEAR, :] + jnp.dot(weight, x, preferred_element_type=F32)
    total = jnp.sum(loss)
    x = x_all[...]
    weight, loss = weigh(x, y_all[NEAR:, :], NEAR, place[...], consts)
    weights[NEAR:, :] = weight
    gy_out[NEAR:, :] = jnp.dot(weight, x, preferred_element_type=F32)
    loss_ref[...] = loss_in[...] + total + jnp.sum(loss)


def score_sib_kernel(consts, x_all, y_all, place, loss_in, gy_out, weights, loss_ref, loss_acc):
    loss_acc[...] = jnp.zeros_like(loss_acc)

    def step(i, carry):
        base = pl.multiple_of(i * FIRST, FIRST)
        here = pl.ds(base, FIRST)
        x = x_all[...]
        weight, loss = weigh(x, y_all[here, :], NY + base, place[...], consts)
        loss_acc[...] += loss
        weights[here, :] = weight
        gy_out[here, :] = jnp.dot(weight, x, preferred_element_type=F32).astype(BF16)
        return carry

    lax.fori_loop(0, NY // FIRST, step, 0)
    loss = loss_in[...] + jnp.sum(loss_acc[...])
    loss_ref[...] = loss
    gy_out[NY:, :] = jnp.zeros((16, D), jnp.bfloat16)
    for i in range(3):
        part = loss.astype(jnp.bfloat16)
        gy_out[NY:, i * 128 : i * 128 + 128] = jnp.concatenate([part, part], axis=0)
        loss = loss - part.astype(jnp.float32)


def image_kernel(slots, w_own, w_sib, y_own, y_sib, *outs):
    outs = list(outs)
    for slot in slots:
        here = slice(slot * R, slot * R + 2 * R)
        grad = lax.dot_general(w_own[:, here], y_own[...], TN, preferred_element_type=F32)
        grad += lax.dot_general(w_sib[:, here], y_sib[...], TN, preferred_element_type=F32)
        at = 0
        while at < 2 * R:
            ref = outs.pop(0)
            ref[...] = grad[at : at + ref.shape[0], :].astype(ref.dtype)
            at += ref.shape[0]


def add_kernel(direct, sibling, loss, own, zed, plus, minus, two, two_z, loss_out):
    def part(slot):
        here = slice(slot * R, (slot + 1) * R)
        return direct[here, :] + sibling[here, :].astype(F32)

    own[...], zed[...] = part(0), part(1)
    plus[:R, :], plus[R:, :] = part(2), part(4)
    minus[:R, :], minus[R:, :] = part(3), part(5)
    two[...], two_z[...] = part(6).astype(BF16), part(7).astype(BF16)
    total = loss[...]
    for i in range(3):
        total = total + sibling[NY : NY + 8, i * 128 : i * 128 + 128].astype(jnp.float32)
    loss_out[...] = total


def turn_kernel(plus, minus, two, two_z, plus_out, minus_out):
    plus_out[:R, :] = (plus[:R, :] + two[...].astype(F32)).astype(BF16)
    plus_out[R:, :] = plus[R:, :].astype(BF16)
    minus_out[:R, :] = minus[:R, :].astype(BF16)
    minus_out[R:, :] = (minus[R:, :] + two_z[...].astype(F32)).astype(BF16)


def turn_loss_kernel(plus, minus, two, two_z, loss, plus_out, minus_out, loss_out):
    turn_kernel(plus, minus, two, two_z, plus_out, minus_out)
    loss_out[...] = loss[...]


def far_kernel(own, plus, minus, out):
    out[...] = (own[...] + plus[R:, :].astype(F32) + minus[R:, :].astype(F32)).astype(BF16)


def far_loss_kernel(own, plus, minus, loss, step, out, loss_out):
    far_kernel(own, plus, minus, out)
    loss_out[...] = loss[...] + step[...]


def final_kernel(values_ref, own_ref, plus, minus, zed, out_ref):
    unit, inverse = normalize(values_ref)
    grad = own_ref[...] + plus[:R, :].astype(F32) + minus[:R, :].astype(F32) + zed[...].astype(F32)
    along = jnp.sum(grad * unit, axis=-1, keepdims=True)
    out_ref[...] = (grad - unit * along) * inverse


def final_loss_kernel(values_ref, own_ref, plus, minus, zed, loss, step, out_ref, loss_out):
    final_kernel(values_ref, own_ref, plus, minus, zed, out_ref)
    loss_out[...] = (loss[...] + step[...]) * (1.0 / (LOG2E * R * N_ROW * N_COL))


def turn(near, away, shift, *loss):
    two, two_z = shift(away[0], 1), shift(away[1], -1)
    outs = [((2 * R, D), BF16)] * 2
    if loss:
        return call(turn_loss_kernel, outs + [LOSS], near[2], near[3], two, two_z, *loss, name="turn", vmem=8)
    return call(turn_kernel, outs, near[2], near[3], two, two_z, name="turn", vmem=8)


def far(near, plus, minus, swap, *loss):
    out = ((R, D), BF16)
    if loss:
        value, total = call(far_loss_kernel, [out, LOSS], near[1], plus, minus, *loss, name="far")
        return swap(value), total
    return swap(call(far_kernel, [out], near[1], plus, minus, name="far")[0])


def local(images, texts, pair_index, log_scale, bias):
    x_low, y_low, consts = pl.pallas_call(
        prep_kernel,
        in_specs=[SMEM] * 2 + [pl.BlockSpec(memory_space=pltpu.HBM)] * 3,
        out_specs=[VMEM] * 3,
        out_shape=[jax.ShapeDtypeStruct(*out) for out in (((RX, D), BF16), ((R, D), BF16), ((24, 128), F32))],
        scratch_shapes=[
            pltpu.VMEM((R, D), BF16),
            pltpu.VMEM((R, D), BF16),
            pltpu.VMEM((1, R), jnp.int32),
            pltpu.SemaphoreType.DMA((3,)),
        ],
        compiler_params=pltpu.CompilerParams(vmem_limit_bytes=56 << 20),
        name="prep",
    )(log_scale, bias, images, texts, pair_index.reshape(1, R))
    x_zed, y_zed = swap_image_z(x_low), swap_text_z(y_low)
    x_plus, x_minus = send_x(x_low, -1), send_x(x_low, 1)
    y_plus, y_minus = send_y(y_low, -1), send_y(y_low, 1)
    x_next = gate(x_zed, x_plus, x_minus)
    y_next = gate(y_zed, y_plus, y_minus, x_next)
    x_plus_z, x_minus_z = send_x(x_next, -1), send_x(x_next, 1)
    y_plus_z, y_minus_z = send_y(y_next, -1), send_y(y_next, 1)
    x_two, x_two_z = send_x(x_minus, 1), send_x(x_plus_z, -1)
    y_two, y_two_z = send_y(y_minus, 1), send_y(y_plus_z, -1)

    image_rows, places = ((NX, D), BF16), ((1, NX), jnp.int32)
    x_all, place = call(
        near_image_kernel, [image_rows, places], x_low, x_zed, x_plus, x_plus_z, x_minus, x_minus_z,
        name="near_images", vmem=8,
    )
    text_rows = ((NY, D), BF16)
    y_all = call(
        functools.partial(text_kernel, 0), [text_rows], y_low, y_zed, y_plus, y_minus,
        name="first_texts", after=(x_all, x_two),
    )[0]

    flops = 4 * NX * NY * D
    scored = [((NY, D), F32), ((NY, NX), BF16), LOSS]
    gy_own, w_own, loss = call(
        score_first_kernel, scored, consts, x_all, y_all, place, name="score_first", flops=flops * 3 // 8, vmem=24
    )
    y_all = call(
        functools.partial(text_kernel, 4), [text_rows], y_all, y_plus_z, y_minus_z,
        name="second_texts", aliases={0: 0}, after=(loss, x_two_z),
    )[0]
    gy_own, w_own, loss = call(
        score_second_kernel, scored, consts, x_all, y_all, place, loss, gy_own, w_own,
        name="score_second", flops=flops * 3 // 16, vmem=20, aliases={5: 0, 6: 1},
    )
    x_all, place = call(
        away_image_kernel, [image_rows, places], x_all, place, x_two, x_two_z,
        name="away_images", aliases={0: 0}, after=(loss,),
    )
    y_all = call(
        functools.partial(text_kernel, 6), [text_rows], y_all, y_two, y_two_z,
        name="away_texts", aliases={0: 0}, after=(loss,),
    )[0]
    s_all = send_core(y_all)
    gy_own, w_own, loss = call(
        score_rest_kernel, scored, consts, x_all, y_all, place, loss, gy_own, w_own,
        name="score_rest", flops=flops * 7 // 16, vmem=30, aliases={5: 0, 6: 1},
    )
    gy_sib, w_sib, loss = call(
        score_sib_kernel, [((NY + 16, D), BF16)] + scored[1:], consts, x_all, s_all, place, loss,
        name="score_sib", flops=flops, vmem=30, scratch=[pltpu.VMEM((8, NX), F32)],
    )
    gy_core = send_core(gy_sib)
    weights = (w_own, w_sib, y_all, s_all)
    gx_away = call(functools.partial(image_kernel, (6,)), AWAY, *weights, name="image_away", flops=flops // 8, vmem=16)
    *gy, loss = call(add_kernel, PARTS + AWAY + [LOSS], gy_own, gy_core, loss, name="add", vmem=16)
    gy_near, gy_away = gy[:4], gy[4:]

    gx_ring = call(
        functools.partial(image_kernel, (2, 4)), PARTS[2:], *weights, name="image_ring", flops=flops // 4, vmem=16
    )
    gx_near = call(
        functools.partial(image_kernel, (0,)), PARTS[:2], *weights, name="image_near", flops=flops // 8, vmem=16
    )
    gx_near = gx_near + gx_ring
    gx_plus, gx_minus = turn(gx_near, gx_away, send_x)
    gy_plus, gy_minus, loss = turn(gy_near, gy_away, send_y, loss)
    gx_plus, gx_minus = send_x(gx_plus, 1), send_x(gx_minus, -1)
    gy_plus, gy_minus = send_y(gy_plus, 1), send_y(gy_minus, -1)

    loss = loss + swap_image_z(loss)
    loss = loss + swap_text_z(loss)
    step = send(loss, lambda y, zl, k, zh, x: (y, zl, k, zh, x ^ 1))
    gx_far, loss = far(gx_near, gx_plus, gx_minus, swap_image_z, loss, step)
    gy_far = far(gy_near, gy_plus, gy_minus, swap_text_z)
    loss = loss + send(loss, lambda y, zl, k, zh, x: (y, zl, k, zh, x ^ 2))
    loss = loss + send(loss, lambda y, zl, k, zh, x: (y ^ 1, zl, k, zh, x))
    step = send(loss, lambda y, zl, k, zh, x: (y ^ 2, zl, k, zh, x))

    grad = ((R, D), F32)
    grad_x = call(final_kernel, [grad], images, gx_near[0], gx_plus, gx_minus, gx_far, name="unproject")[0]
    grad_y, loss = call(
        final_loss_kernel, [grad, LOSS], texts, gy_near[0], gy_plus, gy_minus, gy_far, loss, step, name="unproject"
    )
    return loss[0, :1], grad_x, grad_y


def solution(mesh):
    return jax.shard_map(
        local,
        mesh=mesh,
        in_specs=(P(("row", "col"), None), P(("col", "row"), None), P(("row", "col")), P(), P()),
        out_specs=(P(), P(("row", "col"), None), P(("col", "row"), None)),
        check_vma=False,
    )
```

time: 123 us -> 113 us (0.919)
  waiting for transfers between devices: 32.3 us -> 25 us
  local copies, waits for them, and re-layouts: 6.55 us -> 1.15 us
  starting transfers between devices: 43.9 us -> 47.3 us
    ppermute x28 -> x32, waiting for transfers between devices: 32.3 us -> 25 us  [send(): return lax.ppermute(value, ('row', 'col'), pairs)]
    unnamed x18 -> x10, local copies, waits for them, and re-layouts: 5.95 us -> 0.64 us
    ppermute x28 -> x32, starting transfers between devices: 43.9 us -> 47.3 us  [send(): return lax.ppermute(value, ('row', 'col'), pairs)]
    pallas_call x15 -> x22, Pallas kernels: 37.6 us -> 37.1 us  [the longest x21 35 us: call(): pl.pallas_call(body, in_specs=[SMEM] * scalars + [VMEM] * (count - scalar...]
  transfers between devices with their start and end apart: 28 -> 32, of which waited for: 10 -> 9; matrix products, arithmetic and copies ran while one was open for 0% -> 0% of each run, Pallas kernels for 19% -> 21%
where the time goes in v3:
time: 113 us
  starting transfers between devices  47.3 us (42%)
  Pallas kernels  37.1 us (33%)
  waiting for transfers between devices  25 us (22%)
  between operations  2.23 us (2%)
  local copies, waits for them, and re-layouts  1.15 us (1%)
    ppermute x32, starting transfers between devices, send(): return lax.ppermute(value, ('row', 'col'), pairs)  47.3 us
    pallas_call x21, Pallas kernels, call(): pl.pallas_call(body, in_specs=[SMEM] * scalars + [VMEM] * (count - scalar...  35 us
    ppermute x32, waiting for transfers between devices, send(): return lax.ppermute(value, ('row', 'col'), pairs)  25 us
  transfers between devices with their start and end apart: 32, of which 9 were waited for; matrix products, arithmetic and copies ran while one was open for 0% of the time, Pallas kernels for 21%

profile of v3, /device:TPU:0, one launch (start us, length us, event | category | flops | bytes accessed | tf_op | source)
XLA Modules:
  0.0 112.8 jit_solution(13096440521752990048)
XLA Ops:
  1.9 2.1 %prep.1 = (bf16[208,768]{1,0:T(8,128)(2,1)}, bf16[192,768]{1,0:T(8,128)(2,1)}, f32[24,128]{1,0:T(8,128)}) custom-call(f32[1]{0:T(128)S(6)} %copy.22.log_scale_ref, f32[1]{0:T(128)S(6)} %copy.23.bias_ref, bf16[192,768]{1,0:T(8,128)(2,1)} %refs_0_.3, bf16[192,768]{1,0:T(8,128)(2,1)} %refs_0_.2, s32[1,192]{1,0:T(1,128)} %bitcast.2), custom_call_target="tpu_custom_call" | custom-call | tf_op jit(solution)/shard_map/prep/pallas_call | solution.py:294
  4.0 0.0 copy-start.2
  4.0 0.0 copy-start.3
  4.0 1.6 %collective-permute-start.2 = (bf16[208,768]{1,0:T(8,128)(2,1)}, bf16[208,768]{1,0:T(8,128)(2,1)S(1)}, u32[]{:S(2)}, u32[]{:S(2)}) collective-permute-start(bf16[208,768]{1,0:T(8,128)(2,1)} %get-tuple-element.45.refs_0_), channel_id=1, source_target_pairs={{0,1},{1,2},{2,3},{3,0},{4,5},{5,6},{6,7},{7,4},{8,9},{9,10},{10,1... | collective-permute-start | bytes 958472 | tf_op jit(solution)/shard_map/ppermute | solution.py:37
  5.7 1.7 %collective-permute-start.1 = (bf16[208,768]{1,0:T(8,128)(2,1)}, bf16[208,768]{1,0:T(8,128)(2,1)S(1)}, u32[]{:S(2)}, u32[]{:S(2)}) collective-permute-start(bf16[208,768]{1,0:T(8,128)(2,1)} %get-tuple-element.45.refs_0_), channel_id=1, source_target_pairs={{0,3},{1,0},{2,1},{3,2},{4,7},{5,4},{6,5},{7,6},{8,11},{9,8},{10,9... | collective-permute-start | bytes 958472 | tf_op jit(solution)/shard_map/ppermute | solution.py:37
  7.3 2.0 %collective-permute-start = (bf16[208,768]{1,0:T(8,128)(2,1)}, bf16[208,768]{1,0:T(8,128)(2,1)S(1)}, u32[]{:S(2)}, u32[]{:S(2)}) collective-permute-start(bf16[208,768]{1,0:T(8,128)(2,1)} %get-tuple-element.45.refs_0_), channel_id=1, source_target_pairs={{0,16},{1,17},{2,18},{3,19},{4,20},{5,21},{6,22},{7,23},{8,24},{9,... | collective-permute-start | bytes 958472 | tf_op jit(solution)/shard_map/ppermute | solution.py:37
  9.3 1.6 %collective-permute-start.9 = (bf16[192,768]{1,0:T(8,128)(2,1)}, bf16[192,768]{1,0:T(8,128)(2,1)S(1)}, u32[]{:S(2)}, u32[]{:S(2)}) collective-permute-start(bf16[192,768]{1,0:T(8,128)(2,1)} %get-tuple-element.48.refs_0_), channel_id=1, source_target_pairs={{0,32},{1,33},{2,34},{3,35},{4,36},{5,37},{6,38},{7,39},{8,40},{9,... | collective-permute-start | bytes 884744 | tf_op jit(solution)/shard_map/ppermute | solution.py:37
  10.9 1.7 %collective-permute-start.8 = (bf16[192,768]{1,0:T(8,128)(2,1)}, bf16[192,768]{1,0:T(8,128)(2,1)S(1)}, u32[]{:S(2)}, u32[]{:S(2)}) collective-permute-start(bf16[192,768]{1,0:T(8,128)(2,1)} %get-tuple-element.48.refs_0_), channel_id=1, source_target_pairs={{0,96},{1,97},{2,98},{3,99},{4,100},{5,101},{6,102},{7,103},{8,104... | collective-permute-start | bytes 884744 | tf_op jit(solution)/shard_map/ppermute | solution.py:37
  12.6 2.1 %collective-permute-done.2.refs_2_.refs_4_ = bf16[208,768]{1,0:T(8,128)(2,1)S(1)} collective-permute-done((bf16[208,768]{1,0:T(8,128)(2,1)}, bf16[208,768]{1,0:T(8,128)(2,1)S(1)}, u32[]{:S(2)}, u32[]{:S(2)}) %collective-permute-start.2) | collective-permute-done | bytes 319520 | tf_op jit(solution)/shard_map/ppermute | solution.py:37
  14.7 4.2 %collective-permute-start.7 = (bf16[192,768]{1,0:T(8,128)(2,1)}, bf16[192,768]{1,0:T(8,128)(2,1)S(1)}, u32[]{:S(2)}, u32[]{:S(2)}) collective-permute-start(bf16[192,768]{1,0:T(8,128)(2,1)} %get-tuple-element.48.refs_0_), channel_id=1, source_target_pairs={{0,20},{1,21},{2,22},{3,23},{4,16},{5,17},{6,18},{7,19},{8,28},{9,... | collective-permute-start | bytes 884744 | tf_op jit(solution)/shard_map/ppermute | solution.py:37
  18.9 1.6 %collective-permute-start.3 = (bf16[208,768]{1,0:T(8,128)(2,1)S(1)}, bf16[208,768]{1,0:T(8,128)(2,1)S(1)}, u32[]{:S(2)}, u32[]{:S(2)}) collective-permute-start(bf16[208,768]{1,0:T(8,128)(2,1)S(1)} %gate.2.refs_3_), channel_id=1, source_target_pairs={{0,3},{1,0},{2,1},{3,2},{4,7},{5,4},{6,5},{7,6},{8,11},{9,8},{10,9... | collective-permute-start | bytes 958472 | tf_op jit(solution)/shard_map/ppermute | solution.py:37
  20.6 0.5 collective-permute-start.4
  21.0 0.0 collective-permute-done.9.refs_3_.refs_2_
  21.0 0.3 collective-permute-start.5
  21.3 3.9 %collective-permute-done.7.refs_1_.refs_0_ = bf16[192,768]{1,0:T(8,128)(2,1)S(1)} collective-permute-done((bf16[192,768]{1,0:T(8,128)(2,1)}, bf16[192,768]{1,0:T(8,128)(2,1)S(1)}, u32[]{:S(2)}, u32[]{:S(2)}) %collective-permute-start.7) | collective-permute-done | bytes 294944 | tf_op jit(solution)/shard_map/ppermute | solution.py:37
  25.3 3.1 %collective-permute-start.10 = (bf16[192,768]{1,0:T(8,128)(2,1)S(1)}, bf16[192,768]{1,0:T(8,128)(2,1)S(1)}, u32[]{:S(2)}, u32[]{:S(2)}) collective-permute-start(bf16[192,768]{1,0:T(8,128)(2,1)S(1)} %gate.3), channel_id=1, source_target_pairs={{0,96},{1,97},{2,98},{3,99},{4,100},{5,101},{6,102},{7,103},{8,104... | collective-permute-start | bytes 884744 | tf_op jit(solution)/shard_map/ppermute | solution.py:37
  28.4 0.0 collective-permute-done.3.refs_3_
  28.4 1.5 %collective-permute-start.6 = (bf16[208,768]{1,0:T(8,128)(2,1)S(1)}, bf16[208,768]{1,0:T(8,128)(2,1)S(1)}, u32[]{:S(2)}, u32[]{:S(2)}) collective-permute-start(bf16[208,768]{1,0:T(8,128)(2,1)S(1)} %collective-permute-done.3.refs_3_), channel_id=1, source_target_pairs={{0,3},{1,0},{2,1},{3,2},{4,7},{5,4},{6,5},{7,6},{8,11},{9,8},{10,9... | collective-permute-start | bytes 958472 | tf_op jit(solution)/shard_map/ppermute | solution.py:37
  29.9 1.6 %collective-permute-start.11 = (bf16[192,768]{1,0:T(8,128)(2,1)S(1)}, bf16[192,768]{1,0:T(8,128)(2,1)S(1)}, u32[]{:S(2)}, u32[]{:S(2)}) collective-permute-start(bf16[192,768]{1,0:T(8,128)(2,1)S(1)} %gate.3), channel_id=1, source_target_pairs={{0,32},{1,33},{2,34},{3,35},{4,36},{5,37},{6,38},{7,39},{8,40},{9,... | collective-permute-start | bytes 884744 | tf_op jit(solution)/shard_map/ppermute | solution.py:37
  31.5 1.6 %collective-permute-done.10.refs_1_ = bf16[192,768]{1,0:T(8,128)(2,1)S(1)} collective-permute-done((bf16[192,768]{1,0:T(8,128)(2,1)S(1)}, bf16[192,768]{1,0:T(8,128)(2,1)S(1)}, u32[]{:S(2)}, u32[]{:S(2)}) %collective-permute-start.10) | collective-permute-done | bytes 294944 | tf_op jit(solution)/shard_map/ppermute | solution.py:37
  33.1 1.0 collective-permute-start.12
  34.2 2.7 %collective-permute-start.13 = (bf16[192,768]{1,0:T(8,128)(2,1)S(1)}, bf16[192,768]{1,0:T(8,128)(2,1)S(1)}, u32[]{:S(2)}, u32[]{:S(2)}) collective-permute-start(bf16[192,768]{1,0:T(8,128)(2,1)S(1)} %collective-permute-done.10.refs_1_), channel_id=1, source_target_pairs={{0,96},{1,97},{2,98},{3,99},{4,100},{5,101},{6,102},{7,103},{8,104... | collective-permute-start | bytes 884744 | tf_op jit(solution)/shard_map/ppermute | solution.py:37
  36.8 0.1 near_images.1
  37.0 0.1 first_texts.1.refs_2_.refs_0_
  37.1 0.6 copy-done.4
  37.7 4.4 %score_first.1 = (f32[1536,768]{1,0:T(8,128)S(1)}, bf16[1536,1536]{1,0:T(8,128)(2,1)S(1)}, f32[8,128]{1,0:T(8,128)S(1)}) custom-call(f32[24,128]{1,0:T(8,128)S(1)} %copy-done.4, bf16[1536,768]{1,0:T(8,128)(2,1)S(1)} %get-tuple-element.46.refs_4_.refs_1_.refs_0_, bf16[1536,768]{1,0:T(8,128)(2,1)S(1)} %first_texts.1.refs_2_.refs_0_, ...), custom_call_target="tpu_custom_call" | custom-call | flops 2717908992 | bytes 4194304 | tf_op jit(solution)/shard_map/score_first/pallas_call | solution.py:72
  42.1 2.3 %score_second.1 = (f32[1536,768]{1,0:T(8,128)S(1)}, bf16[1536,1536]{1,0:T(8,128)(2,1)S(1)}, f32[8,128]{1,0:T(8,128)S(1)}) custom-call(f32[24,128]{1,0:T(8,128)S(1)} %copy-done.4, bf16[1536,768]{1,0:T(8,128)(2,1)S(1)} %get-tuple-element.46.refs_4_.refs_1_.refs_0_, ...), custom_call_target="tpu_custom_call", output_to_operand_aliasing={{0}: (5, {}), {1}: (6, {})} | custom-call | flops 1358954496 | bytes 4194304 | tf_op jit(solution)/shard_map/score_second/pallas_call | solution.py:72
  44.5 0.3 collective-permute-start.14
  44.8 0.1 away_images.1
  44.9 6.1 %score_rest.1 = (f32[1536,768]{1,0:T(8,128)S(1)}, bf16[1536,1536]{1,0:T(8,128)(2,1)S(1)}, f32[8,128]{1,0:T(8,128)S(1)}) custom-call(f32[24,128]{1,0:T(8,128)S(1)} %copy-done.4, bf16[1536,768]{1,0:T(8,128)(2,1)S(1)} %get-tuple-element.53.refs_1_, bf16[1536,768]{1,0:T(8,128)(2,1)S(1)} %away_texts.1.refs_2_, ...), custom_call_target="tpu_custom_call", output_to_operand_aliasing={{0}: (5, {}), {1}: (6, {})} | custom-call | flops 3170893824 | bytes 4194304 | tf_op jit(solution)/shard_map/score_rest/pallas_call | solution.py:72
  51.1 10.4 %score_sib.1 = (bf16[1552,768]{1,0:T(8,128)(2,1)S(1)}, bf16[1536,1536]{1,0:T(8,128)(2,1)S(1)}, f32[8,128]{1,0:T(8,128)S(1)}) custom-call(f32[24,128]{1,0:T(8,128)S(1)} %copy-done.4, bf16[1536,768]{1,0:T(8,128)(2,1)S(1)} %get-tuple-element.53.refs_1_, bf16[1536,768]{1,0:T(8,128)(2,1)S(1)} %collective-permute-done.14.refs_2_.refs_3_, ...), custom_call_target="tpu_custom_call" | custom-call | flops 7247757312 | bytes 4194304 | tf_op jit(solution)/shard_map/score_sib/pallas_call | solution.py:72
  61.5 0.6 collective-permute-start.15
  62.1 2.0 %image_away.1 = (bf16[192,768]{1,0:T(8,128)(2,1)S(1)}, bf16[192,768]{1,0:T(8,128)(2,1)S(1)}) custom-call(bf16[1536,1536]{1,0:T(8,128)(2,1)S(1)} %get-tuple-element.70.refs_0_, bf16[1536,1536]{1,0:T(8,128)(2,1)S(1)} %get-tuple-element.71.refs_1_, bf16[1536,768]{1,0:T(8,128)(2,1)S(1)} %away_texts.1.refs_2_, ...), custom_call_target="tpu_custom_call" | custom-call | flops 905969664 | bytes 4194304 | tf_op jit(solution)/shard_map/image_away/pallas_call | solution.py:72
  64.2 0.4 collective-permute-start.21
  64.5 3.0 %collective-permute-start.22 = (bf16[192,768]{1,0:T(8,128)(2,1)S(1)}, bf16[192,768]{1,0:T(8,128)(2,1)S(1)}, u32[]{:S(2)}, u32[]{:S(2)}) collective-permute-start(bf16[192,768]{1,0:T(8,128)(2,1)S(1)} %get-tuple-element.76), channel_id=1, source_target_pairs={{0,3},{1,0},{2,1},{3,2},{4,7},{5,4},{6,5},{7,6},{8,11},{9,8},{10,9... | collective-permute-start | bytes 884744 | tf_op jit(solution)/shard_map/ppermute | solution.py:37
  67.5 0.5 add.17
  67.9 1.1 collective-permute-start.16
  69.0 2.2 %collective-permute-start.17 = (bf16[192,768]{1,0:T(8,128)(2,1)S(1)}, bf16[192,768]{1,0:T(8,128)(2,1)S(1)}, u32[]{:S(2)}, u32[]{:S(2)}) collective-permute-start(bf16[192,768]{1,0:T(8,128)(2,1)S(1)} %get-tuple-element.65), channel_id=1, source_target_pairs={{0,96},{1,97},{2,98},{3,99},{4,100},{5,101},{6,102},{7,103},{8,104... | collective-permute-start | bytes 884744 | tf_op jit(solution)/shard_map/ppermute | solution.py:37
  71.2 3.9 %image_ring.1 = (f32[384,768]{1,0:T(8,128)S(1)}, f32[384,768]{1,0:T(8,128)S(1)}) custom-call(bf16[1536,1536]{1,0:T(8,128)(2,1)S(1)} %get-tuple-element.70.refs_0_, bf16[1536,1536]{1,0:T(8,128)(2,1)S(1)} %get-tuple-element.71.refs_1_, bf16[1536,768]{1,0:T(8,128)(2,1)S(1)} %away_texts.1.refs_2_, bf16[1536,768]{1,0:T(8,128)(2,1)S(1)} %collective-permute-done.14.refs_2_.refs_3_), custom_call_target="tpu_custom_call" | custom-call | flops 1811939328 | bytes 4194304 | tf_op jit(solution)/shard_map/image_ring/pallas_call | solution.py:72
  75.1 0.2 turn.3
  75.3 0.1 collective-permute-start.23
  75.4 3.2 %collective-permute-start.24 = (bf16[384,768]{1,0:T(8,128)(2,1)S(1)}, bf16[384,768]{1,0:T(8,128)(2,1)S(1)}, u32[]{:S(2)}, u32[]{:S(2)}) collective-permute-start(bf16[384,768]{1,0:T(8,128)(2,1)S(1)} %get-tuple-element.78), channel_id=1, source_target_pairs={{0,3},{1,0},{2,1},{3,2},{4,7},{5,4},{6,5},{7,6},{8,11},{9,8},{10,9... | collective-permute-start | bytes 1769480 | tf_op jit(solution)/shard_map/ppermute | solution.py:37
  78.6 0.2 turn.2
  78.8 0.3 collective-permute-start.18
  79.2 3.0 %collective-permute-start.19 = (bf16[384,768]{1,0:T(8,128)(2,1)S(1)}, bf16[384,768]{1,0:T(8,128)(2,1)S(1)}, u32[]{:S(2)}, u32[]{:S(2)}) collective-permute-start(bf16[384,768]{1,0:T(8,128)(2,1)S(1)} %get-tuple-element.68), channel_id=1, source_target_pairs={{0,96},{1,97},{2,98},{3,99},{4,100},{5,101},{6,102},{7,103},{8,104... | collective-permute-start | bytes 1769480 | tf_op jit(solution)/shard_map/ppermute | solution.py:37
  82.1 3.6 %collective-permute-done.25 = f32[8,128]{1,0:T(8,128)S(1)} collective-permute-done((f32[8,128]{1,0:T(8,128)S(1)}, f32[8,128]{1,0:T(8,128)S(1)}, u32[]{:S(2)}, u32[]{:S(2)}) %collective-permute-start.25) | collective-permute-done | bytes 4128 | tf_op jit(solution)/shard_map/ppermute | solution.py:37
  85.7 2.7 %collective-permute-start.26 = (f32[8,128]{1,0:T(8,128)S(1)}, f32[8,128]{1,0:T(8,128)S(1)}, u32[]{:S(2)}, u32[]{:S(2)}) collective-permute-start(f32[8,128]{1,0:T(8,128)S(1)} %add.13), channel_id=1, source_target_pairs={{0,20},{1,21},{2,22},{3,23},{4,16},{5,17},{6,18},{7,19},{8,28},{9,... | collective-permute-start | bytes 12296 | tf_op jit(solution)/shard_map/ppermute | solution.py:37
  88.4 2.1 %collective-permute-done.26 = f32[8,128]{1,0:T(8,128)S(1)} collective-permute-done((f32[8,128]{1,0:T(8,128)S(1)}, f32[8,128]{1,0:T(8,128)S(1)}, u32[]{:S(2)}, u32[]{:S(2)}) %collective-permute-start.26) | collective-permute-done | bytes 4128 | tf_op jit(solution)/shard_map/ppermute | solution.py:37
  90.6 2.0 %image_near.1 = (f32[192,768]{1,0:T(8,128)S(1)}, f32[192,768]{1,0:T(8,128)S(1)}) custom-call(bf16[1536,1536]{1,0:T(8,128)(2,1)S(1)} %get-tuple-element.70.refs_0_, bf16[1536,1536]{1,0:T(8,128)(2,1)S(1)} %get-tuple-element.71.refs_1_, bf16[1536,768]{1,0:T(8,128)(2,1)S(1)} %away_texts.1.refs_2_, bf16[1536,768]{1,0:T(8,128)(2,1)S(1)} %collective-permute-done.14.refs_2_.refs_3_), custom_call_target="tpu_custom_call" | custom-call | flops 905969664 | bytes 4194304 | tf_op jit(solution)/shard_map/image_near/pallas_call | solution.py:72
  92.6 0.0 copy-start
  92.6 1.5 %collective-permute-done.27.refs_4_ = f32[8,128]{1,0:T(8,128)S(1)} collective-permute-done((f32[8,128]{1,0:T(8,128)S(1)}, f32[8,128]{1,0:T(8,128)S(1)}, u32[]{:S(2)}, u32[]{:S(2)}) %collective-permute-start.27) | collective-permute-done | bytes 4128 | tf_op jit(solution)/shard_map/ppermute | solution.py:37
  94.2 0.1 far.3
  94.3 0.1 collective-permute-start.31
  94.4 0.0 copy-start.1
  94.4 0.1 far.2
  94.5 2.8 %collective-permute-start.20 = (bf16[192,768]{1,0:T(8,128)(2,1)S(1)}, bf16[192,768]{1,0:T(8,128)(2,1)S(1)}, u32[]{:S(2)}, u32[]{:S(2)}) collective-permute-start(bf16[192,768]{1,0:T(8,128)(2,1)S(1)} %far.2), channel_id=1, source_target_pairs={{0,20},{1,21},{2,22},{3,23},{4,16},{5,17},{6,18},{7,19},{8,28},{9,... | collective-permute-start | bytes 884744 | tf_op jit(solution)/shard_map/ppermute | solution.py:37
  97.3 1.0 collective-permute-start.28
  98.3 4.1 %collective-permute-done.28 = f32[8,128]{1,0:T(8,128)S(1)} collective-permute-done((f32[8,128]{1,0:T(8,128)S(1)}, f32[8,128]{1,0:T(8,128)S(1)}, u32[]{:S(2)}, u32[]{:S(2)}) %collective-permute-start.28) | collective-permute-done | bytes 4128 | tf_op jit(solution)/shard_map/ppermute | solution.py:37
  102.4 3.6 %collective-permute-done.29 = f32[8,128]{1,0:T(8,128)S(1)} collective-permute-done((f32[8,128]{1,0:T(8,128)S(1)}, f32[8,128]{1,0:T(8,128)S(1)}, u32[]{:S(2)}, u32[]{:S(2)}) %collective-permute-start.29) | collective-permute-done | bytes 4128 | tf_op jit(solution)/shard_map/ppermute | solution.py:37
  106.0 1.7 %collective-permute-start.30 = (f32[8,128]{1,0:T(8,128)S(1)}, f32[8,128]{1,0:T(8,128)S(1)}, u32[]{:S(2)}, u32[]{:S(2)}) collective-permute-start(f32[8,128]{1,0:T(8,128)S(1)} %add.16.refs_5_), channel_id=1, source_target_pairs={{0,64},{1,65},{2,66},{3,67},{4,68},{5,69},{6,70},{7,71},{8,72},{9,... | collective-permute-start | bytes 12296 | tf_op jit(solution)/shard_map/ppermute | solution.py:37
  107.7 1.1 %unproject.3 = f32[192,768]{1,0:T(8,128)} custom-call(bf16[192,768]{1,0:T(8,128)(2,1)S(1)} %copy-done, f32[192,768]{1,0:T(8,128)S(1)} %get-tuple-element.82.refs_1_, bf16[384,768]{1,0:T(8,128)(2,1)S(1)} %collective-permute-done.23.refs_1_.refs_2_, bf16[384,768]{1,0:T(8,128)(2,1)S(1)} %collective-permute-done.24.refs_2_.refs_3_, ...), custom_call_target="tpu_custom_call" | custom-call | bytes 4194304 | tf_op jit(solution)/shard_map/unproject/pallas_call | solution.py:72
  108.8 2.3 %collective-permute-done.30.refs_6_ = f32[8,128]{1,0:T(8,128)S(1)} collective-permute-done((f32[8,128]{1,0:T(8,128)S(1)}, f32[8,128]{1,0:T(8,128)S(1)}, u32[]{:S(2)}, u32[]{:S(2)}) %collective-permute-start.30) | collective-permute-done | bytes 4128 | tf_op jit(solution)/shard_map/ppermute | solution.py:37
  111.1 1.1 %unproject.2 = (f32[192,768]{1,0:T(8,128)}, f32[8,128]{1,0:T(8,128)S(1)}) custom-call(bf16[192,768]{1,0:T(8,128)(2,1)S(1)} %copy-done.1, f32[192,768]{1,0:T(8,128)S(1)} %get-tuple-element.61.refs_1_, bf16[384,768]{1,0:T(8,128)(2,1)S(1)} %collective-permute-done.18.refs_1_.refs_2_, bf16[384,768]{1,0:T(8,128)(2,1)S(1)} %collective-permute-done.19.refs_2_.refs_3_, ...), custom_call_target="tpu_custom_call" | custom-call | bytes 4194304 | tf_op jit(solution)/shard_map/unproject/pallas_call | solution.py:72
  112.2 0.5 slice.3
  (37 shorter events, 0.2 us)
Async XLA Ops:
  4.0 32.8 %copy-start.2 = (bf16[208,768]{1,0:T(8,128)(2,1)S(1)}, bf16[208,768]{1,0:T(8,128)(2,1)}, u32[]{:S(2)}) copy-start(bf16[208,768]{1,0:T(8,128)(2,1)} %get-tuple-element.45.refs_0_) | copy-start | bytes 958468
  4.0 33.0 %copy-start.3 = (bf16[192,768]{1,0:T(8,128)(2,1)S(1)}, bf16[192,768]{1,0:T(8,128)(2,1)}, u32[]{:S(2)}) copy-start(bf16[192,768]{1,0:T(8,128)(2,1)} %get-tuple-element.48.refs_0_) | copy-start | bytes 884740
  4.0 10.7 %collective-permute-start.2 = (bf16[208,768]{1,0:T(8,128)(2,1)}, bf16[208,768]{1,0:T(8,128)(2,1)S(1)}, u32[]{:S(2)}, u32[]{:S(2)}) collective-permute-start(bf16[208,768]{1,0:T(8,128)(2,1)} %get-tuple-element.45.refs_0_), channel_id=1, source_target_pairs={{0,1},{1,2},{2,3},{3,0},{4,5},{5,6},{6,7},{7,4},{8,9},{9,10},{10,1... | collective-permute-start | bytes 958472 | tf_op jit(solution)/shard_map/ppermute | solution.py:37
  5.7 13.2 %collective-permute-start.1 = (bf16[208,768]{1,0:T(8,128)(2,1)}, bf16[208,768]{1,0:T(8,128)(2,1)S(1)}, u32[]{:S(2)}, u32[]{:S(2)}) collective-permute-start(bf16[208,768]{1,0:T(8,128)(2,1)} %get-tuple-element.45.refs_0_), channel_id=1, source_target_pairs={{0,3},{1,0},{2,1},{3,2},{4,7},{5,4},{6,5},{7,6},{8,11},{9,8},{10,9... | collective-permute-start | bytes 958472 | tf_op jit(solution)/shard_map/ppermute | solution.py:37
  7.3 11.6 %collective-permute-start = (bf16[208,768]{1,0:T(8,128)(2,1)}, bf16[208,768]{1,0:T(8,128)(2,1)S(1)}, u32[]{:S(2)}, u32[]{:S(2)}) collective-permute-start(bf16[208,768]{1,0:T(8,128)(2,1)} %get-tuple-element.45.refs_0_), channel_id=1, source_target_pairs={{0,16},{1,17},{2,18},{3,19},{4,20},{5,21},{6,22},{7,23},{8,24},{9,... | collective-permute-start | bytes 958472 | tf_op jit(solution)/shard_map/ppermute | solution.py:37
  9.3 11.7 %collective-permute-start.9 = (bf16[192,768]{1,0:T(8,128)(2,1)}, bf16[192,768]{1,0:T(8,128)(2,1)S(1)}, u32[]{:S(2)}, u32[]{:S(2)}) collective-permute-start(bf16[192,768]{1,0:T(8,128)(2,1)} %get-tuple-element.48.refs_0_), channel_id=1, source_target_pairs={{0,32},{1,33},{2,34},{3,35},{4,36},{5,37},{6,38},{7,39},{8,40},{9,... | collective-permute-start | bytes 884744 | tf_op jit(solution)/shard_map/ppermute | solution.py:37
  10.9 10.4 %collective-permute-start.8 = (bf16[192,768]{1,0:T(8,128)(2,1)}, bf16[192,768]{1,0:T(8,128)(2,1)S(1)}, u32[]{:S(2)}, u32[]{:S(2)}) collective-permute-start(bf16[192,768]{1,0:T(8,128)(2,1)} %get-tuple-element.48.refs_0_), channel_id=1, source_target_pairs={{0,96},{1,97},{2,98},{3,99},{4,100},{5,101},{6,102},{7,103},{8,104... | collective-permute-start | bytes 884744 | tf_op jit(solution)/shard_map/ppermute | solution.py:37
  14.7 10.6 %collective-permute-start.7 = (bf16[192,768]{1,0:T(8,128)(2,1)}, bf16[192,768]{1,0:T(8,128)(2,1)S(1)}, u32[]{:S(2)}, u32[]{:S(2)}) collective-permute-start(bf16[192,768]{1,0:T(8,128)(2,1)} %get-tuple-element.48.refs_0_), channel_id=1, source_target_pairs={{0,20},{1,21},{2,22},{3,23},{4,16},{5,17},{6,18},{7,19},{8,28},{9,... | collective-permute-start | bytes 884744 | tf_op jit(solution)/shard_map/ppermute | solution.py:37
  18.9 9.4 %collective-permute-start.3 = (bf16[208,768]{1,0:T(8,128)(2,1)S(1)}, bf16[208,768]{1,0:T(8,128)(2,1)S(1)}, u32[]{:S(2)}, u32[]{:S(2)}) collective-permute-start(bf16[208,768]{1,0:T(8,128)(2,1)S(1)} %gate.2.refs_3_), channel_id=1, source_target_pairs={{0,3},{1,0},{2,1},{3,2},{4,7},{5,4},{6,5},{7,6},{8,11},{9,8},{10,9... | collective-permute-start | bytes 958472 | tf_op jit(solution)/shard_map/ppermute | solution.py:37
  20.6 13.6 %collective-permute-start.4 = (bf16[208,768]{1,0:T(8,128)(2,1)S(1)}, bf16[208,768]{1,0:T(8,128)(2,1)S(1)}, u32[]{:S(2)}, u32[]{:S(2)}) collective-permute-start(bf16[208,768]{1,0:T(8,128)(2,1)S(1)} %gate.2.refs_3_), channel_id=1, source_target_pairs={{0,1},{1,2},{2,3},{3,0},{4,5},{5,6},{6,7},{7,4},{8,9},{9,10},{10,1... | collective-permute-start | bytes 958472 | tf_op jit(solution)/shard_map/ppermute | solution.py:37
  21.0 15.9 %collective-permute-start.5 = (bf16[208,768]{1,0:T(8,128)(2,1)S(1)}, bf16[208,768]{1,0:T(8,128)(2,1)S(1)}, u32[]{:S(2)}, u32[]{:S(2)}) collective-permute-start(bf16[208,768]{1,0:T(8,128)(2,1)S(1)} %collective-permute-done.2.refs_2_.refs_4_), channel_id=1, source_target_pairs={{0,1},{1,2},{2,3},{3,0},{4,5},{5,6},{6,7},{7,4},{8,9},{9,10},{10,1... | collective-permute-start | bytes 958472 | tf_op jit(solution)/shard_map/ppermute | solution.py:37
  25.3 7.8 %collective-permute-start.10 = (bf16[192,768]{1,0:T(8,128)(2,1)S(1)}, bf16[192,768]{1,0:T(8,128)(2,1)S(1)}, u32[]{:S(2)}, u32[]{:S(2)}) collective-permute-start(bf16[192,768]{1,0:T(8,128)(2,1)S(1)} %gate.3), channel_id=1, source_target_pairs={{0,96},{1,97},{2,98},{3,99},{4,100},{5,101},{6,102},{7,103},{8,104... | collective-permute-start | bytes 884744 | tf_op jit(solution)/shard_map/ppermute | solution.py:37
  28.4 13.7 %collective-permute-start.6 = (bf16[208,768]{1,0:T(8,128)(2,1)S(1)}, bf16[208,768]{1,0:T(8,128)(2,1)S(1)}, u32[]{:S(2)}, u32[]{:S(2)}) collective-permute-start(bf16[208,768]{1,0:T(8,128)(2,1)S(1)} %collective-permute-done.3.refs_3_), channel_id=1, source_target_pairs={{0,3},{1,0},{2,1},{3,2},{4,7},{5,4},{6,5},{7,6},{8,11},{9,8},{10,9... | collective-permute-start | bytes 958472 | tf_op jit(solution)/shard_map/ppermute | solution.py:37
  29.9 12.1 %collective-permute-start.11 = (bf16[192,768]{1,0:T(8,128)(2,1)S(1)}, bf16[192,768]{1,0:T(8,128)(2,1)S(1)}, u32[]{:S(2)}, u32[]{:S(2)}) collective-permute-start(bf16[192,768]{1,0:T(8,128)(2,1)S(1)} %gate.3), channel_id=1, source_target_pairs={{0,32},{1,33},{2,34},{3,35},{4,36},{5,37},{6,38},{7,39},{8,40},{9,... | collective-permute-start | bytes 884744 | tf_op jit(solution)/shard_map/ppermute | solution.py:37
  33.1 11.4 %collective-permute-start.12 = (bf16[192,768]{1,0:T(8,128)(2,1)S(1)}, bf16[192,768]{1,0:T(8,128)(2,1)S(1)}, u32[]{:S(2)}, u32[]{:S(2)}) collective-permute-start(bf16[192,768]{1,0:T(8,128)(2,1)S(1)} %collective-permute-done.9.refs_3_.refs_2_), channel_id=1, source_target_pairs={{0,32},{1,33},{2,34},{3,35},{4,36},{5,37},{6,38},{7,39},{8,40},{9,... | collective-permute-start | bytes 884744 | tf_op jit(solution)/shard_map/ppermute | solution.py:37
  34.2 10.3 %collective-permute-start.13 = (bf16[192,768]{1,0:T(8,128)(2,1)S(1)}, bf16[192,768]{1,0:T(8,128)(2,1)S(1)}, u32[]{:S(2)}, u32[]{:S(2)}) collective-permute-start(bf16[192,768]{1,0:T(8,128)(2,1)S(1)} %collective-permute-done.10.refs_1_), channel_id=1, source_target_pairs={{0,96},{1,97},{2,98},{3,99},{4,100},{5,101},{6,102},{7,103},{8,104... | collective-permute-start | bytes 884744 | tf_op jit(solution)/shard_map/ppermute | solution.py:37
  37.0 0.7 copy-start.4
  44.5 6.5 %collective-permute-start.14 = (bf16[1536,768]{1,0:T(8,128)(2,1)S(1)}, bf16[1536,768]{1,0:T(8,128)(2,1)S(1)}, u32[]{:S(2)}, u32[]{:S(2)}) collective-permute-start(bf16[1536,768]{1,0:T(8,128)(2,1)S(1)} %away_texts.1.refs_2_), channel_id=1, source_target_pairs={{0,8},{1,9},{2,10},{3,11},{4,12},{5,13},{6,14},{7,15},{8,0},{9,1},... | collective-permute-start | bytes 7077896 | tf_op jit(solution)/shard_map/ppermute | solution.py:37
  61.5 5.9 %collective-permute-start.15 = (bf16[1552,768]{1,0:T(8,128)(2,1)S(1)}, bf16[1552,768]{1,0:T(8,128)(2,1)S(1)}, u32[]{:S(2)}, u32[]{:S(2)}) collective-permute-start(bf16[1552,768]{1,0:T(8,128)(2,1)S(1)} %get-tuple-element.59), channel_id=1, source_target_pairs={{0,8},{1,9},{2,10},{3,11},{4,12},{5,13},{6,14},{7,15},{8,0},{9,1},... | collective-permute-start | bytes 7151624 | tf_op jit(solution)/shard_map/ppermute | solution.py:37
  64.2 11.0 %collective-permute-start.21 = (bf16[192,768]{1,0:T(8,128)(2,1)S(1)}, bf16[192,768]{1,0:T(8,128)(2,1)S(1)}, u32[]{:S(2)}, u32[]{:S(2)}) collective-permute-start(bf16[192,768]{1,0:T(8,128)(2,1)S(1)} %get-tuple-element.75), channel_id=1, source_target_pairs={{0,1},{1,2},{2,3},{3,0},{4,5},{5,6},{6,7},{7,4},{8,9},{9,10},{10,1... | collective-permute-start | bytes 884744 | tf_op jit(solution)/shard_map/ppermute | solution.py:37
  64.5 10.6 %collective-permute-start.22 = (bf16[192,768]{1,0:T(8,128)(2,1)S(1)}, bf16[192,768]{1,0:T(8,128)(2,1)S(1)}, u32[]{:S(2)}, u32[]{:S(2)}) collective-permute-start(bf16[192,768]{1,0:T(8,128)(2,1)S(1)} %get-tuple-element.76), channel_id=1, source_target_pairs={{0,3},{1,0},{2,1},{3,2},{4,7},{5,4},{6,5},{7,6},{8,11},{9,8},{10,9... | collective-permute-start | bytes 884744 | tf_op jit(solution)/shard_map/ppermute | solution.py:37
  67.9 10.7 %collective-permute-start.16 = (bf16[192,768]{1,0:T(8,128)(2,1)S(1)}, bf16[192,768]{1,0:T(8,128)(2,1)S(1)}, u32[]{:S(2)}, u32[]{:S(2)}) collective-permute-start(bf16[192,768]{1,0:T(8,128)(2,1)S(1)} %get-tuple-element.64), channel_id=1, source_target_pairs={{0,32},{1,33},{2,34},{3,35},{4,36},{5,37},{6,38},{7,39},{8,40},{9,... | collective-permute-start | bytes 884744 | tf_op jit(solution)/shard_map/ppermute | solution.py:37
  69.0 9.6 %collective-permute-start.17 = (bf16[192,768]{1,0:T(8,128)(2,1)S(1)}, bf16[192,768]{1,0:T(8,128)(2,1)S(1)}, u32[]{:S(2)}, u32[]{:S(2)}) collective-permute-start(bf16[192,768]{1,0:T(8,128)(2,1)S(1)} %get-tuple-element.65), channel_id=1, source_target_pairs={{0,96},{1,97},{2,98},{3,99},{4,100},{5,101},{6,102},{7,103},{8,104... | collective-permute-start | bytes 884744 | tf_op jit(solution)/shard_map/ppermute | solution.py:37
  75.3 17.3 %collective-permute-start.23 = (bf16[384,768]{1,0:T(8,128)(2,1)S(1)}, bf16[384,768]{1,0:T(8,128)(2,1)S(1)}, u32[]{:S(2)}, u32[]{:S(2)}) collective-permute-start(bf16[384,768]{1,0:T(8,128)(2,1)S(1)} %get-tuple-element.77), channel_id=1, source_target_pairs={{0,1},{1,2},{2,3},{3,0},{4,5},{5,6},{6,7},{7,4},{8,9},{9,10},{10,1... | collective-permute-start | bytes 1769480 | tf_op jit(solution)/shard_map/ppermute | solution.py:37
  75.4 17.3 %collective-permute-start.24 = (bf16[384,768]{1,0:T(8,128)(2,1)S(1)}, bf16[384,768]{1,0:T(8,128)(2,1)S(1)}, u32[]{:S(2)}, u32[]{:S(2)}) collective-permute-start(bf16[384,768]{1,0:T(8,128)(2,1)S(1)} %get-tuple-element.78), channel_id=1, source_target_pairs={{0,3},{1,0},{2,1},{3,2},{4,7},{5,4},{6,5},{7,6},{8,11},{9,8},{10,9... | collective-permute-start | bytes 1769480 | tf_op jit(solution)/shard_map/ppermute | solution.py:37
  78.8 15.5 %collective-permute-start.18 = (bf16[384,768]{1,0:T(8,128)(2,1)S(1)}, bf16[384,768]{1,0:T(8,128)(2,1)S(1)}, u32[]{:S(2)}, u32[]{:S(2)}) collective-permute-start(bf16[384,768]{1,0:T(8,128)(2,1)S(1)} %get-tuple-element.67), channel_id=1, source_target_pairs={{0,32},{1,33},{2,34},{3,35},{4,36},{5,37},{6,38},{7,39},{8,40},{9,... | collective-permute-start | bytes 1769480 | tf_op jit(solution)/shard_map/ppermute | solution.py:37
  79.2 15.2 %collective-permute-start.19 = (bf16[384,768]{1,0:T(8,128)(2,1)S(1)}, bf16[384,768]{1,0:T(8,128)(2,1)S(1)}, u32[]{:S(2)}, u32[]{:S(2)}) collective-permute-start(bf16[384,768]{1,0:T(8,128)(2,1)S(1)} %get-tuple-element.68), channel_id=1, source_target_pairs={{0,96},{1,97},{2,98},{3,99},{4,100},{5,101},{6,102},{7,103},{8,104... | collective-permute-start | bytes 1769480 | tf_op jit(solution)/shard_map/ppermute | solution.py:37
  82.1 3.6 %collective-permute-start.25 = (f32[8,128]{1,0:T(8,128)S(1)}, f32[8,128]{1,0:T(8,128)S(1)}, u32[]{:S(2)}, u32[]{:S(2)}) collective-permute-start(f32[8,128]{1,0:T(8,128)S(1)} %get-tuple-element.79), channel_id=1, source_target_pairs={{0,16},{1,17},{2,18},{3,19},{4,20},{5,21},{6,22},{7,23},{8,24},{9,... | collective-permute-start | bytes 12296 | tf_op jit(solution)/shard_map/ppermute | solution.py:37
  85.7 4.8 %collective-permute-start.26 = (f32[8,128]{1,0:T(8,128)S(1)}, f32[8,128]{1,0:T(8,128)S(1)}, u32[]{:S(2)}, u32[]{:S(2)}) collective-permute-start(f32[8,128]{1,0:T(8,128)S(1)} %add.13), channel_id=1, source_target_pairs={{0,20},{1,21},{2,22},{3,23},{4,16},{5,17},{6,18},{7,19},{8,28},{9,... | collective-permute-start | bytes 12296 | tf_op jit(solution)/shard_map/ppermute | solution.py:37
  90.6 3.6 %collective-permute-start.27 = (f32[8,128]{1,0:T(8,128)S(1)}, f32[8,128]{1,0:T(8,128)S(1)}, u32[]{:S(2)}, u32[]{:S(2)}) collective-permute-start(f32[8,128]{1,0:T(8,128)S(1)} %add.14.refs_3_), channel_id=1, source_target_pairs={{0,1},{1,0},{2,3},{3,2},{4,5},{5,4},{6,7},{7,6},{8,9},{9,8},{10,11... | collective-permute-start | bytes 12296 | tf_op jit(solution)/shard_map/ppermute | solution.py:37
  92.6 15.1 %copy-start = (bf16[192,768]{1,0:T(8,128)(2,1)S(1)}, bf16[192,768]{1,0:T(8,128)(2,1)}, u32[]{:S(2)}) copy-start(bf16[192,768]{1,0:T(8,128)(2,1)} %refs_0_.3) | copy-start | bytes 884740
  94.3 13.4 %collective-permute-start.31 = (bf16[192,768]{1,0:T(8,128)(2,1)S(1)}, bf16[192,768]{1,0:T(8,128)(2,1)S(1)}, u32[]{:S(2)}, u32[]{:S(2)}) collective-permute-start(bf16[192,768]{1,0:T(8,128)(2,1)S(1)} %get-tuple-element.83), channel_id=1, source_target_pairs={{0,16},{1,17},{2,18},{3,19},{4,20},{5,21},{6,22},{7,23},{8,24},{9,... | collective-permute-start | bytes 884744 | tf_op jit(solution)/shard_map/ppermute | solution.py:37
  94.4 16.7 %copy-start.1 = (bf16[192,768]{1,0:T(8,128)(2,1)S(1)}, bf16[192,768]{1,0:T(8,128)(2,1)}, u32[]{:S(2)}) copy-start(bf16[192,768]{1,0:T(8,128)(2,1)} %refs_0_.2) | copy-start | bytes 884740
  94.5 16.6 %collective-permute-start.20 = (bf16[192,768]{1,0:T(8,128)(2,1)S(1)}, bf16[192,768]{1,0:T(8,128)(2,1)S(1)}, u32[]{:S(2)}, u32[]{:S(2)}) collective-permute-start(bf16[192,768]{1,0:T(8,128)(2,1)S(1)} %far.2), channel_id=1, source_target_pairs={{0,20},{1,21},{2,22},{3,23},{4,16},{5,17},{6,18},{7,19},{8,28},{9,... | collective-permute-start | bytes 884744 | tf_op jit(solution)/shard_map/ppermute | solution.py:37
  97.3 5.1 %collective-permute-start.28 = (f32[8,128]{1,0:T(8,128)S(1)}, f32[8,128]{1,0:T(8,128)S(1)}, u32[]{:S(2)}, u32[]{:S(2)}) collective-permute-start(f32[8,128]{1,0:T(8,128)S(1)} %get-tuple-element.80), channel_id=1, source_target_pairs={{0,2},{1,3},{2,0},{3,1},{4,6},{5,7},{6,4},{7,5},{8,10},{9,11},{10,... | collective-permute-start | bytes 12296 | tf_op jit(solution)/shard_map/ppermute | solution.py:37
  102.4 3.6 %collective-permute-start.29 = (f32[8,128]{1,0:T(8,128)S(1)}, f32[8,128]{1,0:T(8,128)S(1)}, u32[]{:S(2)}, u32[]{:S(2)}) collective-permute-start(f32[8,128]{1,0:T(8,128)S(1)} %add.15), channel_id=1, source_target_pairs={{0,32},{1,33},{2,34},{3,35},{4,36},{5,37},{6,38},{7,39},{8,40},{9,... | collective-permute-start | bytes 12296 | tf_op jit(solution)/shard_map/ppermute | solution.py:37
  106.0 5.1 %collective-permute-start.30 = (f32[8,128]{1,0:T(8,128)S(1)}, f32[8,128]{1,0:T(8,128)S(1)}, u32[]{:S(2)}, u32[]{:S(2)}) collective-permute-start(f32[8,128]{1,0:T(8,128)S(1)} %add.16.refs_5_), channel_id=1, source_target_pairs={{0,64},{1,65},{2,66},{3,67},{4,68},{5,69},{6,70},{7,71},{8,72},{9,... | collective-permute-start | bytes 12296 | tf_op jit(solution)/shard_map/ppermute | solution.py:37

commit v4 on v3

--- a/solution.py
+++ b/solution.py
@@ -206,11 +206,20 @@
     lax.fori_loop(0, NY // FIRST, step, 0)
     loss = loss_in[...] + jnp.sum(loss_acc[...])
     loss_ref[...] = loss
-    gy_out[NY:, :] = jnp.zeros((16, D), jnp.bfloat16)
+    write_loss(loss, gy_out, NY)
+
+
+def write_loss(loss, ref, row):
+    ref[row:, :] = jnp.zeros((16, D), BF16)
     for i in range(3):
-        part = loss.astype(jnp.bfloat16)
-        gy_out[NY:, i * 128 : i * 128 + 128] = jnp.concatenate([part, part], axis=0)
-        loss = loss - part.astype(jnp.float32)
+        part = loss.astype(BF16)
+        ref[row:, i * 128 : i * 128 + 128] = jnp.concatenate([part, part], axis=0)
+        loss = loss - part.astype(F32)
+
+
+def read_loss(ref, row):
+    parts = [ref[row:, i * 128 : i * 128 + 128].astype(F32) for i in range(3)]
+    return (parts[0] + parts[1] + parts[2])[:8, :]
 
 
 def image_kernel(slots, w_own, w_sib, y_own, y_sib, *outs):
@@ -234,23 +243,24 @@
     own[...], zed[...] = part(0), part(1)
     plus[:R, :], plus[R:, :] = part(2), part(4)
     minus[:R, :], minus[R:, :] = part(3), part(5)
-    two[...], two_z[...] = part(6).astype(BF16), part(7).astype(BF16)
-    total = loss[...]
-    for i in range(3):
-        total = total + sibling[NY : NY + 8, i * 128 : i * 128 + 128].astype(jnp.float32)
+    total = loss[...] + read_loss(sibling, NY)
+    for slot, ref in ((6, two), (7, two_z)):
+        ref[:R, :] = part(slot).astype(BF16)
+        write_loss(total, ref, R)
     loss_out[...] = total
 
 
 def turn_kernel(plus, minus, two, two_z, plus_out, minus_out):
-    plus_out[:R, :] = (plus[:R, :] + two[...].astype(F32)).astype(BF16)
+    plus_out[:R, :] = (plus[:R, :] + two[:R, :].astype(F32)).astype(BF16)
     plus_out[R:, :] = plus[R:, :].astype(BF16)
     minus_out[:R, :] = minus[:R, :].astype(BF16)
-    minus_out[R:, :] = (minus[R:, :] + two_z[...].astype(F32)).astype(BF16)
+    minus_out[R:, :] = (minus[R:, :] + two_z[:R, :].astype(F32)).astype(BF16)
 
 
 def turn_loss_kernel(plus, minus, two, two_z, loss, plus_out, minus_out, loss_out):
     turn_kernel(plus, minus, two, two_z, plus_out, minus_out)
-    loss_out[...] = loss[...]
+    odd = (lax.axis_index("row") >> 2) & 1
+    loss_out[...] = loss[...] + jnp.where(odd == 1, read_loss(two, R), read_loss(two_z, R))
 
 
 def far_kernel(own, plus, minus, out):
@@ -271,15 +281,17 @@
 
 def final_loss_kernel(values_ref, own_ref, plus, minus, zed, loss, step, out_ref, loss_out):
     final_kernel(values_ref, own_ref, plus, minus, zed, out_ref)
-    loss_out[...] = (loss[...] + step[...]) * (1.0 / (LOG2E * R * N_ROW * N_COL))
-
-
-def turn(near, away, shift, *loss):
+    loss_out[0] = (loss[0, 0] + step[0, 0]) * (1.0 / (LOG2E * R * N_ROW * N_COL))
+
+
+def turn(near, away, shift, loss=(), after=(), flops=0):
     two, two_z = shift(away[0], 1), shift(away[1], -1)
     outs = [((2 * R, D), BF16)] * 2
     if loss:
-        return call(turn_loss_kernel, outs + [LOSS], near[2], near[3], two, two_z, *loss, name="turn", vmem=8)
-    return call(turn_kernel, outs, near[2], near[3], two, two_z, name="turn", vmem=8)
+        return call(
+            turn_loss_kernel, outs + [LOSS], near[2], near[3], two, two_z, *loss, name="turn", vmem=8, after=after
+        )
+    return call(turn_kernel, outs, near[2], near[3], two, two_z, name="turn", vmem=8, flops=flops)
 
 
 def far(near, plus, minus, swap, *loss):
@@ -359,7 +371,7 @@
     gy_core = send_core(gy_sib)
     weights = (w_own, w_sib, y_all, s_all)
     gx_away = call(functools.partial(image_kernel, (6,)), AWAY, *weights, name="image_away", flops=flops // 8, vmem=16)
-    *gy, loss = call(add_kernel, PARTS + AWAY + [LOSS], gy_own, gy_core, loss, name="add", vmem=16)
+    *gy, loss = call(add_kernel, PARTS + [((R + 16, D), BF16)] * 2 + [LOSS], gy_own, gy_core, loss, after=gx_away, name="add", vmem=16)
     gy_near, gy_away = gy[:4], gy[4:]
 
     gx_ring = call(
@@ -369,8 +381,8 @@
         functools.partial(image_kernel, (0,)), PARTS[:2], *weights, name="image_near", flops=flops // 8, vmem=16
     )
     gx_near = gx_near + gx_ring
-    gx_plus, gx_minus = turn(gx_near, gx_away, send_x)
-    gy_plus, gy_minus, loss = turn(gy_near, gy_away, send_y, loss)
+    gx_plus, gx_minus = turn(gx_near, gx_away, send_x, flops=flops // 4)
+    gy_plus, gy_minus, loss = turn(gy_near, gy_away, send_y, (loss,), after=(gx_plus,))
     gx_plus, gx_minus = send_x(gx_plus, 1), send_x(gx_minus, -1)
     gy_plus, gy_minus = send_y(gy_plus, 1), send_y(gy_minus, -1)
 
@@ -380,15 +392,19 @@
     gx_far, loss = far(gx_near, gx_plus, gx_minus, swap_image_z, loss, step)
     gy_far = far(gy_near, gy_plus, gy_minus, swap_text_z)
     loss = loss + send(loss, lambda y, zl, k, zh, x: (y, zl, k, zh, x ^ 2))
-    loss = loss + send(loss, lambda y, zl, k, zh, x: (y ^ 1, zl, k, zh, x))
     step = send(loss, lambda y, zl, k, zh, x: (y ^ 2, zl, k, zh, x))
 
     grad = ((R, D), F32)
     grad_x = call(final_kernel, [grad], images, gx_near[0], gx_plus, gx_minus, gx_far, name="unproject")[0]
-    grad_y, loss = call(
-        final_loss_kernel, [grad, LOSS], texts, gy_near[0], gy_plus, gy_minus, gy_far, loss, step, name="unproject"
-    )
-    return loss[0, :1], grad_x, grad_y
+    grad_y, loss = pl.pallas_call(
+        final_loss_kernel,
+        in_specs=[VMEM] * 7,
+        out_specs=[VMEM, SMEM],
+        out_shape=[jax.ShapeDtypeStruct((R, D), F32), jax.ShapeDtypeStruct((1,), F32)],
+        compiler_params=pltpu.CompilerParams(vmem_limit_bytes=8 << 20),
+        name="unproject",
+    )(texts, gy_near[0], gy_plus, gy_minus, gy_far, loss, step)
+    return loss, grad_x, grad_y
 
 
 def solution(mesh):

time: 113 us -> 109 us (0.965)
  waiting for transfers between devices: 25 us -> 20.1 us
    ppermute x32 -> x31, waiting for transfers between devices: 25 us -> 20.1 us  [send(): return lax.ppermute(value, ('row', 'col'), pairs)]
    pallas_call x0 -> x1, Pallas kernels: none -> 1.14 us  [local(): pl.pallas_call(final_loss_kernel, in_specs=[VMEM] * 7, out_specs=[VMEM, S...]
    pallas_call x21 -> x20, Pallas kernels: 35 us -> 34 us  [call(): pl.pallas_call(body, in_specs=[SMEM] * scalars + [VMEM] * (count - scalar...]
    ppermute x32 -> x31, starting transfers between devices: 47.3 us -> 48.1 us  [send(): return lax.ppermute(value, ('row', 'col'), pairs)]
  transfers between devices with their start and end apart: 32 -> 31, of which waited for: 9 -> 10; matrix products, arithmetic and copies ran while one was open for 0% -> 0% of each run, Pallas kernels for 21% -> 22%
where the time goes in v4:
time: 109 us; the launch traced here: 108 us
  starting transfers between devices  48.1 us (44%)
  Pallas kernels  37.2 us (34%)
  waiting for transfers between devices  20.1 us (18%)
  between operations  2.39 us (2%)
    ppermute x31, starting transfers between devices, send(): return lax.ppermute(value, ('row', 'col'), pairs)  48.1 us
    pallas_call x20, Pallas kernels, call(): pl.pallas_call(body, in_specs=[SMEM] * scalars + [VMEM] * (count - scalar...  34 us
    ppermute x31, waiting for transfers between devices, send(): return lax.ppermute(value, ('row', 'col'), pairs)  20.1 us
  transfers between devices with their start and end apart: 31, of which 10 were waited for; matrix products, arithmetic and copies ran while one was open for 0% of the time, Pallas kernels for 22%

profile of v4, /device:TPU:0, one launch (start us, length us, event | category | flops | bytes accessed | tf_op | source)
XLA Modules:
  0.0 108.4 jit_solution(1730140725315182626)
XLA Ops:
  1.9 2.1 %prep.1 = (bf16[208,768]{1,0:T(8,128)(2,1)}, bf16[192,768]{1,0:T(8,128)(2,1)}, f32[24,128]{1,0:T(8,128)}) custom-call(f32[1]{0:T(128)S(6)} %copy.22.log_scale_ref, f32[1]{0:T(128)S(6)} %copy.23.bias_ref, bf16[192,768]{1,0:T(8,128)(2,1)} %refs_0_.1, bf16[192,768]{1,0:T(8,128)(2,1)} %values_ref.1, s32[1,192]{1,0:T(1,128)} %bitcast.1), custom_call_target="tpu_custom_call" | custom-call | tf_op jit(solution)/shard_map/prep/pallas_call | solution.py:306
  4.0 0.0 copy-start.2
  4.0 0.0 copy-start.3
  4.0 1.6 %collective-permute-start.2 = (bf16[208,768]{1,0:T(8,128)(2,1)}, bf16[208,768]{1,0:T(8,128)(2,1)S(1)}, u32[]{:S(2)}, u32[]{:S(2)}) collective-permute-start(bf16[208,768]{1,0:T(8,128)(2,1)} %get-tuple-element.45.refs_0_), channel_id=1, source_target_pairs={{0,1},{1,2},{2,3},{3,0},{4,5},{5,6},{6,7},{7,4},{8,9},{9,10},{10,1... | collective-permute-start | bytes 958472 | tf_op jit(solution)/shard_map/ppermute | solution.py:37
  5.7 1.7 %collective-permute-start.1 = (bf16[208,768]{1,0:T(8,128)(2,1)}, bf16[208,768]{1,0:T(8,128)(2,1)S(1)}, u32[]{:S(2)}, u32[]{:S(2)}) collective-permute-start(bf16[208,768]{1,0:T(8,128)(2,1)} %get-tuple-element.45.refs_0_), channel_id=1, source_target_pairs={{0,3},{1,0},{2,1},{3,2},{4,7},{5,4},{6,5},{7,6},{8,11},{9,8},{10,9... | collective-permute-start | bytes 958472 | tf_op jit(solution)/shard_map/ppermute | solution.py:37
  7.3 2.0 %collective-permute-start = (bf16[208,768]{1,0:T(8,128)(2,1)}, bf16[208,768]{1,0:T(8,128)(2,1)S(1)}, u32[]{:S(2)}, u32[]{:S(2)}) collective-permute-start(bf16[208,768]{1,0:T(8,128)(2,1)} %get-tuple-element.45.refs_0_), channel_id=1, source_target_pairs={{0,16},{1,17},{2,18},{3,19},{4,20},{5,21},{6,22},{7,23},{8,24},{9,... | collective-permute-start | bytes 958472 | tf_op jit(solution)/shard_map/ppermute | solution.py:37
  9.3 1.6 %collective-permute-start.9 = (bf16[192,768]{1,0:T(8,128)(2,1)}, bf16[192,768]{1,0:T(8,128)(2,1)S(1)}, u32[]{:S(2)}, u32[]{:S(2)}) collective-permute-start(bf16[192,768]{1,0:T(8,128)(2,1)} %get-tuple-element.48.refs_0_), channel_id=1, source_target_pairs={{0,32},{1,33},{2,34},{3,35},{4,36},{5,37},{6,38},{7,39},{8,40},{9,... | collective-permute-start | bytes 884744 | tf_op jit(solution)/shard_map/ppermute | solution.py:37
  10.9 1.7 %collective-permute-start.8 = (bf16[192,768]{1,0:T(8,128)(2,1)}, bf16[192,768]{1,0:T(8,128)(2,1)S(1)}, u32[]{:S(2)}, u32[]{:S(2)}) collective-permute-start(bf16[192,768]{1,0:T(8,128)(2,1)} %get-tuple-element.48.refs_0_), channel_id=1, source_target_pairs={{0,96},{1,97},{2,98},{3,99},{4,100},{5,101},{6,102},{7,103},{8,104... | collective-permute-start | bytes 884744 | tf_op jit(solution)/shard_map/ppermute | solution.py:37
  12.6 2.1 %collective-permute-done.2.refs_2_.refs_4_ = bf16[208,768]{1,0:T(8,128)(2,1)S(1)} collective-permute-done((bf16[208,768]{1,0:T(8,128)(2,1)}, bf16[208,768]{1,0:T(8,128)(2,1)S(1)}, u32[]{:S(2)}, u32[]{:S(2)}) %collective-permute-start.2) | collective-permute-done | bytes 319520 | tf_op jit(solution)/shard_map/ppermute | solution.py:37
  14.7 4.2 %collective-permute-start.7 = (bf16[192,768]{1,0:T(8,128)(2,1)}, bf16[192,768]{1,0:T(8,128)(2,1)S(1)}, u32[]{:S(2)}, u32[]{:S(2)}) collective-permute-start(bf16[192,768]{1,0:T(8,128)(2,1)} %get-tuple-element.48.refs_0_), channel_id=1, source_target_pairs={{0,20},{1,21},{2,22},{3,23},{4,16},{5,17},{6,18},{7,19},{8,28},{9,... | collective-permute-start | bytes 884744 | tf_op jit(solution)/shard_map/ppermute | solution.py:37
  18.9 0.0 collective-permute-done.1.refs_1_.refs_2_
  18.9 0.0 collective-permute-done.refs_0_.refs_1_
  18.9 1.6 %collective-permute-start.3 = (bf16[208,768]{1,0:T(8,128)(2,1)S(1)}, bf16[208,768]{1,0:T(8,128)(2,1)S(1)}, u32[]{:S(2)}, u32[]{:S(2)}) collective-permute-start(bf16[208,768]{1,0:T(8,128)(2,1)S(1)} %gate.2.refs_3_), channel_id=1, source_target_pairs={{0,3},{1,0},{2,1},{3,2},{4,7},{5,4},{6,5},{7,6},{8,11},{9,8},{10,9... | collective-permute-start | bytes 958472 | tf_op jit(solution)/shard_map/ppermute | solution.py:37
  20.6 0.5 collective-permute-start.4
  21.0 0.3 collective-permute-start.5
  21.3 3.9 %collective-permute-done.7.refs_1_.refs_0_ = bf16[192,768]{1,0:T(8,128)(2,1)S(1)} collective-permute-done((bf16[192,768]{1,0:T(8,128)(2,1)}, bf16[192,768]{1,0:T(8,128)(2,1)S(1)}, u32[]{:S(2)}, u32[]{:S(2)}) %collective-permute-start.7) | collective-permute-done | bytes 294944 | tf_op jit(solution)/shard_map/ppermute | solution.py:37
  25.3 3.1 %collective-permute-start.10 = (bf16[192,768]{1,0:T(8,128)(2,1)S(1)}, bf16[192,768]{1,0:T(8,128)(2,1)S(1)}, u32[]{:S(2)}, u32[]{:S(2)}) collective-permute-start(bf16[192,768]{1,0:T(8,128)(2,1)S(1)} %gate.3), channel_id=1, source_target_pairs={{0,96},{1,97},{2,98},{3,99},{4,100},{5,101},{6,102},{7,103},{8,104... | collective-permute-start | bytes 884744 | tf_op jit(solution)/shard_map/ppermute | solution.py:37
  28.4 1.5 %collective-permute-start.6 = (bf16[208,768]{1,0:T(8,128)(2,1)S(1)}, bf16[208,768]{1,0:T(8,128)(2,1)S(1)}, u32[]{:S(2)}, u32[]{:S(2)}) collective-permute-start(bf16[208,768]{1,0:T(8,128)(2,1)S(1)} %collective-permute-done.3.refs_3_), channel_id=1, source_target_pairs={{0,3},{1,0},{2,1},{3,2},{4,7},{5,4},{6,5},{7,6},{8,11},{9,8},{10,9... | collective-permute-start | bytes 958472 | tf_op jit(solution)/shard_map/ppermute | solution.py:37
  29.9 1.6 %collective-permute-start.11 = (bf16[192,768]{1,0:T(8,128)(2,1)S(1)}, bf16[192,768]{1,0:T(8,128)(2,1)S(1)}, u32[]{:S(2)}, u32[]{:S(2)}) collective-permute-start(bf16[192,768]{1,0:T(8,128)(2,1)S(1)} %gate.3), channel_id=1, source_target_pairs={{0,32},{1,33},{2,34},{3,35},{4,36},{5,37},{6,38},{7,39},{8,40},{9,... | collective-permute-start | bytes 884744 | tf_op jit(solution)/shard_map/ppermute | solution.py:37
  31.5 1.6 %collective-permute-done.10.refs_1_ = bf16[192,768]{1,0:T(8,128)(2,1)S(1)} collective-permute-done((bf16[192,768]{1,0:T(8,128)(2,1)S(1)}, bf16[192,768]{1,0:T(8,128)(2,1)S(1)}, u32[]{:S(2)}, u32[]{:S(2)}) %collective-permute-start.10) | collective-permute-done | bytes 294944 | tf_op jit(solution)/shard_map/ppermute | solution.py:37
  33.1 1.0 collective-permute-start.12
  34.2 2.7 %collective-permute-start.13 = (bf16[192,768]{1,0:T(8,128)(2,1)S(1)}, bf16[192,768]{1,0:T(8,128)(2,1)S(1)}, u32[]{:S(2)}, u32[]{:S(2)}) collective-permute-start(bf16[192,768]{1,0:T(8,128)(2,1)S(1)} %collective-permute-done.10.refs_1_), channel_id=1, source_target_pairs={{0,96},{1,97},{2,98},{3,99},{4,100},{5,101},{6,102},{7,103},{8,104... | collective-permute-start | bytes 884744 | tf_op jit(solution)/shard_map/ppermute | solution.py:37
  36.8 0.1 near_images.1
  37.0 0.1 first_texts.1.refs_2_.refs_0_
  37.1 0.6 copy-done.4
  37.7 4.4 %score_first.1 = (f32[1536,768]{1,0:T(8,128)S(1)}, bf16[1536,1536]{1,0:T(8,128)(2,1)S(1)}, f32[8,128]{1,0:T(8,128)S(1)}) custom-call(f32[24,128]{1,0:T(8,128)S(1)} %copy-done.4, bf16[1536,768]{1,0:T(8,128)(2,1)S(1)} %get-tuple-element.46.refs_4_.refs_1_.refs_0_, bf16[1536,768]{1,0:T(8,128)(2,1)S(1)} %first_texts.1.refs_2_.refs_0_, ...), custom_call_target="tpu_custom_call" | custom-call | flops 2717908992 | bytes 4194304 | tf_op jit(solution)/shard_map/score_first/pallas_call | solution.py:72
  42.1 2.3 %score_second.1 = (f32[1536,768]{1,0:T(8,128)S(1)}, bf16[1536,1536]{1,0:T(8,128)(2,1)S(1)}, f32[8,128]{1,0:T(8,128)S(1)}) custom-call(f32[24,128]{1,0:T(8,128)S(1)} %copy-done.4, bf16[1536,768]{1,0:T(8,128)(2,1)S(1)} %get-tuple-element.46.refs_4_.refs_1_.refs_0_, ...), custom_call_target="tpu_custom_call", output_to_operand_aliasing={{0}: (5, {}), {1}: (6, {})} | custom-call | flops 1358954496 | bytes 4194304 | tf_op jit(solution)/shard_map/score_second/pallas_call | solution.py:72
  44.5 0.3 collective-permute-start.14
  44.8 0.1 away_images.1
  44.9 6.1 %score_rest.1 = (f32[1536,768]{1,0:T(8,128)S(1)}, bf16[1536,1536]{1,0:T(8,128)(2,1)S(1)}, f32[8,128]{1,0:T(8,128)S(1)}) custom-call(f32[24,128]{1,0:T(8,128)S(1)} %copy-done.4, bf16[1536,768]{1,0:T(8,128)(2,1)S(1)} %get-tuple-element.53.refs_1_, bf16[1536,768]{1,0:T(8,128)(2,1)S(1)} %away_texts.1.refs_2_, ...), custom_call_target="tpu_custom_call", output_to_operand_aliasing={{0}: (5, {}), {1}: (6, {})} | custom-call | flops 3170893824 | bytes 4194304 | tf_op jit(solution)/shard_map/score_rest/pallas_call | solution.py:72
  51.1 10.4 %score_sib.1 = (bf16[1552,768]{1,0:T(8,128)(2,1)S(1)}, bf16[1536,1536]{1,0:T(8,128)(2,1)S(1)}, f32[8,128]{1,0:T(8,128)S(1)}) custom-call(f32[24,128]{1,0:T(8,128)S(1)} %copy-done.4, bf16[1536,768]{1,0:T(8,128)(2,1)S(1)} %get-tuple-element.53.refs_1_, bf16[1536,768]{1,0:T(8,128)(2,1)S(1)} %collective-permute-done.14.refs_2_.refs_3_, ...), custom_call_target="tpu_custom_call" | custom-call | flops 7247757312 | bytes 4194304 | tf_op jit(solution)/shard_map/score_sib/pallas_call | solution.py:72
  61.5 0.6 collective-permute-start.15
  62.1 2.0 %image_away.1 = (bf16[192,768]{1,0:T(8,128)(2,1)S(1)}, bf16[192,768]{1,0:T(8,128)(2,1)S(1)}) custom-call(bf16[1536,1536]{1,0:T(8,128)(2,1)S(1)} %get-tuple-element.61.refs_0_, bf16[1536,1536]{1,0:T(8,128)(2,1)S(1)} %get-tuple-element.62.refs_1_, bf16[1536,768]{1,0:T(8,128)(2,1)S(1)} %away_texts.1.refs_2_, ...), custom_call_target="tpu_custom_call" | custom-call | flops 905969664 | bytes 4194304 | tf_op jit(solution)/shard_map/image_away/pallas_call | solution.py:72
  64.2 0.4 collective-permute-start.18
  64.5 3.0 %collective-permute-start.19 = (bf16[192,768]{1,0:T(8,128)(2,1)S(1)}, bf16[192,768]{1,0:T(8,128)(2,1)S(1)}, u32[]{:S(2)}, u32[]{:S(2)}) collective-permute-start(bf16[192,768]{1,0:T(8,128)(2,1)S(1)} %get-tuple-element.64.refs_4_), channel_id=1, source_target_pairs={{0,3},{1,0},{2,1},{3,2},{4,7},{5,4},{6,5},{7,6},{8,11},{9,8},{10,9... | collective-permute-start | bytes 884744 | tf_op jit(solution)/shard_map/ppermute | solution.py:37
  67.5 0.6 add.13
  68.1 1.1 %collective-permute-start.16 = (bf16[208,768]{1,0:T(8,128)(2,1)S(1)}, bf16[208,768]{1,0:T(8,128)(2,1)S(1)}, u32[]{:S(2)}, u32[]{:S(2)}) collective-permute-start(bf16[208,768]{1,0:T(8,128)(2,1)S(1)} %get-tuple-element.68), channel_id=1, source_target_pairs={{0,32},{1,33},{2,34},{3,35},{4,36},{5,37},{6,38},{7,39},{8,40},{9,... | collective-permute-start | bytes 958472 | tf_op jit(solution)/shard_map/ppermute | solution.py:37
  69.2 2.2 %collective-permute-start.17 = (bf16[208,768]{1,0:T(8,128)(2,1)S(1)}, bf16[208,768]{1,0:T(8,128)(2,1)S(1)}, u32[]{:S(2)}, u32[]{:S(2)}) collective-permute-start(bf16[208,768]{1,0:T(8,128)(2,1)S(1)} %get-tuple-element.69), channel_id=1, source_target_pairs={{0,96},{1,97},{2,98},{3,99},{4,100},{5,101},{6,102},{7,103},{8,104... | collective-permute-start | bytes 958472 | tf_op jit(solution)/shard_map/ppermute | solution.py:37
  71.4 3.9 %image_ring.1 = (f32[384,768]{1,0:T(8,128)S(1)}, f32[384,768]{1,0:T(8,128)S(1)}) custom-call(bf16[1536,1536]{1,0:T(8,128)(2,1)S(1)} %get-tuple-element.61.refs_0_, bf16[1536,1536]{1,0:T(8,128)(2,1)S(1)} %get-tuple-element.62.refs_1_, bf16[1536,768]{1,0:T(8,128)(2,1)S(1)} %away_texts.1.refs_2_, bf16[1536,768]{1,0:T(8,128)(2,1)S(1)} %collective-permute-done.14.refs_2_.refs_3_), custom_call_target="tpu_custom_call" | custom-call | flops 1811939328 | bytes 4194304 | tf_op jit(solution)/shard_map/image_ring/pallas_call | solution.py:72
  75.3 0.2 turn.2
  75.4 2.1 %collective-permute-start.24 = (bf16[384,768]{1,0:T(8,128)(2,1)S(1)}, bf16[384,768]{1,0:T(8,128)(2,1)S(1)}, u32[]{:S(2)}, u32[]{:S(2)}) collective-permute-start(bf16[384,768]{1,0:T(8,128)(2,1)S(1)} %get-tuple-element.78), channel_id=1, source_target_pairs={{0,3},{1,0},{2,1},{3,2},{4,7},{5,4},{6,5},{7,6},{8,11},{9,8},{10,9... | collective-permute-start | bytes 1769480 | tf_op jit(solution)/shard_map/ppermute | solution.py:37
  77.6 0.7 collective-permute-done.16.refs_2_
  78.2 0.2 turn.3
  78.4 1.2 %collective-permute-start.20 = (bf16[384,768]{1,0:T(8,128)(2,1)S(1)}, bf16[384,768]{1,0:T(8,128)(2,1)S(1)}, u32[]{:S(2)}, u32[]{:S(2)}) collective-permute-start(bf16[384,768]{1,0:T(8,128)(2,1)S(1)} %get-tuple-element.74), channel_id=1, source_target_pairs={{0,32},{1,33},{2,34},{3,35},{4,36},{5,37},{6,38},{7,39},{8,40},{9,... | collective-permute-start | bytes 1769480 | tf_op jit(solution)/shard_map/ppermute | solution.py:37
  79.6 2.1 %collective-permute-start.21 = (bf16[384,768]{1,0:T(8,128)(2,1)S(1)}, bf16[384,768]{1,0:T(8,128)(2,1)S(1)}, u32[]{:S(2)}, u32[]{:S(2)}) collective-permute-start(bf16[384,768]{1,0:T(8,128)(2,1)S(1)} %get-tuple-element.75), channel_id=1, source_target_pairs={{0,96},{1,97},{2,98},{3,99},{4,100},{5,101},{6,102},{7,103},{8,104... | collective-permute-start | bytes 1769480 | tf_op jit(solution)/shard_map/ppermute | solution.py:37
  81.7 3.6 %collective-permute-done.25 = f32[8,128]{1,0:T(8,128)S(1)} collective-permute-done((f32[8,128]{1,0:T(8,128)S(1)}, f32[8,128]{1,0:T(8,128)S(1)}, u32[]{:S(2)}, u32[]{:S(2)}) %collective-permute-start.25) | collective-permute-done | bytes 4128 | tf_op jit(solution)/shard_map/ppermute | solution.py:37
  85.4 2.7 %collective-permute-start.26 = (f32[8,128]{1,0:T(8,128)S(1)}, f32[8,128]{1,0:T(8,128)S(1)}, u32[]{:S(2)}, u32[]{:S(2)}) collective-permute-start(f32[8,128]{1,0:T(8,128)S(1)} %add.10), channel_id=1, source_target_pairs={{0,20},{1,21},{2,22},{3,23},{4,16},{5,17},{6,18},{7,19},{8,28},{9,... | collective-permute-start | bytes 12296 | tf_op jit(solution)/shard_map/ppermute | solution.py:37
  88.0 2.1 %collective-permute-done.26 = f32[8,128]{1,0:T(8,128)S(1)} collective-permute-done((f32[8,128]{1,0:T(8,128)S(1)}, f32[8,128]{1,0:T(8,128)S(1)}, u32[]{:S(2)}, u32[]{:S(2)}) %collective-permute-start.26) | collective-permute-done | bytes 4128 | tf_op jit(solution)/shard_map/ppermute | solution.py:37
  90.2 0.0 collective-permute-start.27
  90.2 2.0 %image_near.1 = (f32[192,768]{1,0:T(8,128)S(1)}, f32[192,768]{1,0:T(8,128)S(1)}) custom-call(bf16[1536,1536]{1,0:T(8,128)(2,1)S(1)} %get-tuple-element.61.refs_0_, bf16[1536,1536]{1,0:T(8,128)(2,1)S(1)} %get-tuple-element.62.refs_1_, bf16[1536,768]{1,0:T(8,128)(2,1)S(1)} %away_texts.1.refs_2_, bf16[1536,768]{1,0:T(8,128)(2,1)S(1)} %collective-permute-done.14.refs_2_.refs_3_), custom_call_target="tpu_custom_call" | custom-call | flops 905969664 | bytes 4194304 | tf_op jit(solution)/shard_map/image_near/pallas_call | solution.py:72
  92.3 0.0 copy-start
  92.3 0.3 collective-permute-done.23.refs_1_.refs_2_
  92.6 1.2 %collective-permute-done.27.refs_4_ = f32[8,128]{1,0:T(8,128)S(1)} collective-permute-done((f32[8,128]{1,0:T(8,128)S(1)}, f32[8,128]{1,0:T(8,128)S(1)}, u32[]{:S(2)}, u32[]{:S(2)}) %collective-permute-start.27) | collective-permute-done | bytes 4128 | tf_op jit(solution)/shard_map/ppermute | solution.py:37
  93.8 0.1 far.3
  93.9 0.1 collective-permute-start.30
  94.0 0.0 copy-start.1
  94.0 0.1 far.2
  94.1 2.8 %collective-permute-start.22 = (bf16[192,768]{1,0:T(8,128)(2,1)S(1)}, bf16[192,768]{1,0:T(8,128)(2,1)S(1)}, u32[]{:S(2)}, u32[]{:S(2)}) collective-permute-start(bf16[192,768]{1,0:T(8,128)(2,1)S(1)} %far.2), channel_id=1, source_target_pairs={{0,20},{1,21},{2,22},{3,23},{4,16},{5,17},{6,18},{7,19},{8,28},{9,... | collective-permute-start | bytes 884744 | tf_op jit(solution)/shard_map/ppermute | solution.py:37
  96.9 2.5 %collective-permute-start.28 = (f32[8,128]{1,0:T(8,128)S(1)}, f32[8,128]{1,0:T(8,128)S(1)}, u32[]{:S(2)}, u32[]{:S(2)}) collective-permute-start(f32[8,128]{1,0:T(8,128)S(1)} %get-tuple-element.80), channel_id=1, source_target_pairs={{0,2},{1,3},{2,0},{3,1},{4,6},{5,7},{6,4},{7,5},{8,10},{9,11},{10,... | collective-permute-start | bytes 12296 | tf_op jit(solution)/shard_map/ppermute | solution.py:37
  99.4 2.6 %collective-permute-done.28 = f32[8,128]{1,0:T(8,128)S(1)} collective-permute-done((f32[8,128]{1,0:T(8,128)S(1)}, f32[8,128]{1,0:T(8,128)S(1)}, u32[]{:S(2)}, u32[]{:S(2)}) %collective-permute-start.28) | collective-permute-done | bytes 4128 | tf_op jit(solution)/shard_map/ppermute | solution.py:37
  102.0 2.1 %collective-permute-start.29 = (f32[8,128]{1,0:T(8,128)S(1)}, f32[8,128]{1,0:T(8,128)S(1)}, u32[]{:S(2)}, u32[]{:S(2)}) collective-permute-start(f32[8,128]{1,0:T(8,128)S(1)} %add.12.loss), channel_id=1, source_target_pairs={{0,64},{1,65},{2,66},{3,67},{4,68},{5,69},{6,70},{7,71},{8,72},{9,... | collective-permute-start | bytes 12296 | tf_op jit(solution)/shard_map/ppermute | solution.py:37
  104.1 1.1 %unproject.3 = f32[192,768]{1,0:T(8,128)} custom-call(bf16[192,768]{1,0:T(8,128)(2,1)S(1)} %copy-done, f32[192,768]{1,0:T(8,128)S(1)} %get-tuple-element.82.refs_1_, bf16[384,768]{1,0:T(8,128)(2,1)S(1)} %collective-permute-done.23.refs_1_.refs_2_, bf16[384,768]{1,0:T(8,128)(2,1)S(1)} %collective-permute-done.24.refs_2_.refs_3_, ...), custom_call_target="tpu_custom_call" | custom-call | bytes 4194304 | tf_op jit(solution)/shard_map/unproject/pallas_call | solution.py:72
  105.2 1.9 %collective-permute-done.29.step = f32[8,128]{1,0:T(8,128)S(1)} collective-permute-done((f32[8,128]{1,0:T(8,128)S(1)}, f32[8,128]{1,0:T(8,128)S(1)}, u32[]{:S(2)}, u32[]{:S(2)}) %collective-permute-start.29) | collective-permute-done | bytes 4128 | tf_op jit(solution)/shard_map/ppermute | solution.py:37
  107.1 1.1 %unproject.2 = (f32[192,768]{1,0:T(8,128)}, f32[1]{0:T(128)}) custom-call(bf16[192,768]{1,0:T(8,128)(2,1)S(1)} %copy-done.1, f32[192,768]{1,0:T(8,128)S(1)} %get-tuple-element.65.own_ref, bf16[384,768]{1,0:T(8,128)(2,1)S(1)} %collective-permute-done.20.refs_1_.plus, bf16[384,768]{1,0:T(8,128)(2,1)S(1)} %collective-permute-done.21.refs_2_.minus, ...), custom_call_target="tpu_custom_call" | custom-call | tf_op jit(solution)/shard_map/unproject/pallas_call | solution.py:399
  (33 shorter events, 0.2 us)
Async XLA Ops:
  4.0 32.8 %copy-start.2 = (bf16[208,768]{1,0:T(8,128)(2,1)S(1)}, bf16[208,768]{1,0:T(8,128)(2,1)}, u32[]{:S(2)}) copy-start(bf16[208,768]{1,0:T(8,128)(2,1)} %get-tuple-element.45.refs_0_) | copy-start | bytes 958468
  4.0 33.0 %copy-start.3 = (bf16[192,768]{1,0:T(8,128)(2,1)S(1)}, bf16[192,768]{1,0:T(8,128)(2,1)}, u32[]{:S(2)}) copy-start(bf16[192,768]{1,0:T(8,128)(2,1)} %get-tuple-element.48.refs_0_) | copy-start | bytes 884740
  4.0 10.7 %collective-permute-start.2 = (bf16[208,768]{1,0:T(8,128)(2,1)}, bf16[208,768]{1,0:T(8,128)(2,1)S(1)}, u32[]{:S(2)}, u32[]{:S(2)}) collective-permute-start(bf16[208,768]{1,0:T(8,128)(2,1)} %get-tuple-element.45.refs_0_), channel_id=1, source_target_pairs={{0,1},{1,2},{2,3},{3,0},{4,5},{5,6},{6,7},{7,4},{8,9},{9,10},{10,1... | collective-permute-start | bytes 958472 | tf_op jit(solution)/shard_map/ppermute | solution.py:37
  5.7 13.2 %collective-permute-start.1 = (bf16[208,768]{1,0:T(8,128)(2,1)}, bf16[208,768]{1,0:T(8,128)(2,1)S(1)}, u32[]{:S(2)}, u32[]{:S(2)}) collective-permute-start(bf16[208,768]{1,0:T(8,128)(2,1)} %get-tuple-element.45.refs_0_), channel_id=1, source_target_pairs={{0,3},{1,0},{2,1},{3,2},{4,7},{5,4},{6,5},{7,6},{8,11},{9,8},{10,9... | collective-permute-start | bytes 958472 | tf_op jit(solution)/shard_map/ppermute | solution.py:37
  7.3 11.6 %collective-permute-start = (bf16[208,768]{1,0:T(8,128)(2,1)}, bf16[208,768]{1,0:T(8,128)(2,1)S(1)}, u32[]{:S(2)}, u32[]{:S(2)}) collective-permute-start(bf16[208,768]{1,0:T(8,128)(2,1)} %get-tuple-element.45.refs_0_), channel_id=1, source_target_pairs={{0,16},{1,17},{2,18},{3,19},{4,20},{5,21},{6,22},{7,23},{8,24},{9,... | collective-permute-start | bytes 958472 | tf_op jit(solution)/shard_map/ppermute | solution.py:37
  9.3 11.7 %collective-permute-start.9 = (bf16[192,768]{1,0:T(8,128)(2,1)}, bf16[192,768]{1,0:T(8,128)(2,1)S(1)}, u32[]{:S(2)}, u32[]{:S(2)}) collective-permute-start(bf16[192,768]{1,0:T(8,128)(2,1)} %get-tuple-element.48.refs_0_), channel_id=1, source_target_pairs={{0,32},{1,33},{2,34},{3,35},{4,36},{5,37},{6,38},{7,39},{8,40},{9,... | collective-permute-start | bytes 884744 | tf_op jit(solution)/shard_map/ppermute | solution.py:37
  10.9 10.4 %collective-permute-start.8 = (bf16[192,768]{1,0:T(8,128)(2,1)}, bf16[192,768]{1,0:T(8,128)(2,1)S(1)}, u32[]{:S(2)}, u32[]{:S(2)}) collective-permute-start(bf16[192,768]{1,0:T(8,128)(2,1)} %get-tuple-element.48.refs_0_), channel_id=1, source_target_pairs={{0,96},{1,97},{2,98},{3,99},{4,100},{5,101},{6,102},{7,103},{8,104... | collective-permute-start | bytes 884744 | tf_op jit(solution)/shard_map/ppermute | solution.py:37
  14.7 10.6 %collective-permute-start.7 = (bf16[192,768]{1,0:T(8,128)(2,1)}, bf16[192,768]{1,0:T(8,128)(2,1)S(1)}, u32[]{:S(2)}, u32[]{:S(2)}) collective-permute-start(bf16[192,768]{1,0:T(8,128)(2,1)} %get-tuple-element.48.refs_0_), channel_id=1, source_target_pairs={{0,20},{1,21},{2,22},{3,23},{4,16},{5,17},{6,18},{7,19},{8,28},{9,... | collective-permute-start | bytes 884744 | tf_op jit(solution)/shard_map/ppermute | solution.py:37
  18.9 9.4 %collective-permute-start.3 = (bf16[208,768]{1,0:T(8,128)(2,1)S(1)}, bf16[208,768]{1,0:T(8,128)(2,1)S(1)}, u32[]{:S(2)}, u32[]{:S(2)}) collective-permute-start(bf16[208,768]{1,0:T(8,128)(2,1)S(1)} %gate.2.refs_3_), channel_id=1, source_target_pairs={{0,3},{1,0},{2,1},{3,2},{4,7},{5,4},{6,5},{7,6},{8,11},{9,8},{10,9... | collective-permute-start | bytes 958472 | tf_op jit(solution)/shard_map/ppermute | solution.py:37
  20.6 13.6 %collective-permute-start.4 = (bf16[208,768]{1,0:T(8,128)(2,1)S(1)}, bf16[208,768]{1,0:T(8,128)(2,1)S(1)}, u32[]{:S(2)}, u32[]{:S(2)}) collective-permute-start(bf16[208,768]{1,0:T(8,128)(2,1)S(1)} %gate.2.refs_3_), channel_id=1, source_target_pairs={{0,1},{1,2},{2,3},{3,0},{4,5},{5,6},{6,7},{7,4},{8,9},{9,10},{10,1... | collective-permute-start | bytes 958472 | tf_op jit(solution)/shard_map/ppermute | solution.py:37
  21.0 15.9 %collective-permute-start.5 = (bf16[208,768]{1,0:T(8,128)(2,1)S(1)}, bf16[208,768]{1,0:T(8,128)(2,1)S(1)}, u32[]{:S(2)}, u32[]{:S(2)}) collective-permute-start(bf16[208,768]{1,0:T(8,128)(2,1)S(1)} %collective-permute-done.2.refs_2_.refs_4_), channel_id=1, source_target_pairs={{0,1},{1,2},{2,3},{3,0},{4,5},{5,6},{6,7},{7,4},{8,9},{9,10},{10,1... | collective-permute-start | bytes 958472 | tf_op jit(solution)/shard_map/ppermute | solution.py:37
  25.3 7.8 %collective-permute-start.10 = (bf16[192,768]{1,0:T(8,128)(2,1)S(1)}, bf16[192,768]{1,0:T(8,128)(2,1)S(1)}, u32[]{:S(2)}, u32[]{:S(2)}) collective-permute-start(bf16[192,768]{1,0:T(8,128)(2,1)S(1)} %gate.3), channel_id=1, source_target_pairs={{0,96},{1,97},{2,98},{3,99},{4,100},{5,101},{6,102},{7,103},{8,104... | collective-permute-start | bytes 884744 | tf_op jit(solution)/shard_map/ppermute | solution.py:37
  28.4 13.7 %collective-permute-start.6 = (bf16[208,768]{1,0:T(8,128)(2,1)S(1)}, bf16[208,768]{1,0:T(8,128)(2,1)S(1)}, u32[]{:S(2)}, u32[]{:S(2)}) collective-permute-start(bf16[208,768]{1,0:T(8,128)(2,1)S(1)} %collective-permute-done.3.refs_3_), channel_id=1, source_target_pairs={{0,3},{1,0},{2,1},{3,2},{4,7},{5,4},{6,5},{7,6},{8,11},{9,8},{10,9... | collective-permute-start | bytes 958472 | tf_op jit(solution)/shard_map/ppermute | solution.py:37
  29.9 12.1 %collective-permute-start.11 = (bf16[192,768]{1,0:T(8,128)(2,1)S(1)}, bf16[192,768]{1,0:T(8,128)(2,1)S(1)}, u32[]{:S(2)}, u32[]{:S(2)}) collective-permute-start(bf16[192,768]{1,0:T(8,128)(2,1)S(1)} %gate.3), channel_id=1, source_target_pairs={{0,32},{1,33},{2,34},{3,35},{4,36},{5,37},{6,38},{7,39},{8,40},{9,... | collective-permute-start | bytes 884744 | tf_op jit(solution)/shard_map/ppermute | solution.py:37
  33.1 11.4 %collective-permute-start.12 = (bf16[192,768]{1,0:T(8,128)(2,1)S(1)}, bf16[192,768]{1,0:T(8,128)(2,1)S(1)}, u32[]{:S(2)}, u32[]{:S(2)}) collective-permute-start(bf16[192,768]{1,0:T(8,128)(2,1)S(1)} %collective-permute-done.9.refs_3_.refs_2_), channel_id=1, source_target_pairs={{0,32},{1,33},{2,34},{3,35},{4,36},{5,37},{6,38},{7,39},{8,40},{9,... | collective-permute-start | bytes 884744 | tf_op jit(solution)/shard_map/ppermute | solution.py:37
  34.2 10.3 %collective-permute-start.13 = (bf16[192,768]{1,0:T(8,128)(2,1)S(1)}, bf16[192,768]{1,0:T(8,128)(2,1)S(1)}, u32[]{:S(2)}, u32[]{:S(2)}) collective-permute-start(bf16[192,768]{1,0:T(8,128)(2,1)S(1)} %collective-permute-done.10.refs_1_), channel_id=1, source_target_pairs={{0,96},{1,97},{2,98},{3,99},{4,100},{5,101},{6,102},{7,103},{8,104... | collective-permute-start | bytes 884744 | tf_op jit(solution)/shard_map/ppermute | solution.py:37
  37.0 0.7 copy-start.4
  44.5 6.5 %collective-permute-start.14 = (bf16[1536,768]{1,0:T(8,128)(2,1)S(1)}, bf16[1536,768]{1,0:T(8,128)(2,1)S(1)}, u32[]{:S(2)}, u32[]{:S(2)}) collective-permute-start(bf16[1536,768]{1,0:T(8,128)(2,1)S(1)} %away_texts.1.refs_2_), channel_id=1, source_target_pairs={{0,8},{1,9},{2,10},{3,11},{4,12},{5,13},{6,14},{7,15},{8,0},{9,1},... | collective-permute-start | bytes 7077896 | tf_op jit(solution)/shard_map/ppermute | solution.py:37
  61.5 5.9 %collective-permute-start.15 = (bf16[1552,768]{1,0:T(8,128)(2,1)S(1)}, bf16[1552,768]{1,0:T(8,128)(2,1)S(1)}, u32[]{:S(2)}, u32[]{:S(2)}) collective-permute-start(bf16[1552,768]{1,0:T(8,128)(2,1)S(1)} %get-tuple-element.59), channel_id=1, source_target_pairs={{0,8},{1,9},{2,10},{3,11},{4,12},{5,13},{6,14},{7,15},{8,0},{9,1},... | collective-permute-start | bytes 7151624 | tf_op jit(solution)/shard_map/ppermute | solution.py:37
  64.2 11.1 %collective-permute-start.18 = (bf16[192,768]{1,0:T(8,128)(2,1)S(1)}, bf16[192,768]{1,0:T(8,128)(2,1)S(1)}, u32[]{:S(2)}, u32[]{:S(2)}) collective-permute-start(bf16[192,768]{1,0:T(8,128)(2,1)S(1)} %get-tuple-element.63.refs_3_), channel_id=1, source_target_pairs={{0,1},{1,2},{2,3},{3,0},{4,5},{5,6},{6,7},{7,4},{8,9},{9,10},{10,1... | collective-permute-start | bytes 884744 | tf_op jit(solution)/shard_map/ppermute | solution.py:37
  64.5 10.8 %collective-permute-start.19 = (bf16[192,768]{1,0:T(8,128)(2,1)S(1)}, bf16[192,768]{1,0:T(8,128)(2,1)S(1)}, u32[]{:S(2)}, u32[]{:S(2)}) collective-permute-start(bf16[192,768]{1,0:T(8,128)(2,1)S(1)} %get-tuple-element.64.refs_4_), channel_id=1, source_target_pairs={{0,3},{1,0},{2,1},{3,2},{4,7},{5,4},{6,5},{7,6},{8,11},{9,8},{10,9... | collective-permute-start | bytes 884744 | tf_op jit(solution)/shard_map/ppermute | solution.py:37
  68.1 10.2 %collective-permute-start.16 = (bf16[208,768]{1,0:T(8,128)(2,1)S(1)}, bf16[208,768]{1,0:T(8,128)(2,1)S(1)}, u32[]{:S(2)}, u32[]{:S(2)}) collective-permute-start(bf16[208,768]{1,0:T(8,128)(2,1)S(1)} %get-tuple-element.68), channel_id=1, source_target_pairs={{0,32},{1,33},{2,34},{3,35},{4,36},{5,37},{6,38},{7,39},{8,40},{9,... | collective-permute-start | bytes 958472 | tf_op jit(solution)/shard_map/ppermute | solution.py:37
  69.2 9.1 %collective-permute-start.17 = (bf16[208,768]{1,0:T(8,128)(2,1)S(1)}, bf16[208,768]{1,0:T(8,128)(2,1)S(1)}, u32[]{:S(2)}, u32[]{:S(2)}) collective-permute-start(bf16[208,768]{1,0:T(8,128)(2,1)S(1)} %get-tuple-element.69), channel_id=1, source_target_pairs={{0,96},{1,97},{2,98},{3,99},{4,100},{5,101},{6,102},{7,103},{8,104... | collective-permute-start | bytes 958472 | tf_op jit(solution)/shard_map/ppermute | solution.py:37
  75.4 16.8 %collective-permute-start.24 = (bf16[384,768]{1,0:T(8,128)(2,1)S(1)}, bf16[384,768]{1,0:T(8,128)(2,1)S(1)}, u32[]{:S(2)}, u32[]{:S(2)}) collective-permute-start(bf16[384,768]{1,0:T(8,128)(2,1)S(1)} %get-tuple-element.78), channel_id=1, source_target_pairs={{0,3},{1,0},{2,1},{3,2},{4,7},{5,4},{6,5},{7,6},{8,11},{9,8},{10,9... | collective-permute-start | bytes 1769480 | tf_op jit(solution)/shard_map/ppermute | solution.py:37
  77.6 15.0 %collective-permute-start.23 = (bf16[384,768]{1,0:T(8,128)(2,1)S(1)}, bf16[384,768]{1,0:T(8,128)(2,1)S(1)}, u32[]{:S(2)}, u32[]{:S(2)}) collective-permute-start(bf16[384,768]{1,0:T(8,128)(2,1)S(1)} %get-tuple-element.73.refs_5_), channel_id=1, source_target_pairs={{0,1},{1,2},{2,3},{3,0},{4,5},{5,6},{6,7},{7,4},{8,9},{9,10},{10,1... | collective-permute-start | bytes 1769480 | tf_op jit(solution)/shard_map/ppermute | solution.py:37
  78.4 15.5 %collective-permute-start.20 = (bf16[384,768]{1,0:T(8,128)(2,1)S(1)}, bf16[384,768]{1,0:T(8,128)(2,1)S(1)}, u32[]{:S(2)}, u32[]{:S(2)}) collective-permute-start(bf16[384,768]{1,0:T(8,128)(2,1)S(1)} %get-tuple-element.74), channel_id=1, source_target_pairs={{0,32},{1,33},{2,34},{3,35},{4,36},{5,37},{6,38},{7,39},{8,40},{9,... | collective-permute-start | bytes 1769480 | tf_op jit(solution)/shard_map/ppermute | solution.py:37
  79.6 14.3 %collective-permute-start.21 = (bf16[384,768]{1,0:T(8,128)(2,1)S(1)}, bf16[384,768]{1,0:T(8,128)(2,1)S(1)}, u32[]{:S(2)}, u32[]{:S(2)}) collective-permute-start(bf16[384,768]{1,0:T(8,128)(2,1)S(1)} %get-tuple-element.75), channel_id=1, source_target_pairs={{0,96},{1,97},{2,98},{3,99},{4,100},{5,101},{6,102},{7,103},{8,104... | collective-permute-start | bytes 1769480 | tf_op jit(solution)/shard_map/ppermute | solution.py:37
  81.7 3.6 %collective-permute-start.25 = (f32[8,128]{1,0:T(8,128)S(1)}, f32[8,128]{1,0:T(8,128)S(1)}, u32[]{:S(2)}, u32[]{:S(2)}) collective-permute-start(f32[8,128]{1,0:T(8,128)S(1)} %get-tuple-element.79), channel_id=1, source_target_pairs={{0,16},{1,17},{2,18},{3,19},{4,20},{5,21},{6,22},{7,23},{8,24},{9,... | collective-permute-start | bytes 12296 | tf_op jit(solution)/shard_map/ppermute | solution.py:37
  85.4 4.8 %collective-permute-start.26 = (f32[8,128]{1,0:T(8,128)S(1)}, f32[8,128]{1,0:T(8,128)S(1)}, u32[]{:S(2)}, u32[]{:S(2)}) collective-permute-start(f32[8,128]{1,0:T(8,128)S(1)} %add.10), channel_id=1, source_target_pairs={{0,20},{1,21},{2,22},{3,23},{4,16},{5,17},{6,18},{7,19},{8,28},{9,... | collective-permute-start | bytes 12296 | tf_op jit(solution)/shard_map/ppermute | solution.py:37
  90.2 3.6 %collective-permute-start.27 = (f32[8,128]{1,0:T(8,128)S(1)}, f32[8,128]{1,0:T(8,128)S(1)}, u32[]{:S(2)}, u32[]{:S(2)}) collective-permute-start(f32[8,128]{1,0:T(8,128)S(1)} %add.11.refs_3_), channel_id=1, source_target_pairs={{0,1},{1,0},{2,3},{3,2},{4,5},{5,4},{6,7},{7,6},{8,9},{9,8},{10,11... | collective-permute-start | bytes 12296 | tf_op jit(solution)/shard_map/ppermute | solution.py:37
  92.3 11.9 %copy-start = (bf16[192,768]{1,0:T(8,128)(2,1)S(1)}, bf16[192,768]{1,0:T(8,128)(2,1)}, u32[]{:S(2)}) copy-start(bf16[192,768]{1,0:T(8,128)(2,1)} %refs_0_.1) | copy-start | bytes 884740
  93.9 10.2 %collective-permute-start.30 = (bf16[192,768]{1,0:T(8,128)(2,1)S(1)}, bf16[192,768]{1,0:T(8,128)(2,1)S(1)}, u32[]{:S(2)}, u32[]{:S(2)}) collective-permute-start(bf16[192,768]{1,0:T(8,128)(2,1)S(1)} %get-tuple-element.83), channel_id=1, source_target_pairs={{0,16},{1,17},{2,18},{3,19},{4,20},{5,21},{6,22},{7,23},{8,24},{9,... | collective-permute-start | bytes 884744 | tf_op jit(solution)/shard_map/ppermute | solution.py:37
  94.0 13.1 %copy-start.1 = (bf16[192,768]{1,0:T(8,128)(2,1)S(1)}, bf16[192,768]{1,0:T(8,128)(2,1)}, u32[]{:S(2)}) copy-start(bf16[192,768]{1,0:T(8,128)(2,1)} %values_ref.1) | copy-start | bytes 884740
  94.1 13.0 %collective-permute-start.22 = (bf16[192,768]{1,0:T(8,128)(2,1)S(1)}, bf16[192,768]{1,0:T(8,128)(2,1)S(1)}, u32[]{:S(2)}, u32[]{:S(2)}) collective-permute-start(bf16[192,768]{1,0:T(8,128)(2,1)S(1)} %far.2), channel_id=1, source_target_pairs={{0,20},{1,21},{2,22},{3,23},{4,16},{5,17},{6,18},{7,19},{8,28},{9,... | collective-permute-start | bytes 884744 | tf_op jit(solution)/shard_map/ppermute | solution.py:37
  96.9 5.1 %collective-permute-start.28 = (f32[8,128]{1,0:T(8,128)S(1)}, f32[8,128]{1,0:T(8,128)S(1)}, u32[]{:S(2)}, u32[]{:S(2)}) collective-permute-start(f32[8,128]{1,0:T(8,128)S(1)} %get-tuple-element.80), channel_id=1, source_target_pairs={{0,2},{1,3},{2,0},{3,1},{4,6},{5,7},{6,4},{7,5},{8,10},{9,11},{10,... | collective-permute-start | bytes 12296 | tf_op jit(solution)/shard_map/ppermute | solution.py:37
  102.0 5.1 %collective-permute-start.29 = (f32[8,128]{1,0:T(8,128)S(1)}, f32[8,128]{1,0:T(8,128)S(1)}, u32[]{:S(2)}, u32[]{:S(2)}) collective-permute-start(f32[8,128]{1,0:T(8,128)S(1)} %add.12.loss), channel_id=1, source_target_pairs={{0,64},{1,65},{2,66},{3,67},{4,68},{5,69},{6,70},{7,71},{8,72},{9,... | collective-permute-start | bytes 12296 | tf_op jit(solution)/shard_map/ppermute | solution.py:37

commit v5 on v4

--- a/solution.py
+++ b/solution.py
@@ -82,22 +82,17 @@
     )(*args, *after)
 
 
-def prep_kernel(log_scale_ref, bias_ref, images_hbm, texts_hbm, pair_hbm, x_ref, y_ref, const_ref, images, texts, pairs, sems):
-    copies = [
-        pltpu.make_async_copy(source, target, sems.at[i])
-        for i, (source, target) in enumerate(((images_hbm, images), (texts_hbm, texts), (pair_hbm, pairs)))
-    ]
-    for copy in copies:
-        copy.start()
+def prep_text_kernel(texts_ref, y_ref):
+    y_ref[...] = normalize(texts_ref)[0].astype(BF16)
+
+
+def prep_image_kernel(log_scale_ref, bias_ref, images_ref, pair_ref, x_ref, const_ref):
     scale = jnp.exp(jnp.full((8, 128), log_scale_ref[0], F32))
     const_ref[:8, :] = scale * LOG2E
     const_ref[8:16, :] = jnp.full((8, 128), bias_ref[0] * LOG2E, F32)
     const_ref[16:, :] = scale
-    for copy in copies:
-        copy.wait()
-    x_ref[:R, :] = normalize(images)[0].astype(BF16)
-    y_ref[...] = normalize(texts)[0].astype(BF16)
-    pair = pairs[...]
+    x_ref[:R, :] = normalize(images_ref)[0].astype(BF16)
+    pair = pair_ref[...]
     shard = ((pair.astype(F32) + 0.5) * (1.0 / R)).astype(jnp.int32)
     x_ref[R:, :] = jnp.zeros((16, D), BF16)
     x_ref[R:, :R] = jnp.broadcast_to(shard.astype(F32), (16, R)).astype(BF16)
@@ -303,25 +298,16 @@
 
 
 def local(images, texts, pair_index, log_scale, bias):
-    x_low, y_low, consts = pl.pallas_call(
-        prep_kernel,
-        in_specs=[SMEM] * 2 + [pl.BlockSpec(memory_space=pltpu.HBM)] * 3,
-        out_specs=[VMEM] * 3,
-        out_shape=[jax.ShapeDtypeStruct(*out) for out in (((RX, D), BF16), ((R, D), BF16), ((24, 128), F32))],
-        scratch_shapes=[
-            pltpu.VMEM((R, D), BF16),
-            pltpu.VMEM((R, D), BF16),
-            pltpu.VMEM((1, R), jnp.int32),
-            pltpu.SemaphoreType.DMA((3,)),
-        ],
-        compiler_params=pltpu.CompilerParams(vmem_limit_bytes=56 << 20),
-        name="prep",
-    )(log_scale, bias, images, texts, pair_index.reshape(1, R))
+    x_low, consts = call(
+        prep_image_kernel, [((RX, D), BF16), ((24, 128), F32)], log_scale, bias, images, pair_index.reshape(1, R),
+        name="prep_images", scalars=2,
+    )
+    y_low = call(prep_text_kernel, [((R, D), BF16)], texts, name="prep_texts")[0]
     x_zed, y_zed = swap_image_z(x_low), swap_text_z(y_low)
     x_plus, x_minus = send_x(x_low, -1), send_x(x_low, 1)
     y_plus, y_minus = send_y(y_low, -1), send_y(y_low, 1)
     x_next = gate(x_zed, x_plus, x_minus)
-    y_next = gate(y_zed, y_plus, y_minus, x_next)
+    y_next = gate(gate(y_zed, y_plus), y_minus, x_next)
     x_plus_z, x_minus_z = send_x(x_next, -1), send_x(x_next, 1)
     y_plus_z, y_minus_z = send_y(y_next, -1), send_y(y_next, 1)
     x_two, x_two_z = send_x(x_minus, 1), send_x(x_plus_z, -1)

time: 109 us -> 107 us (0.982)
  starting transfers between devices: 48.1 us -> 45.4 us
  local copies, waits for them, and re-layouts: 0.64 us -> 2.61 us
  Pallas kernels: 37.2 us -> 35.4 us
    ppermute x31, starting transfers between devices: 48.1 us -> 45.4 us  [send(): return lax.ppermute(value, ('row', 'col'), pairs)]
    pallas_call x1 -> x0, Pallas kernels: 2.06 us -> none  [local(): pl.pallas_call(prep_kernel, in_specs=[SMEM] * 2 + [pl.BlockSpec(memory_sp...]
    unnamed x10, local copies, waits for them, and re-layouts: 0.64 us -> 2.61 us
    pallas_call x20 -> x23, Pallas kernels: 34 us -> 34.3 us  [call(): pl.pallas_call(body, in_specs=[SMEM] * scalars + [VMEM] * (count - scalar...]
  transfers between devices with their start and end apart: 31 -> 31, of which waited for: 10 -> 12; matrix products, arithmetic and copies ran while one was open for 0% -> 0% of each run, Pallas kernels for 22% -> 22%
where the time goes in v5:
time: 107 us; the launch traced here: 106 us
  starting transfers between devices  45.4 us (42%)
  Pallas kernels  35.4 us (33%)
  waiting for transfers between devices  20.5 us (19%)
  local copies, waits for them, and re-layouts  2.61 us (2%)
  between operations  2.39 us (2%)
    ppermute x31, starting transfers between devices, send(): return lax.ppermute(value, ('row', 'col'), pairs)  45.4 us
    pallas_call x23, Pallas kernels, call(): pl.pallas_call(body, in_specs=[SMEM] * scalars + [VMEM] * (count - scalar...  34.3 us
    ppermute x31, waiting for transfers between devices, send(): return lax.ppermute(value, ('row', 'col'), pairs)  20.5 us
    unnamed x10, local copies, waits for them, and re-layouts  2.61 us
  transfers between devices with their start and end apart: 31, of which 12 were waited for; matrix products, arithmetic and copies ran while one was open for 0% of the time, Pallas kernels for 22%

profile of v5, /device:TPU:0, one launch (start us, length us, event | category | flops | bytes accessed | tf_op | source)
XLA Modules:
  0.0 106.4 jit_solution(17661702377630046765)
XLA Ops:
  1.9 0.0 copy-start
  1.9 1.0 copy-done
  2.9 0.7 copy-done.4
  3.6 0.1 prep_images.1
  3.7 1.6 %collective-permute-start.2 = (bf16[208,768]{1,0:T(8,128)(2,1)S(1)}, bf16[208,768]{1,0:T(8,128)(2,1)S(1)}, u32[]{:S(2)}, u32[]{:S(2)}) collective-permute-start(bf16[208,768]{1,0:T(8,128)(2,1)S(1)} %get-tuple-element.44.refs_0_), channel_id=1, source_target_pairs={{0,1},{1,2},{2,3},{3,0},{4,5},{5,6},{6,7},{7,4},{8,9},{9,10},{10,1... | collective-permute-start | bytes 958472 | tf_op jit(solution)/shard_map/ppermute | solution.py:37
  5.4 1.7 %collective-permute-start.1 = (bf16[208,768]{1,0:T(8,128)(2,1)S(1)}, bf16[208,768]{1,0:T(8,128)(2,1)S(1)}, u32[]{:S(2)}, u32[]{:S(2)}) collective-permute-start(bf16[208,768]{1,0:T(8,128)(2,1)S(1)} %get-tuple-element.44.refs_0_), channel_id=1, source_target_pairs={{0,3},{1,0},{2,1},{3,2},{4,7},{5,4},{6,5},{7,6},{8,11},{9,8},{10,9... | collective-permute-start | bytes 958472 | tf_op jit(solution)/shard_map/ppermute | solution.py:37
  7.0 2.0 %collective-permute-start = (bf16[208,768]{1,0:T(8,128)(2,1)S(1)}, bf16[208,768]{1,0:T(8,128)(2,1)S(1)}, u32[]{:S(2)}, u32[]{:S(2)}) collective-permute-start(bf16[208,768]{1,0:T(8,128)(2,1)S(1)} %get-tuple-element.44.refs_0_), channel_id=1, source_target_pairs={{0,16},{1,17},{2,18},{3,19},{4,20},{5,21},{6,22},{7,23},{8,24},{9,... | collective-permute-start | bytes 958472 | tf_op jit(solution)/shard_map/ppermute | solution.py:37
  9.0 1.0 copy-done.2
  10.0 0.1 prep_texts.1.refs_0_
  10.1 3.1 %collective-permute-start.8 = (bf16[192,768]{1,0:T(8,128)(2,1)S(1)}, bf16[192,768]{1,0:T(8,128)(2,1)S(1)}, u32[]{:S(2)}, u32[]{:S(2)}) collective-permute-start(bf16[192,768]{1,0:T(8,128)(2,1)S(1)} %prep_texts.1.refs_0_), channel_id=1, source_target_pairs={{0,96},{1,97},{2,98},{3,99},{4,100},{5,101},{6,102},{7,103},{8,104... | collective-permute-start | bytes 884744 | tf_op jit(solution)/shard_map/ppermute | solution.py:37
  13.2 2.5 %collective-permute-start.7 = (bf16[192,768]{1,0:T(8,128)(2,1)S(1)}, bf16[192,768]{1,0:T(8,128)(2,1)S(1)}, u32[]{:S(2)}, u32[]{:S(2)}) collective-permute-start(bf16[192,768]{1,0:T(8,128)(2,1)S(1)} %prep_texts.1.refs_0_), channel_id=1, source_target_pairs={{0,20},{1,21},{2,22},{3,23},{4,16},{5,17},{6,18},{7,19},{8,28},{9,... | collective-permute-start | bytes 884744 | tf_op jit(solution)/shard_map/ppermute | solution.py:37
  15.7 0.2 collective-permute-start.9
  15.9 0.1 collective-permute-done.refs_0_.refs_1_
  16.0 1.6 %collective-permute-start.3 = (bf16[208,768]{1,0:T(8,128)(2,1)S(1)}, bf16[208,768]{1,0:T(8,128)(2,1)S(1)}, u32[]{:S(2)}, u32[]{:S(2)}) collective-permute-start(bf16[208,768]{1,0:T(8,128)(2,1)S(1)} %gate.3.refs_2_), channel_id=1, source_target_pairs={{0,3},{1,0},{2,1},{3,2},{4,7},{5,4},{6,5},{7,6},{8,11},{9,8},{10,9... | collective-permute-start | bytes 958472 | tf_op jit(solution)/shard_map/ppermute | solution.py:37
  17.6 0.5 collective-permute-start.4
  18.1 0.5 collective-permute-done.8.refs_2_.refs_1_
  18.6 0.3 collective-permute-start.5
  18.9 3.1 %collective-permute-done.7.refs_1_.refs_0_ = bf16[192,768]{1,0:T(8,128)(2,1)S(1)} collective-permute-done((bf16[192,768]{1,0:T(8,128)(2,1)S(1)}, bf16[192,768]{1,0:T(8,128)(2,1)S(1)}, u32[]{:S(2)}, u32[]{:S(2)}) %collective-permute-start.7) | collective-permute-done | bytes 294944 | tf_op jit(solution)/shard_map/ppermute | solution.py:37
  22.1 2.2 %collective-permute-done.9.refs_3_.refs_1_ = bf16[192,768]{1,0:T(8,128)(2,1)S(1)} collective-permute-done((bf16[192,768]{1,0:T(8,128)(2,1)S(1)}, bf16[192,768]{1,0:T(8,128)(2,1)S(1)}, u32[]{:S(2)}, u32[]{:S(2)}) %collective-permute-start.9) | collective-permute-done | bytes 294944 | tf_op jit(solution)/shard_map/ppermute | solution.py:37
  24.3 1.0 collective-permute-start.10
  25.3 1.6 %collective-permute-start.6 = (bf16[208,768]{1,0:T(8,128)(2,1)S(1)}, bf16[208,768]{1,0:T(8,128)(2,1)S(1)}, u32[]{:S(2)}, u32[]{:S(2)}) collective-permute-start(bf16[208,768]{1,0:T(8,128)(2,1)S(1)} %collective-permute-done.3.refs_3_), channel_id=1, source_target_pairs={{0,3},{1,0},{2,1},{3,2},{4,7},{5,4},{6,5},{7,6},{8,11},{9,8},{10,9... | collective-permute-start | bytes 958472 | tf_op jit(solution)/shard_map/ppermute | solution.py:37
  26.9 1.6 %collective-permute-start.11 = (bf16[192,768]{1,0:T(8,128)(2,1)S(1)}, bf16[192,768]{1,0:T(8,128)(2,1)S(1)}, u32[]{:S(2)}, u32[]{:S(2)}) collective-permute-start(bf16[192,768]{1,0:T(8,128)(2,1)S(1)} %gate.5), channel_id=1, source_target_pairs={{0,32},{1,33},{2,34},{3,35},{4,36},{5,37},{6,38},{7,39},{8,40},{9,... | collective-permute-start | bytes 884744 | tf_op jit(solution)/shard_map/ppermute | solution.py:37
  28.5 3.3 %collective-permute-done.10.refs_1_ = bf16[192,768]{1,0:T(8,128)(2,1)S(1)} collective-permute-done((bf16[192,768]{1,0:T(8,128)(2,1)S(1)}, bf16[192,768]{1,0:T(8,128)(2,1)S(1)}, u32[]{:S(2)}, u32[]{:S(2)}) %collective-permute-start.10) | collective-permute-done | bytes 294944 | tf_op jit(solution)/shard_map/ppermute | solution.py:37
  31.8 3.2 %collective-permute-start.13 = (bf16[192,768]{1,0:T(8,128)(2,1)S(1)}, bf16[192,768]{1,0:T(8,128)(2,1)S(1)}, u32[]{:S(2)}, u32[]{:S(2)}) collective-permute-start(bf16[192,768]{1,0:T(8,128)(2,1)S(1)} %collective-permute-done.10.refs_1_), channel_id=1, source_target_pairs={{0,96},{1,97},{2,98},{3,99},{4,100},{5,101},{6,102},{7,103},{8,104... | collective-permute-start | bytes 884744 | tf_op jit(solution)/shard_map/ppermute | solution.py:37
  35.0 0.1 near_images.1
  35.2 0.1 first_texts.1.refs_2_.refs_0_
  35.3 4.4 %score_first.1 = (f32[1536,768]{1,0:T(8,128)S(1)}, bf16[1536,1536]{1,0:T(8,128)(2,1)S(1)}, f32[8,128]{1,0:T(8,128)S(1)}) custom-call(f32[24,128]{1,0:T(8,128)S(1)} %get-tuple-element.43.refs_0_, bf16[1536,768]{1,0:T(8,128)(2,1)S(1)} %get-tuple-element.45.refs_4_.refs_1_.refs_0_, bf16[1536,768]{1,0:T(8,128)(2,1)S(1)} %first_texts.1.refs_2_.refs_0_, ...), custom_call_target="tpu_custom_call" | custom-call | flops 2717908992 | bytes 4194304 | tf_op jit(solution)/shard_map/score_first/pallas_call | solution.py:72
  39.7 2.3 %score_second.1 = (f32[1536,768]{1,0:T(8,128)S(1)}, bf16[1536,1536]{1,0:T(8,128)(2,1)S(1)}, f32[8,128]{1,0:T(8,128)S(1)}) custom-call(f32[24,128]{1,0:T(8,128)S(1)} %get-tuple-element.43.refs_0_, bf16[1536,768]{1,0:T(8,128)(2,1)S(1)} %get-tuple-element.45.refs_4_.refs_1_.refs_0_, ...), custom_call_target="tpu_custom_call", output_to_operand_aliasing={{0}: (5, {}), {1}: (6, {})} | custom-call | flops 1358954496 | bytes 4194304 | tf_op jit(solution)/shard_map/score_second/pallas_call | solution.py:72
  42.1 0.3 collective-permute-start.14
  42.4 0.1 away_images.1
  42.5 6.1 %score_rest.1 = (f32[1536,768]{1,0:T(8,128)S(1)}, bf16[1536,1536]{1,0:T(8,128)(2,1)S(1)}, f32[8,128]{1,0:T(8,128)S(1)}) custom-call(f32[24,128]{1,0:T(8,128)S(1)} %get-tuple-element.43.refs_0_, bf16[1536,768]{1,0:T(8,128)(2,1)S(1)} %get-tuple-element.51.refs_1_, ...), custom_call_target="tpu_custom_call", output_to_operand_aliasing={{0}: (5, {}), {1}: (6, {})} | custom-call | flops 3170893824 | bytes 4194304 | tf_op jit(solution)/shard_map/score_rest/pallas_call | solution.py:72
  48.7 10.4 %score_sib.1 = (bf16[1552,768]{1,0:T(8,128)(2,1)S(1)}, bf16[1536,1536]{1,0:T(8,128)(2,1)S(1)}, f32[8,128]{1,0:T(8,128)S(1)}) custom-call(f32[24,128]{1,0:T(8,128)S(1)} %get-tuple-element.43.refs_0_, bf16[1536,768]{1,0:T(8,128)(2,1)S(1)} %get-tuple-element.51.refs_1_, bf16[1536,768]{1,0:T(8,128)(2,1)S(1)} %collective-permute-done.14.refs_2_.refs_3_, ...), custom_call_target="tpu_custom_call" | custom-call | flops 7247757312 | bytes 4194304 | tf_op jit(solution)/shard_map/score_sib/pallas_call | solution.py:72
  59.1 0.6 collective-permute-start.15
  59.7 2.0 %image_away.1 = (bf16[192,768]{1,0:T(8,128)(2,1)S(1)}, bf16[192,768]{1,0:T(8,128)(2,1)S(1)}) custom-call(bf16[1536,1536]{1,0:T(8,128)(2,1)S(1)} %get-tuple-element.59.refs_0_, bf16[1536,1536]{1,0:T(8,128)(2,1)S(1)} %get-tuple-element.60.refs_1_, bf16[1536,768]{1,0:T(8,128)(2,1)S(1)} %away_texts.1.refs_2_, ...), custom_call_target="tpu_custom_call" | custom-call | flops 905969664 | bytes 4194304 | tf_op jit(solution)/shard_map/image_away/pallas_call | solution.py:72
  61.8 0.3 collective-permute-start.18
  62.1 3.0 %collective-permute-start.19 = (bf16[192,768]{1,0:T(8,128)(2,1)S(1)}, bf16[192,768]{1,0:T(8,128)(2,1)S(1)}, u32[]{:S(2)}, u32[]{:S(2)}) collective-permute-start(bf16[192,768]{1,0:T(8,128)(2,1)S(1)} %get-tuple-element.62.refs_4_), channel_id=1, source_target_pairs={{0,3},{1,0},{2,1},{3,2},{4,7},{5,4},{6,5},{7,6},{8,11},{9,8},{10,9... | collective-permute-start | bytes 884744 | tf_op jit(solution)/shard_map/ppermute | solution.py:37
  65.1 0.6 add.13
  65.7 0.1 collective-permute-start.16
  65.7 3.2 %collective-permute-start.17 = (bf16[208,768]{1,0:T(8,128)(2,1)S(1)}, bf16[208,768]{1,0:T(8,128)(2,1)S(1)}, u32[]{:S(2)}, u32[]{:S(2)}) collective-permute-start(bf16[208,768]{1,0:T(8,128)(2,1)S(1)} %get-tuple-element.67), channel_id=1, source_target_pairs={{0,96},{1,97},{2,98},{3,99},{4,100},{5,101},{6,102},{7,103},{8,104... | collective-permute-start | bytes 958472 | tf_op jit(solution)/shard_map/ppermute | solution.py:37
  69.0 3.9 %image_ring.1 = (f32[384,768]{1,0:T(8,128)S(1)}, f32[384,768]{1,0:T(8,128)S(1)}) custom-call(bf16[1536,1536]{1,0:T(8,128)(2,1)S(1)} %get-tuple-element.59.refs_0_, bf16[1536,1536]{1,0:T(8,128)(2,1)S(1)} %get-tuple-element.60.refs_1_, bf16[1536,768]{1,0:T(8,128)(2,1)S(1)} %away_texts.1.refs_2_, bf16[1536,768]{1,0:T(8,128)(2,1)S(1)} %collective-permute-done.14.refs_2_.refs_3_), custom_call_target="tpu_custom_call" | custom-call | flops 1811939328 | bytes 4194304 | tf_op jit(solution)/shard_map/image_ring/pallas_call | solution.py:72
  72.9 0.2 turn.2
  73.0 2.1 %collective-permute-start.24 = (bf16[384,768]{1,0:T(8,128)(2,1)S(1)}, bf16[384,768]{1,0:T(8,128)(2,1)S(1)}, u32[]{:S(2)}, u32[]{:S(2)}) collective-permute-start(bf16[384,768]{1,0:T(8,128)(2,1)S(1)} %get-tuple-element.76), channel_id=1, source_target_pairs={{0,3},{1,0},{2,1},{3,2},{4,7},{5,4},{6,5},{7,6},{8,11},{9,8},{10,9... | collective-permute-start | bytes 1769480 | tf_op jit(solution)/shard_map/ppermute | solution.py:37
  75.2 0.7 collective-permute-done.16.refs_2_
  75.8 0.2 turn.3
  76.0 0.1 collective-permute-start.20
  76.1 3.2 %collective-permute-start.21 = (bf16[384,768]{1,0:T(8,128)(2,1)S(1)}, bf16[384,768]{1,0:T(8,128)(2,1)S(1)}, u32[]{:S(2)}, u32[]{:S(2)}) collective-permute-start(bf16[384,768]{1,0:T(8,128)(2,1)S(1)} %get-tuple-element.73), channel_id=1, source_target_pairs={{0,96},{1,97},{2,98},{3,99},{4,100},{5,101},{6,102},{7,103},{8,104... | collective-permute-start | bytes 1769480 | tf_op jit(solution)/shard_map/ppermute | solution.py:37
  79.3 0.8 collective-permute-start.25
  80.1 2.8 %collective-permute-done.25 = f32[8,128]{1,0:T(8,128)S(1)} collective-permute-done((f32[8,128]{1,0:T(8,128)S(1)}, f32[8,128]{1,0:T(8,128)S(1)}, u32[]{:S(2)}, u32[]{:S(2)}) %collective-permute-start.25) | collective-permute-done | bytes 4128 | tf_op jit(solution)/shard_map/ppermute | solution.py:37
  83.0 3.0 %collective-permute-start.26 = (f32[8,128]{1,0:T(8,128)S(1)}, f32[8,128]{1,0:T(8,128)S(1)}, u32[]{:S(2)}, u32[]{:S(2)}) collective-permute-start(f32[8,128]{1,0:T(8,128)S(1)} %add.10), channel_id=1, source_target_pairs={{0,20},{1,21},{2,22},{3,23},{4,16},{5,17},{6,18},{7,19},{8,28},{9,... | collective-permute-start | bytes 12296 | tf_op jit(solution)/shard_map/ppermute | solution.py:37
  86.0 1.8 %collective-permute-done.26 = f32[8,128]{1,0:T(8,128)S(1)} collective-permute-done((f32[8,128]{1,0:T(8,128)S(1)}, f32[8,128]{1,0:T(8,128)S(1)}, u32[]{:S(2)}, u32[]{:S(2)}) %collective-permute-start.26) | collective-permute-done | bytes 4128 | tf_op jit(solution)/shard_map/ppermute | solution.py:37
  87.8 0.0 collective-permute-start.27
  87.8 2.0 %image_near.1 = (f32[192,768]{1,0:T(8,128)S(1)}, f32[192,768]{1,0:T(8,128)S(1)}) custom-call(bf16[1536,1536]{1,0:T(8,128)(2,1)S(1)} %get-tuple-element.59.refs_0_, bf16[1536,1536]{1,0:T(8,128)(2,1)S(1)} %get-tuple-element.60.refs_1_, bf16[1536,768]{1,0:T(8,128)(2,1)S(1)} %away_texts.1.refs_2_, bf16[1536,768]{1,0:T(8,128)(2,1)S(1)} %collective-permute-done.14.refs_2_.refs_3_), custom_call_target="tpu_custom_call" | custom-call | flops 905969664 | bytes 4194304 | tf_op jit(solution)/shard_map/image_near/pallas_call | solution.py:72
  89.9 0.3 collective-permute-done.23.refs_1_.refs_2_
  90.2 1.2 %collective-permute-done.27.refs_4_ = f32[8,128]{1,0:T(8,128)S(1)} collective-permute-done((f32[8,128]{1,0:T(8,128)S(1)}, f32[8,128]{1,0:T(8,128)S(1)}, u32[]{:S(2)}, u32[]{:S(2)}) %collective-permute-start.27) | collective-permute-done | bytes 4128 | tf_op jit(solution)/shard_map/ppermute | solution.py:37
  91.4 0.1 far.3
  91.5 0.1 collective-permute-start.30
  91.6 0.1 far.2
  91.7 3.1 %collective-permute-start.22 = (bf16[192,768]{1,0:T(8,128)(2,1)S(1)}, bf16[192,768]{1,0:T(8,128)(2,1)S(1)}, u32[]{:S(2)}, u32[]{:S(2)}) collective-permute-start(bf16[192,768]{1,0:T(8,128)(2,1)S(1)} %far.2), channel_id=1, source_target_pairs={{0,20},{1,21},{2,22},{3,23},{4,16},{5,17},{6,18},{7,19},{8,28},{9,... | collective-permute-start | bytes 884744 | tf_op jit(solution)/shard_map/ppermute | solution.py:37
  94.8 2.5 %collective-permute-start.28 = (f32[8,128]{1,0:T(8,128)S(1)}, f32[8,128]{1,0:T(8,128)S(1)}, u32[]{:S(2)}, u32[]{:S(2)}) collective-permute-start(f32[8,128]{1,0:T(8,128)S(1)} %get-tuple-element.78), channel_id=1, source_target_pairs={{0,2},{1,3},{2,0},{3,1},{4,6},{5,7},{6,4},{7,5},{8,10},{9,11},{10,... | collective-permute-start | bytes 12296 | tf_op jit(solution)/shard_map/ppermute | solution.py:37
  97.3 2.6 %collective-permute-done.28 = f32[8,128]{1,0:T(8,128)S(1)} collective-permute-done((f32[8,128]{1,0:T(8,128)S(1)}, f32[8,128]{1,0:T(8,128)S(1)}, u32[]{:S(2)}, u32[]{:S(2)}) %collective-permute-start.28) | collective-permute-done | bytes 4128 | tf_op jit(solution)/shard_map/ppermute | solution.py:37
  99.9 2.1 %collective-permute-start.29 = (f32[8,128]{1,0:T(8,128)S(1)}, f32[8,128]{1,0:T(8,128)S(1)}, u32[]{:S(2)}, u32[]{:S(2)}) collective-permute-start(f32[8,128]{1,0:T(8,128)S(1)} %add.12.loss), channel_id=1, source_target_pairs={{0,64},{1,65},{2,66},{3,67},{4,68},{5,69},{6,70},{7,71},{8,72},{9,... | collective-permute-start | bytes 12296 | tf_op jit(solution)/shard_map/ppermute | solution.py:37
  102.0 1.1 %unproject.3 = f32[192,768]{1,0:T(8,128)} custom-call(bf16[192,768]{1,0:T(8,128)(2,1)S(1)} %copy-done.1, f32[192,768]{1,0:T(8,128)S(1)} %get-tuple-element.80.refs_1_, bf16[384,768]{1,0:T(8,128)(2,1)S(1)} %collective-permute-done.23.refs_1_.refs_2_, bf16[384,768]{1,0:T(8,128)(2,1)S(1)} %collective-permute-done.24.refs_2_.refs_3_, ...), custom_call_target="tpu_custom_call" | custom-call | bytes 4194304 | tf_op jit(solution)/shard_map/unproject/pallas_call | solution.py:72
  103.2 1.9 %collective-permute-done.29.step = f32[8,128]{1,0:T(8,128)S(1)} collective-permute-done((f32[8,128]{1,0:T(8,128)S(1)}, f32[8,128]{1,0:T(8,128)S(1)}, u32[]{:S(2)}, u32[]{:S(2)}) %collective-permute-start.29) | collective-permute-done | bytes 4128 | tf_op jit(solution)/shard_map/ppermute | solution.py:37
  105.0 1.1 %unproject.2 = (f32[192,768]{1,0:T(8,128)}, f32[1]{0:T(128)}) custom-call(bf16[192,768]{1,0:T(8,128)(2,1)S(1)} %copy-done.3, f32[192,768]{1,0:T(8,128)S(1)} %get-tuple-element.63.own_ref, bf16[384,768]{1,0:T(8,128)(2,1)S(1)} %collective-permute-done.20.refs_1_.plus, bf16[384,768]{1,0:T(8,128)(2,1)S(1)} %collective-permute-done.21.refs_2_.minus, ...), custom_call_target="tpu_custom_call" | custom-call | tf_op jit(solution)/shard_map/unproject/pallas_call | solution.py:385
  (35 shorter events, 0.2 us)
Async XLA Ops:
  1.9 1.0 copy-start
  2.9 0.7 copy-start.4
  3.7 12.0 %collective-permute-start.2 = (bf16[208,768]{1,0:T(8,128)(2,1)S(1)}, bf16[208,768]{1,0:T(8,128)(2,1)S(1)}, u32[]{:S(2)}, u32[]{:S(2)}) collective-permute-start(bf16[208,768]{1,0:T(8,128)(2,1)S(1)} %get-tuple-element.44.refs_0_), channel_id=1, source_target_pairs={{0,1},{1,2},{2,3},{3,0},{4,5},{5,6},{6,7},{7,4},{8,9},{9,10},{10,1... | collective-permute-start | bytes 958472 | tf_op jit(solution)/shard_map/ppermute | solution.py:37
  5.4 10.6 %collective-permute-start.1 = (bf16[208,768]{1,0:T(8,128)(2,1)S(1)}, bf16[208,768]{1,0:T(8,128)(2,1)S(1)}, u32[]{:S(2)}, u32[]{:S(2)}) collective-permute-start(bf16[208,768]{1,0:T(8,128)(2,1)S(1)} %get-tuple-element.44.refs_0_), channel_id=1, source_target_pairs={{0,3},{1,0},{2,1},{3,2},{4,7},{5,4},{6,5},{7,6},{8,11},{9,8},{10,9... | collective-permute-start | bytes 958472 | tf_op jit(solution)/shard_map/ppermute | solution.py:37
  7.0 9.0 %collective-permute-start = (bf16[208,768]{1,0:T(8,128)(2,1)S(1)}, bf16[208,768]{1,0:T(8,128)(2,1)S(1)}, u32[]{:S(2)}, u32[]{:S(2)}) collective-permute-start(bf16[208,768]{1,0:T(8,128)(2,1)S(1)} %get-tuple-element.44.refs_0_), channel_id=1, source_target_pairs={{0,16},{1,17},{2,18},{3,19},{4,20},{5,21},{6,22},{7,23},{8,24},{9,... | collective-permute-start | bytes 958472 | tf_op jit(solution)/shard_map/ppermute | solution.py:37
  9.0 1.0 copy-start.2
  10.1 8.5 %collective-permute-start.8 = (bf16[192,768]{1,0:T(8,128)(2,1)S(1)}, bf16[192,768]{1,0:T(8,128)(2,1)S(1)}, u32[]{:S(2)}, u32[]{:S(2)}) collective-permute-start(bf16[192,768]{1,0:T(8,128)(2,1)S(1)} %prep_texts.1.refs_0_), channel_id=1, source_target_pairs={{0,96},{1,97},{2,98},{3,99},{4,100},{5,101},{6,102},{7,103},{8,104... | collective-permute-start | bytes 884744 | tf_op jit(solution)/shard_map/ppermute | solution.py:37
  13.2 8.8 %collective-permute-start.7 = (bf16[192,768]{1,0:T(8,128)(2,1)S(1)}, bf16[192,768]{1,0:T(8,128)(2,1)S(1)}, u32[]{:S(2)}, u32[]{:S(2)}) collective-permute-start(bf16[192,768]{1,0:T(8,128)(2,1)S(1)} %prep_texts.1.refs_0_), channel_id=1, source_target_pairs={{0,20},{1,21},{2,22},{3,23},{4,16},{5,17},{6,18},{7,19},{8,28},{9,... | collective-permute-start | bytes 884744 | tf_op jit(solution)/shard_map/ppermute | solution.py:37
  15.7 8.6 %collective-permute-start.9 = (bf16[192,768]{1,0:T(8,128)(2,1)S(1)}, bf16[192,768]{1,0:T(8,128)(2,1)S(1)}, u32[]{:S(2)}, u32[]{:S(2)}) collective-permute-start(bf16[192,768]{1,0:T(8,128)(2,1)S(1)} %prep_texts.1.refs_0_), channel_id=1, source_target_pairs={{0,32},{1,33},{2,34},{3,35},{4,36},{5,37},{6,38},{7,39},{8,40},{9,... | collective-permute-start | bytes 884744 | tf_op jit(solution)/shard_map/ppermute | solution.py:37
  16.0 9.3 %collective-permute-start.3 = (bf16[208,768]{1,0:T(8,128)(2,1)S(1)}, bf16[208,768]{1,0:T(8,128)(2,1)S(1)}, u32[]{:S(2)}, u32[]{:S(2)}) collective-permute-start(bf16[208,768]{1,0:T(8,128)(2,1)S(1)} %gate.3.refs_2_), channel_id=1, source_target_pairs={{0,3},{1,0},{2,1},{3,2},{4,7},{5,4},{6,5},{7,6},{8,11},{9,8},{10,9... | collective-permute-start | bytes 958472 | tf_op jit(solution)/shard_map/ppermute | solution.py:37
  17.6 14.2 %collective-permute-start.4 = (bf16[208,768]{1,0:T(8,128)(2,1)S(1)}, bf16[208,768]{1,0:T(8,128)(2,1)S(1)}, u32[]{:S(2)}, u32[]{:S(2)}) collective-permute-start(bf16[208,768]{1,0:T(8,128)(2,1)S(1)} %gate.3.refs_2_), channel_id=1, source_target_pairs={{0,1},{1,2},{2,3},{3,0},{4,5},{5,6},{6,7},{7,4},{8,9},{9,10},{10,1... | collective-permute-start | bytes 958472 | tf_op jit(solution)/shard_map/ppermute | solution.py:37
  18.6 16.5 %collective-permute-start.5 = (bf16[208,768]{1,0:T(8,128)(2,1)S(1)}, bf16[208,768]{1,0:T(8,128)(2,1)S(1)}, u32[]{:S(2)}, u32[]{:S(2)}) collective-permute-start(bf16[208,768]{1,0:T(8,128)(2,1)S(1)} %collective-permute-done.2.refs_2_.refs_4_), channel_id=1, source_target_pairs={{0,1},{1,2},{2,3},{3,0},{4,5},{5,6},{6,7},{7,4},{8,9},{9,10},{10,1... | collective-permute-start | bytes 958472 | tf_op jit(solution)/shard_map/ppermute | solution.py:37
  24.3 7.5 %collective-permute-start.10 = (bf16[192,768]{1,0:T(8,128)(2,1)S(1)}, bf16[192,768]{1,0:T(8,128)(2,1)S(1)}, u32[]{:S(2)}, u32[]{:S(2)}) collective-permute-start(bf16[192,768]{1,0:T(8,128)(2,1)S(1)} %gate.5), channel_id=1, source_target_pairs={{0,96},{1,97},{2,98},{3,99},{4,100},{5,101},{6,102},{7,103},{8,104... | collective-permute-start | bytes 884744 | tf_op jit(solution)/shard_map/ppermute | solution.py:37
  25.3 14.3 %collective-permute-start.6 = (bf16[208,768]{1,0:T(8,128)(2,1)S(1)}, bf16[208,768]{1,0:T(8,128)(2,1)S(1)}, u32[]{:S(2)}, u32[]{:S(2)}) collective-permute-start(bf16[208,768]{1,0:T(8,128)(2,1)S(1)} %collective-permute-done.3.refs_3_), channel_id=1, source_target_pairs={{0,3},{1,0},{2,1},{3,2},{4,7},{5,4},{6,5},{7,6},{8,11},{9,8},{10,9... | collective-permute-start | bytes 958472 | tf_op jit(solution)/shard_map/ppermute | solution.py:37
  26.9 12.7 %collective-permute-start.11 = (bf16[192,768]{1,0:T(8,128)(2,1)S(1)}, bf16[192,768]{1,0:T(8,128)(2,1)S(1)}, u32[]{:S(2)}, u32[]{:S(2)}) collective-permute-start(bf16[192,768]{1,0:T(8,128)(2,1)S(1)} %gate.5), channel_id=1, source_target_pairs={{0,32},{1,33},{2,34},{3,35},{4,36},{5,37},{6,38},{7,39},{8,40},{9,... | collective-permute-start | bytes 884744 | tf_op jit(solution)/shard_map/ppermute | solution.py:37
  31.8 10.3 %collective-permute-start.12 = (bf16[192,768]{1,0:T(8,128)(2,1)S(1)}, bf16[192,768]{1,0:T(8,128)(2,1)S(1)}, u32[]{:S(2)}, u32[]{:S(2)}) collective-permute-start(bf16[192,768]{1,0:T(8,128)(2,1)S(1)} %collective-permute-done.9.refs_3_.refs_1_), channel_id=1, source_target_pairs={{0,32},{1,33},{2,34},{3,35},{4,36},{5,37},{6,38},{7,39},{8,40},{9,... | collective-permute-start | bytes 884744 | tf_op jit(solution)/shard_map/ppermute | solution.py:37
  31.8 10.3 %collective-permute-start.13 = (bf16[192,768]{1,0:T(8,128)(2,1)S(1)}, bf16[192,768]{1,0:T(8,128)(2,1)S(1)}, u32[]{:S(2)}, u32[]{:S(2)}) collective-permute-start(bf16[192,768]{1,0:T(8,128)(2,1)S(1)} %collective-permute-done.10.refs_1_), channel_id=1, source_target_pairs={{0,96},{1,97},{2,98},{3,99},{4,100},{5,101},{6,102},{7,103},{8,104... | collective-permute-start | bytes 884744 | tf_op jit(solution)/shard_map/ppermute | solution.py:37
  42.1 6.5 %collective-permute-start.14 = (bf16[1536,768]{1,0:T(8,128)(2,1)S(1)}, bf16[1536,768]{1,0:T(8,128)(2,1)S(1)}, u32[]{:S(2)}, u32[]{:S(2)}) collective-permute-start(bf16[1536,768]{1,0:T(8,128)(2,1)S(1)} %away_texts.1.refs_2_), channel_id=1, source_target_pairs={{0,8},{1,9},{2,10},{3,11},{4,12},{5,13},{6,14},{7,15},{8,0},{9,1},... | collective-permute-start | bytes 7077896 | tf_op jit(solution)/shard_map/ppermute | solution.py:37
  59.1 5.9 %collective-permute-start.15 = (bf16[1552,768]{1,0:T(8,128)(2,1)S(1)}, bf16[1552,768]{1,0:T(8,128)(2,1)S(1)}, u32[]{:S(2)}, u32[]{:S(2)}) collective-permute-start(bf16[1552,768]{1,0:T(8,128)(2,1)S(1)} %get-tuple-element.57), channel_id=1, source_target_pairs={{0,8},{1,9},{2,10},{3,11},{4,12},{5,13},{6,14},{7,15},{8,0},{9,1},... | collective-permute-start | bytes 7151624 | tf_op jit(solution)/shard_map/ppermute | solution.py:37
  61.8 11.1 %collective-permute-start.18 = (bf16[192,768]{1,0:T(8,128)(2,1)S(1)}, bf16[192,768]{1,0:T(8,128)(2,1)S(1)}, u32[]{:S(2)}, u32[]{:S(2)}) collective-permute-start(bf16[192,768]{1,0:T(8,128)(2,1)S(1)} %get-tuple-element.61.refs_3_), channel_id=1, source_target_pairs={{0,1},{1,2},{2,3},{3,0},{4,5},{5,6},{6,7},{7,4},{8,9},{9,10},{10,1... | collective-permute-start | bytes 884744 | tf_op jit(solution)/shard_map/ppermute | solution.py:37
  62.1 10.8 %collective-permute-start.19 = (bf16[192,768]{1,0:T(8,128)(2,1)S(1)}, bf16[192,768]{1,0:T(8,128)(2,1)S(1)}, u32[]{:S(2)}, u32[]{:S(2)}) collective-permute-start(bf16[192,768]{1,0:T(8,128)(2,1)S(1)} %get-tuple-element.62.refs_4_), channel_id=1, source_target_pairs={{0,3},{1,0},{2,1},{3,2},{4,7},{5,4},{6,5},{7,6},{8,11},{9,8},{10,9... | collective-permute-start | bytes 884744 | tf_op jit(solution)/shard_map/ppermute | solution.py:37
  65.7 10.2 %collective-permute-start.16 = (bf16[208,768]{1,0:T(8,128)(2,1)S(1)}, bf16[208,768]{1,0:T(8,128)(2,1)S(1)}, u32[]{:S(2)}, u32[]{:S(2)}) collective-permute-start(bf16[208,768]{1,0:T(8,128)(2,1)S(1)} %get-tuple-element.66), channel_id=1, source_target_pairs={{0,32},{1,33},{2,34},{3,35},{4,36},{5,37},{6,38},{7,39},{8,40},{9,... | collective-permute-start | bytes 958472 | tf_op jit(solution)/shard_map/ppermute | solution.py:37
  65.7 10.1 %collective-permute-start.17 = (bf16[208,768]{1,0:T(8,128)(2,1)S(1)}, bf16[208,768]{1,0:T(8,128)(2,1)S(1)}, u32[]{:S(2)}, u32[]{:S(2)}) collective-permute-start(bf16[208,768]{1,0:T(8,128)(2,1)S(1)} %get-tuple-element.67), channel_id=1, source_target_pairs={{0,96},{1,97},{2,98},{3,99},{4,100},{5,101},{6,102},{7,103},{8,104... | collective-permute-start | bytes 958472 | tf_op jit(solution)/shard_map/ppermute | solution.py:37
  73.0 16.8 %collective-permute-start.24 = (bf16[384,768]{1,0:T(8,128)(2,1)S(1)}, bf16[384,768]{1,0:T(8,128)(2,1)S(1)}, u32[]{:S(2)}, u32[]{:S(2)}) collective-permute-start(bf16[384,768]{1,0:T(8,128)(2,1)S(1)} %get-tuple-element.76), channel_id=1, source_target_pairs={{0,3},{1,0},{2,1},{3,2},{4,7},{5,4},{6,5},{7,6},{8,11},{9,8},{10,9... | collective-permute-start | bytes 1769480 | tf_op jit(solution)/shard_map/ppermute | solution.py:37
  75.2 15.0 %collective-permute-start.23 = (bf16[384,768]{1,0:T(8,128)(2,1)S(1)}, bf16[384,768]{1,0:T(8,128)(2,1)S(1)}, u32[]{:S(2)}, u32[]{:S(2)}) collective-permute-start(bf16[384,768]{1,0:T(8,128)(2,1)S(1)} %get-tuple-element.71.refs_5_), channel_id=1, source_target_pairs={{0,1},{1,2},{2,3},{3,0},{4,5},{5,6},{6,7},{7,4},{8,9},{9,10},{10,1... | collective-permute-start | bytes 1769480 | tf_op jit(solution)/shard_map/ppermute | solution.py:37
  76.0 15.5 %collective-permute-start.20 = (bf16[384,768]{1,0:T(8,128)(2,1)S(1)}, bf16[384,768]{1,0:T(8,128)(2,1)S(1)}, u32[]{:S(2)}, u32[]{:S(2)}) collective-permute-start(bf16[384,768]{1,0:T(8,128)(2,1)S(1)} %get-tuple-element.72), channel_id=1, source_target_pairs={{0,32},{1,33},{2,34},{3,35},{4,36},{5,37},{6,38},{7,39},{8,40},{9,... | collective-permute-start | bytes 1769480 | tf_op jit(solution)/shard_map/ppermute | solution.py:37
  76.1 15.5 %collective-permute-start.21 = (bf16[384,768]{1,0:T(8,128)(2,1)S(1)}, bf16[384,768]{1,0:T(8,128)(2,1)S(1)}, u32[]{:S(2)}, u32[]{:S(2)}) collective-permute-start(bf16[384,768]{1,0:T(8,128)(2,1)S(1)} %get-tuple-element.73), channel_id=1, source_target_pairs={{0,96},{1,97},{2,98},{3,99},{4,100},{5,101},{6,102},{7,103},{8,104... | collective-permute-start | bytes 1769480 | tf_op jit(solution)/shard_map/ppermute | solution.py:37
  79.3 3.6 %collective-permute-start.25 = (f32[8,128]{1,0:T(8,128)S(1)}, f32[8,128]{1,0:T(8,128)S(1)}, u32[]{:S(2)}, u32[]{:S(2)}) collective-permute-start(f32[8,128]{1,0:T(8,128)S(1)} %get-tuple-element.77), channel_id=1, source_target_pairs={{0,16},{1,17},{2,18},{3,19},{4,20},{5,21},{6,22},{7,23},{8,24},{9,... | collective-permute-start | bytes 12296 | tf_op jit(solution)/shard_map/ppermute | solution.py:37
  83.0 4.8 %collective-permute-start.26 = (f32[8,128]{1,0:T(8,128)S(1)}, f32[8,128]{1,0:T(8,128)S(1)}, u32[]{:S(2)}, u32[]{:S(2)}) collective-permute-start(f32[8,128]{1,0:T(8,128)S(1)} %add.10), channel_id=1, source_target_pairs={{0,20},{1,21},{2,22},{3,23},{4,16},{5,17},{6,18},{7,19},{8,28},{9,... | collective-permute-start | bytes 12296 | tf_op jit(solution)/shard_map/ppermute | solution.py:37
  87.8 3.6 %collective-permute-start.27 = (f32[8,128]{1,0:T(8,128)S(1)}, f32[8,128]{1,0:T(8,128)S(1)}, u32[]{:S(2)}, u32[]{:S(2)}) collective-permute-start(f32[8,128]{1,0:T(8,128)S(1)} %add.11.refs_3_), channel_id=1, source_target_pairs={{0,1},{1,0},{2,3},{3,2},{4,5},{5,4},{6,7},{7,6},{8,9},{9,8},{10,11... | collective-permute-start | bytes 12296 | tf_op jit(solution)/shard_map/ppermute | solution.py:37
  89.8 12.2 %copy-start.1 = (bf16[192,768]{1,0:T(8,128)(2,1)S(1)}, bf16[192,768]{1,0:T(8,128)(2,1)}, u32[]{:S(2)}) copy-start(bf16[192,768]{1,0:T(8,128)(2,1)} %refs_0_.4) | copy-start | bytes 884740
  91.5 10.6 %collective-permute-start.30 = (bf16[192,768]{1,0:T(8,128)(2,1)S(1)}, bf16[192,768]{1,0:T(8,128)(2,1)S(1)}, u32[]{:S(2)}, u32[]{:S(2)}) collective-permute-start(bf16[192,768]{1,0:T(8,128)(2,1)S(1)} %get-tuple-element.81), channel_id=1, source_target_pairs={{0,16},{1,17},{2,18},{3,19},{4,20},{5,21},{6,22},{7,23},{8,24},{9,... | collective-permute-start | bytes 884744 | tf_op jit(solution)/shard_map/ppermute | solution.py:37
  91.6 13.4 %copy-start.3 = (bf16[192,768]{1,0:T(8,128)(2,1)S(1)}, bf16[192,768]{1,0:T(8,128)(2,1)}, u32[]{:S(2)}) copy-start(bf16[192,768]{1,0:T(8,128)(2,1)} %values_ref.1) | copy-start | bytes 884740
  91.7 13.3 %collective-permute-start.22 = (bf16[192,768]{1,0:T(8,128)(2,1)S(1)}, bf16[192,768]{1,0:T(8,128)(2,1)S(1)}, u32[]{:S(2)}, u32[]{:S(2)}) collective-permute-start(bf16[192,768]{1,0:T(8,128)(2,1)S(1)} %far.2), channel_id=1, source_target_pairs={{0,20},{1,21},{2,22},{3,23},{4,16},{5,17},{6,18},{7,19},{8,28},{9,... | collective-permute-start | bytes 884744 | tf_op jit(solution)/shard_map/ppermute | solution.py:37
  94.8 5.1 %collective-permute-start.28 = (f32[8,128]{1,0:T(8,128)S(1)}, f32[8,128]{1,0:T(8,128)S(1)}, u32[]{:S(2)}, u32[]{:S(2)}) collective-permute-start(f32[8,128]{1,0:T(8,128)S(1)} %get-tuple-element.78), channel_id=1, source_target_pairs={{0,2},{1,3},{2,0},{3,1},{4,6},{5,7},{6,4},{7,5},{8,10},{9,11},{10,... | collective-permute-start | bytes 12296 | tf_op jit(solution)/shard_map/ppermute | solution.py:37
  99.9 5.1 %collective-permute-start.29 = (f32[8,128]{1,0:T(8,128)S(1)}, f32[8,128]{1,0:T(8,128)S(1)}, u32[]{:S(2)}, u32[]{:S(2)}) collective-permute-start(f32[8,128]{1,0:T(8,128)S(1)} %add.12.loss), channel_id=1, source_target_pairs={{0,64},{1,65},{2,66},{3,67},{4,68},{5,69},{6,70},{7,71},{8,72},{9,... | collective-permute-start | bytes 12296 | tf_op jit(solution)/shard_map/ppermute | solution.py:37

commit v6 on v5

--- a/solution.py
+++ b/solution.py
@@ -274,8 +274,7 @@
     out_ref[...] = (grad - unit * along) * inverse
 
 
-def final_loss_kernel(values_ref, own_ref, plus, minus, zed, loss, step, out_ref, loss_out):
-    final_kernel(values_ref, own_ref, plus, minus, zed, out_ref)
+def loss_kernel(loss, step, grad_x, grad_y, loss_out):
     loss_out[0] = (loss[0, 0] + step[0, 0]) * (1.0 / (LOG2E * R * N_ROW * N_COL))
 
 
@@ -382,14 +381,15 @@
 
     grad = ((R, D), F32)
     grad_x = call(final_kernel, [grad], images, gx_near[0], gx_plus, gx_minus, gx_far, name="unproject")[0]
-    grad_y, loss = pl.pallas_call(
-        final_loss_kernel,
-        in_specs=[VMEM] * 7,
-        out_specs=[VMEM, SMEM],
-        out_shape=[jax.ShapeDtypeStruct((R, D), F32), jax.ShapeDtypeStruct((1,), F32)],
-        compiler_params=pltpu.CompilerParams(vmem_limit_bytes=8 << 20),
-        name="unproject",
-    )(texts, gy_near[0], gy_plus, gy_minus, gy_far, loss, step)
+    grad_y = call(final_kernel, [grad], texts, gy_near[0], gy_plus, gy_minus, gy_far, name="unproject")[0]
+    loss = pl.pallas_call(
+        loss_kernel,
+        in_specs=[VMEM] * 2 + [pl.BlockSpec(memory_space=pl.ANY)] * 2,
+        out_specs=SMEM,
+        out_shape=jax.ShapeDtypeStruct((1,), F32),
+        compiler_params=pltpu.CompilerParams(vmem_limit_bytes=1 << 20),
+        name="loss",
+    )(loss, step, grad_x, grad_y)
     return loss, grad_x, grad_y
 
 

time: 107 us -> 108 us (level)
  starting transfers between devices: 45.4 us -> 43.5 us
  waiting for transfers between devices: 20.5 us -> 21.8 us
    ppermute x31, starting transfers between devices: 45.4 us -> 43.5 us  [send(): return lax.ppermute(value, ('row', 'col'), pairs)]
    ppermute x31, waiting for transfers between devices: 20.5 us -> 21.8 us  [send(): return lax.ppermute(value, ('row', 'col'), pairs)]
    pallas_call x23 -> x24, Pallas kernels: 34.3 us -> 35.4 us  [call(): pl.pallas_call(body, in_specs=[SMEM] * scalars + [VMEM] * (count - scalar...]
    unnamed x10 -> x14, local copies, waits for them, and re-layouts: 2.61 us -> 3.68 us
  transfers between devices with their start and end apart: 31 -> 31, of which waited for: 12 -> 12; matrix products, arithmetic and copies ran while one was open for 0% -> 0% of each run, Pallas kernels for 22% -> 23%
where the time goes in v6:
time: 108 us; the launch traced here: 107 us
  starting transfers between devices  43.5 us (40%)
  Pallas kernels  36 us (33%)
  waiting for transfers between devices  21.8 us (20%)
  local copies, waits for them, and re-layouts  3.68 us (3%)
  between operations  2.33 us (2%)
    ppermute x31, starting transfers between devices, send(): return lax.ppermute(value, ('row', 'col'), pairs)  43.5 us
    pallas_call x24, Pallas kernels, call(): pl.pallas_call(body, in_specs=[SMEM] * scalars + [VMEM] * (count - scalar...  35.4 us
    ppermute x31, waiting for transfers between devices, send(): return lax.ppermute(value, ('row', 'col'), pairs)  21.8 us
    unnamed x14, local copies, waits for them, and re-layouts  3.68 us
  transfers between devices with their start and end apart: 31, of which 12 were waited for; matrix products, arithmetic and copies ran while one was open for 0% of the time, Pallas kernels for 23%

profile of v6, /device:TPU:0, one launch (start us, length us, event | category | flops | bytes accessed | tf_op | source)
XLA Modules:
  0.0 107.3 jit_solution(11786564243294813493)
XLA Ops:
  1.9 1.0 copy-done.2
  2.9 0.7 copy-done.6
  3.6 0.1 prep_images.1
  3.7 2.1 %collective-permute-start = (bf16[208,768]{1,0:T(8,128)(2,1)S(1)}, bf16[208,768]{1,0:T(8,128)(2,1)S(1)}, u32[]{:S(2)}, u32[]{:S(2)}) collective-permute-start(bf16[208,768]{1,0:T(8,128)(2,1)S(1)} %get-tuple-element.42.refs_0_), channel_id=1, source_target_pairs={{0,16},{1,17},{2,18},{3,19},{4,20},{5,21},{6,22},{7,23},{8,24},{9,... | collective-permute-start | bytes 958472 | tf_op jit(solution)/shard_map/ppermute | solution.py:37
  5.8 2.8 %collective-permute-start.1 = (bf16[208,768]{1,0:T(8,128)(2,1)S(1)}, bf16[208,768]{1,0:T(8,128)(2,1)S(1)}, u32[]{:S(2)}, u32[]{:S(2)}) collective-permute-start(bf16[208,768]{1,0:T(8,128)(2,1)S(1)} %get-tuple-element.42.refs_0_), channel_id=1, source_target_pairs={{0,3},{1,0},{2,1},{3,2},{4,7},{5,4},{6,5},{7,6},{8,11},{9,8},{10,9... | collective-permute-start | bytes 958472 | tf_op jit(solution)/shard_map/ppermute | solution.py:37
  8.6 1.0 copy-done.4
  9.5 0.1 prep_texts.1.refs_0_
  9.7 2.6 %collective-permute-start.7 = (bf16[192,768]{1,0:T(8,128)(2,1)S(1)}, bf16[192,768]{1,0:T(8,128)(2,1)S(1)}, u32[]{:S(2)}, u32[]{:S(2)}) collective-permute-start(bf16[192,768]{1,0:T(8,128)(2,1)S(1)} %prep_texts.1.refs_0_), channel_id=1, source_target_pairs={{0,20},{1,21},{2,22},{3,23},{4,16},{5,17},{6,18},{7,19},{8,28},{9,... | collective-permute-start | bytes 884744 | tf_op jit(solution)/shard_map/ppermute | solution.py:37
  12.3 3.0 %collective-permute-start.8 = (bf16[192,768]{1,0:T(8,128)(2,1)S(1)}, bf16[192,768]{1,0:T(8,128)(2,1)S(1)}, u32[]{:S(2)}, u32[]{:S(2)}) collective-permute-start(bf16[192,768]{1,0:T(8,128)(2,1)S(1)} %prep_texts.1.refs_0_), channel_id=1, source_target_pairs={{0,96},{1,97},{2,98},{3,99},{4,100},{5,101},{6,102},{7,103},{8,104... | collective-permute-start | bytes 884744 | tf_op jit(solution)/shard_map/ppermute | solution.py:37
  15.3 3.2 %collective-permute-done.2.refs_2_.refs_4_ = bf16[208,768]{1,0:T(8,128)(2,1)S(1)} collective-permute-done((bf16[208,768]{1,0:T(8,128)(2,1)S(1)}, bf16[208,768]{1,0:T(8,128)(2,1)S(1)}, u32[]{:S(2)}, u32[]{:S(2)}) %collective-permute-start.2) | collective-permute-done | bytes 319520 | tf_op jit(solution)/shard_map/ppermute | solution.py:37
  18.5 0.4 collective-permute-start.3
  18.9 1.7 %collective-permute-start.4 = (bf16[208,768]{1,0:T(8,128)(2,1)S(1)}, bf16[208,768]{1,0:T(8,128)(2,1)S(1)}, u32[]{:S(2)}, u32[]{:S(2)}) collective-permute-start(bf16[208,768]{1,0:T(8,128)(2,1)S(1)} %gate.3.refs_2_), channel_id=1, source_target_pairs={{0,1},{1,2},{2,3},{3,0},{4,5},{5,6},{6,7},{7,4},{8,9},{9,10},{10,1... | collective-permute-start | bytes 958472 | tf_op jit(solution)/shard_map/ppermute | solution.py:37
  20.6 0.0 collective-permute-start.5
  20.6 0.1 collective-permute-done.8.refs_2_.refs_1_
  20.7 3.4 %collective-permute-done.9.refs_3_.refs_1_ = bf16[192,768]{1,0:T(8,128)(2,1)S(1)} collective-permute-done((bf16[192,768]{1,0:T(8,128)(2,1)S(1)}, bf16[192,768]{1,0:T(8,128)(2,1)S(1)}, u32[]{:S(2)}, u32[]{:S(2)}) %collective-permute-start.9) | collective-permute-done | bytes 294944 | tf_op jit(solution)/shard_map/ppermute | solution.py:37
  24.1 0.4 collective-permute-start.10
  24.5 1.8 %collective-permute-done.3.refs_3_ = bf16[208,768]{1,0:T(8,128)(2,1)S(1)} collective-permute-done((bf16[208,768]{1,0:T(8,128)(2,1)S(1)}, bf16[208,768]{1,0:T(8,128)(2,1)S(1)}, u32[]{:S(2)}, u32[]{:S(2)}) %collective-permute-start.3) | collective-permute-done | bytes 319520 | tf_op jit(solution)/shard_map/ppermute | solution.py:37
  26.4 1.8 %collective-permute-start.6 = (bf16[208,768]{1,0:T(8,128)(2,1)S(1)}, bf16[208,768]{1,0:T(8,128)(2,1)S(1)}, u32[]{:S(2)}, u32[]{:S(2)}) collective-permute-start(bf16[208,768]{1,0:T(8,128)(2,1)S(1)} %collective-permute-done.3.refs_3_), channel_id=1, source_target_pairs={{0,3},{1,0},{2,1},{3,2},{4,7},{5,4},{6,5},{7,6},{8,11},{9,8},{10,9... | collective-permute-start | bytes 958472 | tf_op jit(solution)/shard_map/ppermute | solution.py:37
  28.2 1.6 %collective-permute-start.11 = (bf16[192,768]{1,0:T(8,128)(2,1)S(1)}, bf16[192,768]{1,0:T(8,128)(2,1)S(1)}, u32[]{:S(2)}, u32[]{:S(2)}) collective-permute-start(bf16[192,768]{1,0:T(8,128)(2,1)S(1)} %gate.5), channel_id=1, source_target_pairs={{0,32},{1,33},{2,34},{3,35},{4,36},{5,37},{6,38},{7,39},{8,40},{9,... | collective-permute-start | bytes 884744 | tf_op jit(solution)/shard_map/ppermute | solution.py:37
  29.7 1.3 %collective-permute-done.10.refs_1_ = bf16[192,768]{1,0:T(8,128)(2,1)S(1)} collective-permute-done((bf16[192,768]{1,0:T(8,128)(2,1)S(1)}, bf16[192,768]{1,0:T(8,128)(2,1)S(1)}, u32[]{:S(2)}, u32[]{:S(2)}) %collective-permute-start.10) | collective-permute-done | bytes 294944 | tf_op jit(solution)/shard_map/ppermute | solution.py:37
  31.0 0.3 collective-permute-start.12
  31.3 3.0 %collective-permute-start.13 = (bf16[192,768]{1,0:T(8,128)(2,1)S(1)}, bf16[192,768]{1,0:T(8,128)(2,1)S(1)}, u32[]{:S(2)}, u32[]{:S(2)}) collective-permute-start(bf16[192,768]{1,0:T(8,128)(2,1)S(1)} %collective-permute-done.10.refs_1_), channel_id=1, source_target_pairs={{0,96},{1,97},{2,98},{3,99},{4,100},{5,101},{6,102},{7,103},{8,104... | collective-permute-start | bytes 884744 | tf_op jit(solution)/shard_map/ppermute | solution.py:37
  34.3 0.1 near_images.1
  34.4 0.3 collective-permute-done.5.refs_5_.refs_2_
  34.7 0.1 first_texts.1.refs_2_.refs_0_
  34.8 4.4 %score_first.1 = (f32[1536,768]{1,0:T(8,128)S(1)}, bf16[1536,1536]{1,0:T(8,128)(2,1)S(1)}, f32[8,128]{1,0:T(8,128)S(1)}) custom-call(f32[24,128]{1,0:T(8,128)S(1)} %get-tuple-element.41.refs_0_, bf16[1536,768]{1,0:T(8,128)(2,1)S(1)} %get-tuple-element.43.refs_4_.refs_1_.refs_0_, bf16[1536,768]{1,0:T(8,128)(2,1)S(1)} %first_texts.1.refs_2_.refs_0_, ...), custom_call_target="tpu_custom_call" | custom-call | flops 2717908992 | bytes 4194304 | tf_op jit(solution)/shard_map/score_first/pallas_call | solution.py:72
  39.2 2.3 %score_second.1 = (f32[1536,768]{1,0:T(8,128)S(1)}, bf16[1536,1536]{1,0:T(8,128)(2,1)S(1)}, f32[8,128]{1,0:T(8,128)S(1)}) custom-call(f32[24,128]{1,0:T(8,128)S(1)} %get-tuple-element.41.refs_0_, bf16[1536,768]{1,0:T(8,128)(2,1)S(1)} %get-tuple-element.43.refs_4_.refs_1_.refs_0_, ...), custom_call_target="tpu_custom_call", output_to_operand_aliasing={{0}: (5, {}), {1}: (6, {})} | custom-call | flops 1358954496 | bytes 4194304 | tf_op jit(solution)/shard_map/score_second/pallas_call | solution.py:72
  41.6 0.5 collective-permute-done.12.refs_1_
  42.1 0.3 collective-permute-start.14
  42.4 0.1 away_images.1
  42.6 6.1 %score_rest.1 = (f32[1536,768]{1,0:T(8,128)S(1)}, bf16[1536,1536]{1,0:T(8,128)(2,1)S(1)}, f32[8,128]{1,0:T(8,128)S(1)}) custom-call(f32[24,128]{1,0:T(8,128)S(1)} %get-tuple-element.41.refs_0_, bf16[1536,768]{1,0:T(8,128)(2,1)S(1)} %get-tuple-element.49.refs_1_, ...), custom_call_target="tpu_custom_call", output_to_operand_aliasing={{0}: (5, {}), {1}: (6, {})} | custom-call | flops 3170893824 | bytes 4194304 | tf_op jit(solution)/shard_map/score_rest/pallas_call | solution.py:72
  48.7 10.4 %score_sib.1 = (bf16[1552,768]{1,0:T(8,128)(2,1)S(1)}, bf16[1536,1536]{1,0:T(8,128)(2,1)S(1)}, f32[8,128]{1,0:T(8,128)S(1)}) custom-call(f32[24,128]{1,0:T(8,128)S(1)} %get-tuple-element.41.refs_0_, bf16[1536,768]{1,0:T(8,128)(2,1)S(1)} %get-tuple-element.49.refs_1_, bf16[1536,768]{1,0:T(8,128)(2,1)S(1)} %collective-permute-done.14.refs_2_.refs_3_, ...), custom_call_target="tpu_custom_call" | custom-call | flops 7247757312 | bytes 4194304 | tf_op jit(solution)/shard_map/score_sib/pallas_call | solution.py:72
  59.1 0.6 collective-permute-start.19
  59.7 2.0 %image_away.1 = (bf16[192,768]{1,0:T(8,128)(2,1)S(1)}, bf16[192,768]{1,0:T(8,128)(2,1)S(1)}) custom-call(bf16[1536,1536]{1,0:T(8,128)(2,1)S(1)} %get-tuple-element.53.refs_0_, bf16[1536,1536]{1,0:T(8,128)(2,1)S(1)} %get-tuple-element.55.refs_1_, bf16[1536,768]{1,0:T(8,128)(2,1)S(1)} %away_texts.1.refs_2_, ...), custom_call_target="tpu_custom_call" | custom-call | flops 905969664 | bytes 4194304 | tf_op jit(solution)/shard_map/image_away/pallas_call | solution.py:72
  61.8 0.1 collective-permute-start.15
  61.8 3.2 %collective-permute-start.16 = (bf16[192,768]{1,0:T(8,128)(2,1)S(1)}, bf16[192,768]{1,0:T(8,128)(2,1)S(1)}, u32[]{:S(2)}, u32[]{:S(2)}) collective-permute-start(bf16[192,768]{1,0:T(8,128)(2,1)S(1)} %get-tuple-element.60.refs_4_), channel_id=1, source_target_pairs={{0,3},{1,0},{2,1},{3,2},{4,7},{5,4},{6,5},{7,6},{8,11},{9,8},{10,9... | collective-permute-start | bytes 884744 | tf_op jit(solution)/shard_map/ppermute | solution.py:37
  65.1 0.6 add.13
  65.7 1.1 %collective-permute-start.20 = (bf16[208,768]{1,0:T(8,128)(2,1)S(1)}, bf16[208,768]{1,0:T(8,128)(2,1)S(1)}, u32[]{:S(2)}, u32[]{:S(2)}) collective-permute-start(bf16[208,768]{1,0:T(8,128)(2,1)S(1)} %get-tuple-element.68), channel_id=1, source_target_pairs={{0,32},{1,33},{2,34},{3,35},{4,36},{5,37},{6,38},{7,39},{8,40},{9,... | collective-permute-start | bytes 958472 | tf_op jit(solution)/shard_map/ppermute | solution.py:37
  66.8 2.2 %collective-permute-start.21 = (bf16[208,768]{1,0:T(8,128)(2,1)S(1)}, bf16[208,768]{1,0:T(8,128)(2,1)S(1)}, u32[]{:S(2)}, u32[]{:S(2)}) collective-permute-start(bf16[208,768]{1,0:T(8,128)(2,1)S(1)} %get-tuple-element.69), channel_id=1, source_target_pairs={{0,96},{1,97},{2,98},{3,99},{4,100},{5,101},{6,102},{7,103},{8,104... | collective-permute-start | bytes 958472 | tf_op jit(solution)/shard_map/ppermute | solution.py:37
  69.0 3.9 %image_ring.1 = (f32[384,768]{1,0:T(8,128)S(1)}, f32[384,768]{1,0:T(8,128)S(1)}) custom-call(bf16[1536,1536]{1,0:T(8,128)(2,1)S(1)} %get-tuple-element.53.refs_0_, bf16[1536,1536]{1,0:T(8,128)(2,1)S(1)} %get-tuple-element.55.refs_1_, bf16[1536,768]{1,0:T(8,128)(2,1)S(1)} %away_texts.1.refs_2_, bf16[1536,768]{1,0:T(8,128)(2,1)S(1)} %collective-permute-done.14.refs_2_.refs_3_), custom_call_target="tpu_custom_call" | custom-call | flops 1811939328 | bytes 4194304 | tf_op jit(solution)/shard_map/image_ring/pallas_call | solution.py:72
  72.9 0.2 turn.2
  73.1 0.1 collective-permute-start.17
  73.2 3.2 %collective-permute-start.18 = (bf16[384,768]{1,0:T(8,128)(2,1)S(1)}, bf16[384,768]{1,0:T(8,128)(2,1)S(1)}, u32[]{:S(2)}, u32[]{:S(2)}) collective-permute-start(bf16[384,768]{1,0:T(8,128)(2,1)S(1)} %get-tuple-element.62), channel_id=1, source_target_pairs={{0,3},{1,0},{2,1},{3,2},{4,7},{5,4},{6,5},{7,6},{8,11},{9,8},{10,9... | collective-permute-start | bytes 1769480 | tf_op jit(solution)/shard_map/ppermute | solution.py:37
  76.4 0.2 turn.3
  76.6 0.7 collective-permute-start.28
  77.3 2.6 %collective-permute-start.29 = (bf16[384,768]{1,0:T(8,128)(2,1)S(1)}, bf16[384,768]{1,0:T(8,128)(2,1)S(1)}, u32[]{:S(2)}, u32[]{:S(2)}) collective-permute-start(bf16[384,768]{1,0:T(8,128)(2,1)S(1)} %get-tuple-element.77), channel_id=1, source_target_pairs={{0,96},{1,97},{2,98},{3,99},{4,100},{5,101},{6,102},{7,103},{8,104... | collective-permute-start | bytes 1769480 | tf_op jit(solution)/shard_map/ppermute | solution.py:37
  79.9 0.9 collective-permute-start.22
  80.7 2.8 %collective-permute-done.22 = f32[8,128]{1,0:T(8,128)S(1)} collective-permute-done((f32[8,128]{1,0:T(8,128)S(1)}, f32[8,128]{1,0:T(8,128)S(1)}, u32[]{:S(2)}, u32[]{:S(2)}) %collective-permute-start.22) | collective-permute-done | bytes 4128 | tf_op jit(solution)/shard_map/ppermute | solution.py:37
  83.5 2.8 %collective-permute-start.23 = (f32[8,128]{1,0:T(8,128)S(1)}, f32[8,128]{1,0:T(8,128)S(1)}, u32[]{:S(2)}, u32[]{:S(2)}) collective-permute-start(f32[8,128]{1,0:T(8,128)S(1)} %add.10), channel_id=1, source_target_pairs={{0,20},{1,21},{2,22},{3,23},{4,16},{5,17},{6,18},{7,19},{8,28},{9,... | collective-permute-start | bytes 12296 | tf_op jit(solution)/shard_map/ppermute | solution.py:37
  86.3 2.0 %collective-permute-done.23 = f32[8,128]{1,0:T(8,128)S(1)} collective-permute-done((f32[8,128]{1,0:T(8,128)S(1)}, f32[8,128]{1,0:T(8,128)S(1)}, u32[]{:S(2)}, u32[]{:S(2)}) %collective-permute-start.23) | collective-permute-done | bytes 4128 | tf_op jit(solution)/shard_map/ppermute | solution.py:37
  88.3 2.0 %image_near.1 = (f32[192,768]{1,0:T(8,128)S(1)}, f32[192,768]{1,0:T(8,128)S(1)}) custom-call(bf16[1536,1536]{1,0:T(8,128)(2,1)S(1)} %get-tuple-element.53.refs_0_, bf16[1536,1536]{1,0:T(8,128)(2,1)S(1)} %get-tuple-element.55.refs_1_, bf16[1536,768]{1,0:T(8,128)(2,1)S(1)} %away_texts.1.refs_2_, bf16[1536,768]{1,0:T(8,128)(2,1)S(1)} %collective-permute-done.14.refs_2_.refs_3_), custom_call_target="tpu_custom_call" | custom-call | flops 905969664 | bytes 4194304 | tf_op jit(solution)/shard_map/image_near/pallas_call | solution.py:72
  90.4 1.5 %collective-permute-done.24.refs_4_ = f32[8,128]{1,0:T(8,128)S(1)} collective-permute-done((f32[8,128]{1,0:T(8,128)S(1)}, f32[8,128]{1,0:T(8,128)S(1)}, u32[]{:S(2)}, u32[]{:S(2)}) %collective-permute-start.24) | collective-permute-done | bytes 4128 | tf_op jit(solution)/shard_map/ppermute | solution.py:37
  91.9 0.1 far.2
  92.0 0.4 collective-permute-start.27
  92.4 0.1 far.3
  92.5 2.7 %collective-permute-start.30 = (bf16[192,768]{1,0:T(8,128)(2,1)S(1)}, bf16[192,768]{1,0:T(8,128)(2,1)S(1)}, u32[]{:S(2)}, u32[]{:S(2)}) collective-permute-start(bf16[192,768]{1,0:T(8,128)(2,1)S(1)} %far.3), channel_id=1, source_target_pairs={{0,20},{1,21},{2,22},{3,23},{4,16},{5,17},{6,18},{7,19},{8,28},{9,... | collective-permute-start | bytes 884744 | tf_op jit(solution)/shard_map/ppermute | solution.py:37
  95.2 1.6 %collective-permute-start.25 = (f32[8,128]{1,0:T(8,128)S(1)}, f32[8,128]{1,0:T(8,128)S(1)}, u32[]{:S(2)}, u32[]{:S(2)}) collective-permute-start(f32[8,128]{1,0:T(8,128)S(1)} %get-tuple-element.72), channel_id=1, source_target_pairs={{0,2},{1,3},{2,0},{3,1},{4,6},{5,7},{6,4},{7,5},{8,10},{9,11},{10,... | collective-permute-start | bytes 12296 | tf_op jit(solution)/shard_map/ppermute | solution.py:37
  96.9 3.5 %collective-permute-done.25 = f32[8,128]{1,0:T(8,128)S(1)} collective-permute-done((f32[8,128]{1,0:T(8,128)S(1)}, f32[8,128]{1,0:T(8,128)S(1)}, u32[]{:S(2)}, u32[]{:S(2)}) %collective-permute-start.25) | collective-permute-done | bytes 4128 | tf_op jit(solution)/shard_map/ppermute | solution.py:37
  100.3 1.5 %collective-permute-start.26 = (f32[8,128]{1,0:T(8,128)S(1)}, f32[8,128]{1,0:T(8,128)S(1)}, u32[]{:S(2)}, u32[]{:S(2)}) collective-permute-start(f32[8,128]{1,0:T(8,128)S(1)} %add.12.loss), channel_id=1, source_target_pairs={{0,64},{1,65},{2,66},{3,67},{4,68},{5,69},{6,70},{7,71},{8,72},{9,... | collective-permute-start | bytes 12296 | tf_op jit(solution)/shard_map/ppermute | solution.py:37
  101.8 1.1 %unproject.2.grad_x = f32[192,768]{1,0:T(8,128)} custom-call(bf16[192,768]{1,0:T(8,128)(2,1)S(1)} %copy-done.3, f32[192,768]{1,0:T(8,128)S(1)} %get-tuple-element.73.refs_1_, bf16[384,768]{1,0:T(8,128)(2,1)S(1)} %collective-permute-done.17.refs_1_.refs_2_, bf16[384,768]{1,0:T(8,128)(2,1)S(1)} %collective-permute-done.18.refs_2_.refs_3_, ...), custom_call_target="tpu_custom_call" | custom-call | bytes 4194304 | tf_op jit(solution)/shard_map/unproject/pallas_call | solution.py:72
  103.0 1.1 %unproject.3.grad_y = f32[192,768]{1,0:T(8,128)} custom-call(bf16[192,768]{1,0:T(8,128)(2,1)S(1)} %copy-done.5, f32[192,768]{1,0:T(8,128)S(1)} %get-tuple-element.75.refs_1_, bf16[384,768]{1,0:T(8,128)(2,1)S(1)} %collective-permute-done.28.refs_1_.refs_2_, bf16[384,768]{1,0:T(8,128)(2,1)S(1)} %collective-permute-done.29.refs_2_.refs_3_, ...), custom_call_target="tpu_custom_call" | custom-call | bytes 4194304 | tf_op jit(solution)/shard_map/unproject/pallas_call | solution.py:72
  104.1 1.4 %collective-permute-done.26.step = f32[8,128]{1,0:T(8,128)S(1)} collective-permute-done((f32[8,128]{1,0:T(8,128)S(1)}, f32[8,128]{1,0:T(8,128)S(1)}, u32[]{:S(2)}, u32[]{:S(2)}) %collective-permute-start.26) | collective-permute-done | bytes 4128 | tf_op jit(solution)/shard_map/ppermute | solution.py:37
  105.5 1.1 copy-done.1
  106.5 0.6 loss.1
  (40 shorter events, 0.2 us)
Async XLA Ops:
  1.9 1.0 copy-start.2
  2.9 0.7 copy-start.6
  3.7 11.6 %collective-permute-start = (bf16[208,768]{1,0:T(8,128)(2,1)S(1)}, bf16[208,768]{1,0:T(8,128)(2,1)S(1)}, u32[]{:S(2)}, u32[]{:S(2)}) collective-permute-start(bf16[208,768]{1,0:T(8,128)(2,1)S(1)} %get-tuple-element.42.refs_0_), channel_id=1, source_target_pairs={{0,16},{1,17},{2,18},{3,19},{4,20},{5,21},{6,22},{7,23},{8,24},{9,... | collective-permute-start | bytes 958472 | tf_op jit(solution)/shard_map/ppermute | solution.py:37
  5.8 9.5 %collective-permute-start.1 = (bf16[208,768]{1,0:T(8,128)(2,1)S(1)}, bf16[208,768]{1,0:T(8,128)(2,1)S(1)}, u32[]{:S(2)}, u32[]{:S(2)}) collective-permute-start(bf16[208,768]{1,0:T(8,128)(2,1)S(1)} %get-tuple-element.42.refs_0_), channel_id=1, source_target_pairs={{0,3},{1,0},{2,1},{3,2},{4,7},{5,4},{6,5},{7,6},{8,11},{9,8},{10,9... | collective-permute-start | bytes 958472 | tf_op jit(solution)/shard_map/ppermute | solution.py:37
  8.6 9.9 %collective-permute-start.2 = (bf16[208,768]{1,0:T(8,128)(2,1)S(1)}, bf16[208,768]{1,0:T(8,128)(2,1)S(1)}, u32[]{:S(2)}, u32[]{:S(2)}) collective-permute-start(bf16[208,768]{1,0:T(8,128)(2,1)S(1)} %get-tuple-element.42.refs_0_), channel_id=1, source_target_pairs={{0,1},{1,2},{2,3},{3,0},{4,5},{5,6},{6,7},{7,4},{8,9},{9,10},{10,1... | collective-permute-start | bytes 958472 | tf_op jit(solution)/shard_map/ppermute | solution.py:37
  8.6 1.0 copy-start.4
  9.7 10.9 %collective-permute-start.7 = (bf16[192,768]{1,0:T(8,128)(2,1)S(1)}, bf16[192,768]{1,0:T(8,128)(2,1)S(1)}, u32[]{:S(2)}, u32[]{:S(2)}) collective-permute-start(bf16[192,768]{1,0:T(8,128)(2,1)S(1)} %prep_texts.1.refs_0_), channel_id=1, source_target_pairs={{0,20},{1,21},{2,22},{3,23},{4,16},{5,17},{6,18},{7,19},{8,28},{9,... | collective-permute-start | bytes 884744 | tf_op jit(solution)/shard_map/ppermute | solution.py:37
  12.3 8.4 %collective-permute-start.8 = (bf16[192,768]{1,0:T(8,128)(2,1)S(1)}, bf16[192,768]{1,0:T(8,128)(2,1)S(1)}, u32[]{:S(2)}, u32[]{:S(2)}) collective-permute-start(bf16[192,768]{1,0:T(8,128)(2,1)S(1)} %prep_texts.1.refs_0_), channel_id=1, source_target_pairs={{0,96},{1,97},{2,98},{3,99},{4,100},{5,101},{6,102},{7,103},{8,104... | collective-permute-start | bytes 884744 | tf_op jit(solution)/shard_map/ppermute | solution.py:37
  15.3 8.8 %collective-permute-start.9 = (bf16[192,768]{1,0:T(8,128)(2,1)S(1)}, bf16[192,768]{1,0:T(8,128)(2,1)S(1)}, u32[]{:S(2)}, u32[]{:S(2)}) collective-permute-start(bf16[192,768]{1,0:T(8,128)(2,1)S(1)} %prep_texts.1.refs_0_), channel_id=1, source_target_pairs={{0,32},{1,33},{2,34},{3,35},{4,36},{5,37},{6,38},{7,39},{8,40},{9,... | collective-permute-start | bytes 884744 | tf_op jit(solution)/shard_map/ppermute | solution.py:37
  18.5 7.9 %collective-permute-start.3 = (bf16[208,768]{1,0:T(8,128)(2,1)S(1)}, bf16[208,768]{1,0:T(8,128)(2,1)S(1)}, u32[]{:S(2)}, u32[]{:S(2)}) collective-permute-start(bf16[208,768]{1,0:T(8,128)(2,1)S(1)} %gate.3.refs_2_), channel_id=1, source_target_pairs={{0,3},{1,0},{2,1},{3,2},{4,7},{5,4},{6,5},{7,6},{8,11},{9,8},{10,9... | collective-permute-start | bytes 958472 | tf_op jit(solution)/shard_map/ppermute | solution.py:37
  18.9 12.5 %collective-permute-start.4 = (bf16[208,768]{1,0:T(8,128)(2,1)S(1)}, bf16[208,768]{1,0:T(8,128)(2,1)S(1)}, u32[]{:S(2)}, u32[]{:S(2)}) collective-permute-start(bf16[208,768]{1,0:T(8,128)(2,1)S(1)} %gate.3.refs_2_), channel_id=1, source_target_pairs={{0,1},{1,2},{2,3},{3,0},{4,5},{5,6},{6,7},{7,4},{8,9},{9,10},{10,1... | collective-permute-start | bytes 958472 | tf_op jit(solution)/shard_map/ppermute | solution.py:37
  20.6 14.1 %collective-permute-start.5 = (bf16[208,768]{1,0:T(8,128)(2,1)S(1)}, bf16[208,768]{1,0:T(8,128)(2,1)S(1)}, u32[]{:S(2)}, u32[]{:S(2)}) collective-permute-start(bf16[208,768]{1,0:T(8,128)(2,1)S(1)} %collective-permute-done.2.refs_2_.refs_4_), channel_id=1, source_target_pairs={{0,1},{1,2},{2,3},{3,0},{4,5},{5,6},{6,7},{7,4},{8,9},{9,10},{10,1... | collective-permute-start | bytes 958472 | tf_op jit(solution)/shard_map/ppermute | solution.py:37
  24.1 6.9 %collective-permute-start.10 = (bf16[192,768]{1,0:T(8,128)(2,1)S(1)}, bf16[192,768]{1,0:T(8,128)(2,1)S(1)}, u32[]{:S(2)}, u32[]{:S(2)}) collective-permute-start(bf16[192,768]{1,0:T(8,128)(2,1)S(1)} %gate.5), channel_id=1, source_target_pairs={{0,96},{1,97},{2,98},{3,99},{4,100},{5,101},{6,102},{7,103},{8,104... | collective-permute-start | bytes 884744 | tf_op jit(solution)/shard_map/ppermute | solution.py:37
  26.4 12.8 %collective-permute-start.6 = (bf16[208,768]{1,0:T(8,128)(2,1)S(1)}, bf16[208,768]{1,0:T(8,128)(2,1)S(1)}, u32[]{:S(2)}, u32[]{:S(2)}) collective-permute-start(bf16[208,768]{1,0:T(8,128)(2,1)S(1)} %collective-permute-done.3.refs_3_), channel_id=1, source_target_pairs={{0,3},{1,0},{2,1},{3,2},{4,7},{5,4},{6,5},{7,6},{8,11},{9,8},{10,9... | collective-permute-start | bytes 958472 | tf_op jit(solution)/shard_map/ppermute | solution.py:37
  28.2 11.0 %collective-permute-start.11 = (bf16[192,768]{1,0:T(8,128)(2,1)S(1)}, bf16[192,768]{1,0:T(8,128)(2,1)S(1)}, u32[]{:S(2)}, u32[]{:S(2)}) collective-permute-start(bf16[192,768]{1,0:T(8,128)(2,1)S(1)} %gate.5), channel_id=1, source_target_pairs={{0,32},{1,33},{2,34},{3,35},{4,36},{5,37},{6,38},{7,39},{8,40},{9,... | collective-permute-start | bytes 884744 | tf_op jit(solution)/shard_map/ppermute | solution.py:37
  31.0 11.1 %collective-permute-start.12 = (bf16[192,768]{1,0:T(8,128)(2,1)S(1)}, bf16[192,768]{1,0:T(8,128)(2,1)S(1)}, u32[]{:S(2)}, u32[]{:S(2)}) collective-permute-start(bf16[192,768]{1,0:T(8,128)(2,1)S(1)} %collective-permute-done.9.refs_3_.refs_1_), channel_id=1, source_target_pairs={{0,32},{1,33},{2,34},{3,35},{4,36},{5,37},{6,38},{7,39},{8,40},{9,... | collective-permute-start | bytes 884744 | tf_op jit(solution)/shard_map/ppermute | solution.py:37
  31.3 10.8 %collective-permute-start.13 = (bf16[192,768]{1,0:T(8,128)(2,1)S(1)}, bf16[192,768]{1,0:T(8,128)(2,1)S(1)}, u32[]{:S(2)}, u32[]{:S(2)}) collective-permute-start(bf16[192,768]{1,0:T(8,128)(2,1)S(1)} %collective-permute-done.10.refs_1_), channel_id=1, source_target_pairs={{0,96},{1,97},{2,98},{3,99},{4,100},{5,101},{6,102},{7,103},{8,104... | collective-permute-start | bytes 884744 | tf_op jit(solution)/shard_map/ppermute | solution.py:37
  42.1 6.5 %collective-permute-start.14 = (bf16[1536,768]{1,0:T(8,128)(2,1)S(1)}, bf16[1536,768]{1,0:T(8,128)(2,1)S(1)}, u32[]{:S(2)}, u32[]{:S(2)}) collective-permute-start(bf16[1536,768]{1,0:T(8,128)(2,1)S(1)} %away_texts.1.refs_2_), channel_id=1, source_target_pairs={{0,8},{1,9},{2,10},{3,11},{4,12},{5,13},{6,14},{7,15},{8,0},{9,1},... | collective-permute-start | bytes 7077896 | tf_op jit(solution)/shard_map/ppermute | solution.py:37
  59.1 5.9 %collective-permute-start.19 = (bf16[1552,768]{1,0:T(8,128)(2,1)S(1)}, bf16[1552,768]{1,0:T(8,128)(2,1)S(1)}, u32[]{:S(2)}, u32[]{:S(2)}) collective-permute-start(bf16[1552,768]{1,0:T(8,128)(2,1)S(1)} %get-tuple-element.64), channel_id=1, source_target_pairs={{0,8},{1,9},{2,10},{3,11},{4,12},{5,13},{6,14},{7,15},{8,0},{9,1},... | collective-permute-start | bytes 7151624 | tf_op jit(solution)/shard_map/ppermute | solution.py:37
  61.8 11.1 %collective-permute-start.15 = (bf16[192,768]{1,0:T(8,128)(2,1)S(1)}, bf16[192,768]{1,0:T(8,128)(2,1)S(1)}, u32[]{:S(2)}, u32[]{:S(2)}) collective-permute-start(bf16[192,768]{1,0:T(8,128)(2,1)S(1)} %get-tuple-element.59.refs_3_), channel_id=1, source_target_pairs={{0,1},{1,2},{2,3},{3,0},{4,5},{5,6},{6,7},{7,4},{8,9},{9,10},{10,1... | collective-permute-start | bytes 884744 | tf_op jit(solution)/shard_map/ppermute | solution.py:37
  61.8 11.0 %collective-permute-start.16 = (bf16[192,768]{1,0:T(8,128)(2,1)S(1)}, bf16[192,768]{1,0:T(8,128)(2,1)S(1)}, u32[]{:S(2)}, u32[]{:S(2)}) collective-permute-start(bf16[192,768]{1,0:T(8,128)(2,1)S(1)} %get-tuple-element.60.refs_4_), channel_id=1, source_target_pairs={{0,3},{1,0},{2,1},{3,2},{4,7},{5,4},{6,5},{7,6},{8,11},{9,8},{10,9... | collective-permute-start | bytes 884744 | tf_op jit(solution)/shard_map/ppermute | solution.py:37
  65.7 10.7 %collective-permute-start.20 = (bf16[208,768]{1,0:T(8,128)(2,1)S(1)}, bf16[208,768]{1,0:T(8,128)(2,1)S(1)}, u32[]{:S(2)}, u32[]{:S(2)}) collective-permute-start(bf16[208,768]{1,0:T(8,128)(2,1)S(1)} %get-tuple-element.68), channel_id=1, source_target_pairs={{0,32},{1,33},{2,34},{3,35},{4,36},{5,37},{6,38},{7,39},{8,40},{9,... | collective-permute-start | bytes 958472 | tf_op jit(solution)/shard_map/ppermute | solution.py:37
  66.8 9.6 %collective-permute-start.21 = (bf16[208,768]{1,0:T(8,128)(2,1)S(1)}, bf16[208,768]{1,0:T(8,128)(2,1)S(1)}, u32[]{:S(2)}, u32[]{:S(2)}) collective-permute-start(bf16[208,768]{1,0:T(8,128)(2,1)S(1)} %get-tuple-element.69), channel_id=1, source_target_pairs={{0,96},{1,97},{2,98},{3,99},{4,100},{5,101},{6,102},{7,103},{8,104... | collective-permute-start | bytes 958472 | tf_op jit(solution)/shard_map/ppermute | solution.py:37
  73.1 17.3 %collective-permute-start.17 = (bf16[384,768]{1,0:T(8,128)(2,1)S(1)}, bf16[384,768]{1,0:T(8,128)(2,1)S(1)}, u32[]{:S(2)}, u32[]{:S(2)}) collective-permute-start(bf16[384,768]{1,0:T(8,128)(2,1)S(1)} %get-tuple-element.61.refs_5_), channel_id=1, source_target_pairs={{0,1},{1,2},{2,3},{3,0},{4,5},{5,6},{6,7},{7,4},{8,9},{9,10},{10,1... | collective-permute-start | bytes 1769480 | tf_op jit(solution)/shard_map/ppermute | solution.py:37
  73.2 17.2 %collective-permute-start.18 = (bf16[384,768]{1,0:T(8,128)(2,1)S(1)}, bf16[384,768]{1,0:T(8,128)(2,1)S(1)}, u32[]{:S(2)}, u32[]{:S(2)}) collective-permute-start(bf16[384,768]{1,0:T(8,128)(2,1)S(1)} %get-tuple-element.62), channel_id=1, source_target_pairs={{0,3},{1,0},{2,1},{3,2},{4,7},{5,4},{6,5},{7,6},{8,11},{9,8},{10,9... | collective-permute-start | bytes 1769480 | tf_op jit(solution)/shard_map/ppermute | solution.py:37
  76.6 15.8 %collective-permute-start.28 = (bf16[384,768]{1,0:T(8,128)(2,1)S(1)}, bf16[384,768]{1,0:T(8,128)(2,1)S(1)}, u32[]{:S(2)}, u32[]{:S(2)}) collective-permute-start(bf16[384,768]{1,0:T(8,128)(2,1)S(1)} %get-tuple-element.76), channel_id=1, source_target_pairs={{0,32},{1,33},{2,34},{3,35},{4,36},{5,37},{6,38},{7,39},{8,40},{9,... | collective-permute-start | bytes 1769480 | tf_op jit(solution)/shard_map/ppermute | solution.py:37
  77.3 15.1 %collective-permute-start.29 = (bf16[384,768]{1,0:T(8,128)(2,1)S(1)}, bf16[384,768]{1,0:T(8,128)(2,1)S(1)}, u32[]{:S(2)}, u32[]{:S(2)}) collective-permute-start(bf16[384,768]{1,0:T(8,128)(2,1)S(1)} %get-tuple-element.77), channel_id=1, source_target_pairs={{0,96},{1,97},{2,98},{3,99},{4,100},{5,101},{6,102},{7,103},{8,104... | collective-permute-start | bytes 1769480 | tf_op jit(solution)/shard_map/ppermute | solution.py:37
  79.9 3.6 %collective-permute-start.22 = (f32[8,128]{1,0:T(8,128)S(1)}, f32[8,128]{1,0:T(8,128)S(1)}, u32[]{:S(2)}, u32[]{:S(2)}) collective-permute-start(f32[8,128]{1,0:T(8,128)S(1)} %get-tuple-element.71), channel_id=1, source_target_pairs={{0,16},{1,17},{2,18},{3,19},{4,20},{5,21},{6,22},{7,23},{8,24},{9,... | collective-permute-start | bytes 12296 | tf_op jit(solution)/shard_map/ppermute | solution.py:37
  83.5 4.8 %collective-permute-start.23 = (f32[8,128]{1,0:T(8,128)S(1)}, f32[8,128]{1,0:T(8,128)S(1)}, u32[]{:S(2)}, u32[]{:S(2)}) collective-permute-start(f32[8,128]{1,0:T(8,128)S(1)} %add.10), channel_id=1, source_target_pairs={{0,20},{1,21},{2,22},{3,23},{4,16},{5,17},{6,18},{7,19},{8,28},{9,... | collective-permute-start | bytes 12296 | tf_op jit(solution)/shard_map/ppermute | solution.py:37
  88.3 3.6 %collective-permute-start.24 = (f32[8,128]{1,0:T(8,128)S(1)}, f32[8,128]{1,0:T(8,128)S(1)}, u32[]{:S(2)}, u32[]{:S(2)}) collective-permute-start(f32[8,128]{1,0:T(8,128)S(1)} %add.11.refs_3_), channel_id=1, source_target_pairs={{0,1},{1,0},{2,3},{3,2},{4,5},{5,4},{6,7},{7,6},{8,9},{9,8},{10,11... | collective-permute-start | bytes 12296 | tf_op jit(solution)/shard_map/ppermute | solution.py:37
  90.4 11.5 %copy-start.3 = (bf16[192,768]{1,0:T(8,128)(2,1)S(1)}, bf16[192,768]{1,0:T(8,128)(2,1)}, u32[]{:S(2)}) copy-start(bf16[192,768]{1,0:T(8,128)(2,1)} %refs_0_.5) | copy-start | bytes 884740
  92.0 9.8 %collective-permute-start.27 = (bf16[192,768]{1,0:T(8,128)(2,1)S(1)}, bf16[192,768]{1,0:T(8,128)(2,1)S(1)}, u32[]{:S(2)}, u32[]{:S(2)}) collective-permute-start(bf16[192,768]{1,0:T(8,128)(2,1)S(1)} %get-tuple-element.74), channel_id=1, source_target_pairs={{0,16},{1,17},{2,18},{3,19},{4,20},{5,21},{6,22},{7,23},{8,24},{9,... | collective-permute-start | bytes 884744 | tf_op jit(solution)/shard_map/ppermute | solution.py:37
  92.4 10.6 %copy-start.5 = (bf16[192,768]{1,0:T(8,128)(2,1)S(1)}, bf16[192,768]{1,0:T(8,128)(2,1)}, u32[]{:S(2)}) copy-start(bf16[192,768]{1,0:T(8,128)(2,1)} %refs_0_.6) | copy-start | bytes 884740
  92.5 10.4 %collective-permute-start.30 = (bf16[192,768]{1,0:T(8,128)(2,1)S(1)}, bf16[192,768]{1,0:T(8,128)(2,1)S(1)}, u32[]{:S(2)}, u32[]{:S(2)}) collective-permute-start(bf16[192,768]{1,0:T(8,128)(2,1)S(1)} %far.3), channel_id=1, source_target_pairs={{0,20},{1,21},{2,22},{3,23},{4,16},{5,17},{6,18},{7,19},{8,28},{9,... | collective-permute-start | bytes 884744 | tf_op jit(solution)/shard_map/ppermute | solution.py:37
  95.2 5.1 %collective-permute-start.25 = (f32[8,128]{1,0:T(8,128)S(1)}, f32[8,128]{1,0:T(8,128)S(1)}, u32[]{:S(2)}, u32[]{:S(2)}) collective-permute-start(f32[8,128]{1,0:T(8,128)S(1)} %get-tuple-element.72), channel_id=1, source_target_pairs={{0,2},{1,3},{2,0},{3,1},{4,6},{5,7},{6,4},{7,5},{8,10},{9,11},{10,... | collective-permute-start | bytes 12296 | tf_op jit(solution)/shard_map/ppermute | solution.py:37
  100.3 5.1 %collective-permute-start.26 = (f32[8,128]{1,0:T(8,128)S(1)}, f32[8,128]{1,0:T(8,128)S(1)}, u32[]{:S(2)}, u32[]{:S(2)}) collective-permute-start(f32[8,128]{1,0:T(8,128)S(1)} %add.12.loss), channel_id=1, source_target_pairs={{0,64},{1,65},{2,66},{3,67},{4,68},{5,69},{6,70},{7,71},{8,72},{9,... | collective-permute-start | bytes 12296 | tf_op jit(solution)/shard_map/ppermute | solution.py:37
  103.0 2.5 %copy-start = (f32[192,768]{1,0:T(8,128)S(1)}, f32[192,768]{1,0:T(8,128)}, u32[]{:S(2)}) copy-start(f32[192,768]{1,0:T(8,128)} %unproject.2.grad_x) | copy-start | bytes 1769476
  105.5 1.1 copy-start.1
